TPU v7x, 128 devices: a whole 4x4x4 slice. The times are simulated.
128 devices in a mesh: fsdp: 8 (over x, y_hi), tile: 8 (over z, core), dp: 2 (over y_lo).
Axes of the slice: x: 4, y: 4 (y_hi: 2, y_lo: 2; y = y_hi * 2 + y_lo), z: 4, core: 2. Of those that a mesh axis runs over, the one named last changes fastest.
Arguments:
- features: bfloat16 [16, 16, 384, 512], P(('fsdp', 'dp'), 'tile'), may hold values from -6 to 6
- frame_table: bfloat16 [600, 512], replicated, may hold values from -6 to 6
- frame_ids: int32 [16], P(('fsdp', 'dp')), may hold values from 0 to 599
- conv_weight: bfloat16 [1024, 4608], P('fsdp'), may hold values from -0.09375 to 0.09375
- cotangent: bfloat16 [16, 32, 768, 256], P(('fsdp', 'dp'), 'tile'), may hold values from -6 to 6
Outputs:
- upsampled: bfloat16 [16, 32, 768, 256], P(('fsdp', 'dp'), 'tile')
- grad_weight: float32 [1024, 4608], P('fsdp')
- grad_features: bfloat16 [16, 16, 384, 512], P(('fsdp', 'dp'), 'tile')
- grad_table: float32 [600, 512], replicated
All inputs are finite; a program needn't handle non-finite values.
Results may differ from a plain program's by a relative error of at most 0.0061.
Values may be sent and summed in bfloat16 or wider, within the bound.
A program may use at most 256 MiB of HBM per device.

v0:
```python
import jax
import jax.numpy as jnp
from jax import lax
from jax.sharding import PartitionSpec as P

inv_root_two = 0.7071067811865476
inv_root_tau = 0.3989422804014327


def extended(cells, sides, width):
    for axis, dim in sides:
        count = lax.axis_size(axis)
        ends = count - 1
        head = lax.slice_in_dim(cells, 0, width, axis=dim)
        tail = lax.slice_in_dim(cells, cells.shape[dim] - width, cells.shape[dim], axis=dim)
        cells = jnp.concatenate(
            [
                lax.ppermute(tail, axis, [(i, (i + 1) % count) for i in range(ends)]),
                cells,
                lax.ppermute(head, axis, [((i + 1) % count, i) for i in range(ends)]),
            ],
            axis=dim,
        )
    return cells


def gelu_value(values):
    return 0.5 * values * (1.0 + lax.erf(values * inv_root_two))


def gelu_slope(values):
    return (
        0.5 * (1.0 + lax.erf(values * inv_root_two))
        + values * jnp.exp(-0.5 * values * values) * inv_root_tau
    )


def pad_columns(blocks):
    return jnp.pad(blocks, ((0, 0), (0, 0), (1, 1), (0, 0)))


def shuffle(blocks):
    count, row_count, col_count, channels = blocks.shape
    narrow = channels // 4
    spread = blocks.reshape(count, row_count, col_count, 2, 2, narrow).transpose(0, 1, 3, 2, 4, 5)
    return spread.reshape(count, 2 * row_count, 2 * col_count, narrow)


def unshuffle(image):
    count, tall, broad, narrow = image.shape
    split = image.reshape(count, tall // 2, 2, broad // 2, 2, narrow).transpose(0, 1, 3, 2, 4, 5)
    return split.reshape(count, tall // 2, broad // 2, 4 * narrow)


def conv_rows(padded, weight_rows):
    row_count = padded.shape[1] - 2
    col_count = padded.shape[2] - 2
    chan_in = padded.shape[3]
    summed = None
    for tap_index in range(9):
        row_off, col_off = (tap_index // 3, tap_index % 3)
        window = padded[:, row_off : row_off + row_count, col_off : col_off + col_count, :]
        taps = weight_rows[:, tap_index * chan_in : (tap_index + 1) * chan_in]
        partial_sum = lax.dot_general(
            window, taps, (((3,), (1,)), ((), ())), preferred_element_type=jnp.float32
        )
        summed = partial_sum if summed is None else summed + partial_sum
    return summed


def weight_term(padded, slopes):
    row_count = slopes.shape[1]
    col_count = slopes.shape[2]
    pieces = []
    for tap_index in range(9):
        row_off, col_off = (tap_index // 3, tap_index % 3)
        window = padded[:, row_off : row_off + row_count, col_off : col_off + col_count, :]
        pieces.append(
            lax.dot_general(
                slopes,
                window,
                (((0, 1, 2), (0, 1, 2)), ((), ())),
                preferred_element_type=jnp.float32,
            )
        )
    return jnp.concatenate(pieces, axis=1)


def input_term(slope_pad, weight_rows):
    row_count = slope_pad.shape[1] - 2
    col_count = slope_pad.shape[2] - 2
    chan_in = weight_rows.shape[1] // 9
    summed = None
    for tap_index in range(9):
        row_off, col_off = (tap_index // 3, tap_index % 3)
        window = slope_pad[
            :, 2 - row_off : 2 - row_off + row_count, 2 - col_off : 2 - col_off + col_count, :
        ]
        taps = weight_rows[:, tap_index * chan_in : (tap_index + 1) * chan_in]
        partial_sum = lax.dot_general(
            window, taps, (((3,), (0,)), ((), ())), preferred_element_type=jnp.float32
        )
        summed = partial_sum if summed is None else summed + partial_sum
    return summed


def shards(features, frame_table, frame_ids, conv_weight, cotangent):
    video_len = frame_table.shape[0]
    picker = (frame_ids[:, None] == jnp.arange(video_len, dtype=jnp.int32)[None, :]).astype(
        jnp.bfloat16
    )
    frame_shift = jnp.dot(picker, frame_table, preferred_element_type=jnp.float32)
    inputs = (features.astype(jnp.float32) + frame_shift[:, None, None, :]).astype(jnp.bfloat16)
    rimmed = extended(inputs, (("tile", 1),), 1)
    padded = pad_columns(rimmed)
    cot_blocks = unshuffle(cotangent)
    conv_first = conv_rows(padded, lax.all_gather(conv_weight, "fsdp", axis=0, tiled=True))
    activated = gelu_value(conv_first).astype(jnp.bfloat16)
    gathered = lax.all_gather(conv_weight, "fsdp", axis=0, tiled=True)
    conv_out = conv_rows(padded, gathered)
    upsampled = shuffle(activated)
    slopes = (cot_blocks.astype(jnp.float32) * gelu_slope(conv_out)).astype(jnp.bfloat16)
    weight_partial = lax.psum_scatter(
        weight_term(padded, slopes), "fsdp", scatter_dimension=0, tiled=True
    )
    slope_rim = pad_columns(extended(slopes, (("tile", 1),), 1))
    input_grad = input_term(slope_rim, gathered)
    grad_weight = lax.psum(weight_partial, ("tile", "dp"))
    frame_sums = jnp.sum(input_grad, axis=(1, 2))
    table_term = lax.dot_general(
        picker.astype(jnp.float32),
        frame_sums,
        (((0,), (0,)), ((), ())),
        precision=lax.Precision.HIGHEST,
        preferred_element_type=jnp.float32,
    )
    grad_table = lax.psum(table_term, ("fsdp", "tile", "dp"))
    return (upsampled, grad_weight, input_grad.astype(jnp.bfloat16), grad_table)


def solution(mesh):
    return jax.shard_map(
        shards,
        mesh=mesh,
        in_specs=(
            P(("fsdp", "dp"), "tile", None, None),
            P(),
            P(("fsdp", "dp")),
            P("fsdp", None),
            P(("fsdp", "dp"), "tile", None, None),
        ),
        out_specs=(
            P(("fsdp", "dp"), "tile", None, None),
            P("fsdp", None),
            P(("fsdp", "dp"), "tile", None, None),
            P(),
        ),
        check_vma=False,
    )
```

profile of v0, /device:TPU:1, one launch (start us, length us, event | category | flops | bytes accessed | tf_op | source)
XLA Modules:
  0.0 693.3 jit_solution(12468511293420638595)
XLA Ops:
  8.8 1.3 add_convert_fusion
  11.1 4.9 collective-permute-start
  16.0 1.9 collective-permute-start.1
  17.9 3.0 reshape.194
  20.9 4.6 copy.31
  25.6 5.7 reshape.193
  31.7 100.0 %all-gather.2.cloned.1.call-done = bf16[1024,4608]{1,0:T(8,128)(2,1)} async-done(((bf16[128,4608]{1,0:T(8,128)(2,1)}), bf16[1024,4608]{1,0:T(8,128)(2,1)}) %all-gather.2.cloned.1.call-update) | async-done | bytes 9437200 | tf_op jit(solution)/shard_map/all_gather | solution.py:117
  131.7 2.4 fusion.39
  134.1 2.9 fusion.38
  137.9 2.7 fusion.34
  140.6 2.6 fusion.32
  143.3 2.7 fusion.40
  146.0 2.7 fusion.33
  148.6 2.7 fusion.37
  151.3 8.2 %fusion.12 = (bf16[2,384,1024]{2,1,0:T(8,128)(2,1)S(1)}, bf16[2,384,1024]{2,1,0:T(8,128)(2,1)}) fusion(f32[2,384,1024]{2,1,0:T(8,128)S(1)} %copy-done.4, f32[2,384,1024]{2,1,0:T(8,128)} %fusion.40, bf16[1024,4608]{1,0:T(8,128)(2,1)} %all-gather.2.cloned.1.call-done, bf16[1,1,384,512]{3,2,1,0:T(8,128)(2,1)S(1)} %collective-permute-done.1, ...), kind=kOutput, calls=%fused_computation.17 | convolution fusion | flops 822214656 | bytes 33685504 | tf_op jit(solution)/shard_map/dot_general | solution.py:64
  159.6 2.4 bitcast_dynamic-update-slice_fusion.8
  161.9 2.3 bitcast_dynamic-update-slice_fusion.7
  164.2 2.4 bitcast_dynamic-update-slice_fusion.6
  166.6 2.4 bitcast_dynamic-update-slice_fusion.5
  169.0 2.4 bitcast_dynamic-update-slice_fusion.4
  171.4 2.4 bitcast_dynamic-update-slice_fusion.3
  173.8 2.4 bitcast_dynamic-update-slice_fusion.2
  176.2 2.3 bitcast_dynamic-update-slice_fusion.1
  178.5 2.4 bitcast_dynamic-update-slice_fusion
  180.9 1.3 copy-done.3
  182.4 4.2 collective-permute-start.2
  186.6 1.9 collective-permute-start.3
  188.5 3.7 fusion.36
  192.2 3.3 collective-permute-done.2
  195.5 3.3 fusion.20
  198.8 1.5 collective-permute-done.3
  200.3 1.0 fusion.5
  201.3 4.2 fusion.24
  205.5 3.4 fusion.26
  208.9 179.4 %reduce-scatter.2.cloned.1.call-done = f32[128,4608]{0,1:T(8,128)} async-done(((f32[1024,4608]{0,1:T(8,128)}), f32[128,4608]{0,1:T(8,128)}) %reduce-scatter.2.cloned.1.call-update) | async-done | bytes 2359312 | tf_op jit(solution)/shard_map/reduce_scatter | solution.py:123
  388.6 2.4 fusion.28
  390.9 2.2 fusion.23
  393.1 2.2 fusion.25
  395.4 2.4 fusion.31
  398.5 3.5 fusion.56
  402.0 1.2 broadcast_multiply_fusion
  403.9 2.3 reshape.183
  406.2 2.5 copy.9
  408.7 2.0 reshape.184
  410.7 119.0 %all-reduce.5.cloned.1.call-done = f32[128,4608]{0,1:T(8,128)} async-done(((f32[128,4608]{0,1:T(8,128)}), f32[128,4608]{0,1:T(8,128)}) %all-reduce.5.cloned.1.call-update) | async-done | bytes 2359312 | tf_op jit(solution)/shard_map/psum | solution.py:128
  529.7 3.0 copy.20
  532.7 151.7 %all-reduce.7.cloned.1.call-done = f32[600,512]{1,0:T(8,128)} async-done(((f32[600,512]{1,0:T(8,128)}), f32[600,512]{1,0:T(8,128)}) %all-reduce.7.cloned.1.call-update) | async-done | bytes 1228816 | tf_op jit(solution)/shard_map/psum | solution.py:137
  684.4 2.4 copy.43
  (44 shorter events, 5.2 us)
Async XLA Ops:
  7.2 1.5 copy-start
  7.2 10.7 %copy-start.13 = (bf16[1,4,768,256]{3,2,1,0:T(8,128)(2,1)S(1)}, bf16[1,4,768,256]{3,2,1,0:T(8,128)(2,1)}, u32[]{:S(2)}) copy-start(bf16[1,4,768,256]{3,2,1,0:T(8,128)(2,1)} %param.9) | copy-start | bytes 4718596
  7.2 124.5 %all-gather.2.cloned.1.call-start = ((), (), s32[]{:S(2)}) async-start(), calls=%async_computation.1 | async-start | bytes 10616832 | tf_op jit(solution)/shard_map/all_gather | solution.py:117
  7.9 380.3 %reduce-scatter.2.cloned.1.call-start = ((), (), s32[]{:S(2)}) async-start(), calls=%async_computation.2 | async-start | bytes 21233664 | tf_op jit(solution)/shard_map/reduce_scatter | solution.py:123
  11.1 20.2 %collective-permute-start = (bf16[1,1,384,512]{3,2,1,0:T(8,128)(2,1)}, bf16[1,1,384,512]{3,2,1,0:T(8,128)(2,1)S(1)}, u32[]{:S(2)}, u32[]{:S(2)}) collective-permute-start(bf16[1,1,384,512]{3,2,1,0:T(8,128)(2,1)} %get-tuple-element.14), channel_id=1, source_target_pairs={{0,2},{2,4},{4,6},{6,8},{8,10},{10,12},{12,14},{1,3},{3,5},{5,7},{... | collective-permute-start | bytes 1179656 | tf_op jit(solution)/shard_map/ppermute | solution.py:18
  16.0 15.3 %collective-permute-start.1 = (bf16[1,1,384,512]{3,2,1,0:T(8,128)(2,1)}, bf16[1,1,384,512]{3,2,1,0:T(8,128)(2,1)S(1)}, u32[]{:S(2)}, u32[]{:S(2)}) collective-permute-start(bf16[1,1,384,512]{3,2,1,0:T(8,128)(2,1)} %get-tuple-element.15), channel_id=1, source_target_pairs={{2,0},{4,2},{6,4},{8,6},{10,8},{12,10},{14,12},{3,1},{5,3},{7,5},{... | collective-permute-start | bytes 1179656 | tf_op jit(solution)/shard_map/ppermute | solution.py:20
  131.7 5.2 copy-start.5
  148.6 2.7 copy-start.4
  159.6 19.0 %copy-start.2 = (bf16[2,384,1024]{2,1,0:T(8,128)(2,1)}, bf16[2,384,1024]{2,1,0:T(8,128)(2,1)S(1)}, u32[]{:S(2)}) copy-start(bf16[2,384,1024]{2,1,0:T(8,128)(2,1)S(1)} %get-tuple-element.8) | copy-start | bytes 4718596
  180.9 1.4 copy-start.3
  180.9 348.8 %all-reduce.5.cloned.1.call-start = ((), (), s32[]{:S(2)}) async-start(), calls=%async_computation.3 | async-start | bytes 4718592 | tf_op jit(solution)/shard_map/psum | solution.py:128
  182.4 13.1 %collective-permute-start.2 = (bf16[1,1,384,1024]{3,2,1,0:T(8,128)(2,1)S(1)}, bf16[1,1,384,1024]{3,2,1,0:T(8,128)(2,1)S(1)}, u32[]{:S(2)}, u32[]{:S(2)}) collective-permute-start(bf16[1,1,384,1024]{3,2,1,0:T(8,128)(2,1)S(1)} %get-tuple-element.13), channel_id=1, source_target_pairs={{0,2},{2,4},{4,6},{6,8},{8,10},{10,12},{12,14},{1,3},{3,5},{5,7},{... | collective-permute-start | bytes 2359304 | tf_op jit(solution)/shard_map/ppermute | solution.py:18
  186.6 13.7 %collective-permute-start.3 = (bf16[1,1,384,1024]{3,2,1,0:T(8,128)(2,1)S(1)}, bf16[1,1,384,1024]{3,2,1,0:T(8,128)(2,1)S(1)}, u32[]{:S(2)}, u32[]{:S(2)}) collective-permute-start(bf16[1,1,384,1024]{3,2,1,0:T(8,128)(2,1)S(1)} %get-tuple-element.12), channel_id=1, source_target_pairs={{2,0},{4,2},{6,4},{8,6},{10,8},{12,10},{14,12},{3,1},{5,3},{7,5},{... | collective-permute-start | bytes 2359304 | tf_op jit(solution)/shard_map/ppermute | solution.py:20
  201.3 4.2 copy-start.6
  388.3 296.1 %all-reduce.7.cloned.1.call-start = ((), (), s32[]{:S(2)}) async-start(), calls=%async_computation.4 | async-start | bytes 2457600 | tf_op jit(solution)/shard_map/psum | solution.py:137
  388.6 2.4 copy-start.7
  395.4 2.4 copy-start.9
  395.4 2.4 copy-start.10
  395.4 2.7 copy-start.11
  395.4 3.1 copy-start.12
  402.0 1.9 copy-start.8
  408.7 278.1 %copy-start.1 = (bf16[600,512]{1,0:T(8,128)(2,1)S(1)}, bf16[600,512]{1,0:T(8,128)(2,1)}, u32[]{:S(2)}) copy-start(bf16[600,512]{1,0:T(8,128)(2,1)} %param.6) | copy-start | bytes 1843204
Sparse Core Ops, SparseCore 0:
  10.3 121.2 all-gather.1
  181.0 207.1 reduce-scatter.1
  390.9 138.6 all-reduce.4
  535.6 148.7 all-reduce.6
where the time goes:
time: 694 us; the launch traced here: 693 us
  waiting for transfers between devices  555 us (80%)
  matrix products  76.6 us (11%)
  local copies, waits for them, and re-layouts  29.5 us (4%)
  between operations  14.6 us (2%)
  starting transfers between devices  13.3 us (2%)
    reduce_scatter x1, waiting for transfers between devices, shards(): lax.psum_scatter(weight_term(padded, slopes), 'fsdp', scatter_dimension=0...  179 us
    psum x1, waiting for transfers between devices, shards(): grad_table = lax.psum(table_term, ('fsdp', 'tile', 'dp'))  152 us
    psum x1, waiting for transfers between devices, shards(): grad_weight = lax.psum(weight_partial, ('tile', 'dp'))  119 us
    all_gather x1, waiting for transfers between devices, shards(): lax.all_gather(conv_weight, 'fsdp', axis=0, tiled=True)  100 us
    dot_general x9, matrix products, conv_rows(): lax.dot_general(window, taps, (((3,), (1,)), ((), ())), preferred_element...  27.9 us
    dot_general x9, matrix products, input_term(): lax.dot_general(window, taps, (((3,), (0,)), ((), ())), preferred_element...  27.2 us
    dot_general x9, matrix products, weight_term(): lax.dot_general(slopes, window, (((0, 1, 2), (0, 1, 2)), ((), ())), prefe...  21.3 us
  transfers between devices with their start and end apart: 8, of which 6 were waited for; matrix products, arithmetic and copies ran while one was open for 8% of the time, Pallas kernels for 0%

commit v1 on v0

v1 whole, which is shorter than its diff:
```python
import jax
import jax.numpy as jnp
from jax import lax
from jax.experimental import pallas as pl
from jax.experimental.pallas import tpu as pltpu
from jax.sharding import PartitionSpec as P

inv_root_two = 0.7071067811865476
inv_root_tau = 0.3989422804014327

WIDTH = 384
CIN = 512
HALF = 512
PARTS = 6
PCOLS = 768
CHUNKS = 18

DIMS = 6

GATHER = [
    (0, (3, 4, 5), (2, 1, 0)),
    (1, (3, 4, 5), (0, 2, 1)),
    (2, (3, 4, 5), (1, 0, 2)),
    (3, (), (2, 1, 0, 5, 4, 3)),
    (4, (3,), (2, 1, 0, 5, 4)),
    (5, (4, 3), (2, 1, 0, 5)),
]
REDUCE = [tuple((i + k) % DIMS for k in range(DIMS)) for i in range(PARTS)]
SPREAD = [((3, 4, 5)[g:] + (3, 4, 5)[:g]) for g in range(3)]

G_STEPS = sum(len(order) for _, _, order in GATHER)
MESH = pl.DeviceIdType.MESH


def kernel(
    feat, weight, cot, id_row,
    up_out, gw_out, gf_out, tab_out,
    xs, ss, st, wall, gwb, rcv, fin, ctv, upb, wide_a, wide_b, acc, igp, igr, gfb,
    trow, tpeer, tall,
    loc_sem, x_send, x_recv, g_send, g_recv, s_send, s_recv, r_send, r_recv,
    f_send, f_recv, u_send, u_recv, i_send, i_recv, t_send, t_recv, v_send, v_recv,
):
    f = lax.axis_index("fsdp")
    t = lax.axis_index("tile")
    lo = lax.axis_index("dp")
    x, h = f // 2, f % 2
    z, c = t // 2, t % 2
    xa, xb = x // 2, x % 2
    xe = (xa + xb) % 2
    ye = (h + lo) % 2
    za = z // 2
    ze = (za + z % 2) % 2
    keep = (c + xe) % 2
    active = c == xa
    mine = {1: keep, 2: h, 3: ye, 4: za, 5: ze}
    x_flip = x + 1 - 2 * xb
    z_flip = z + 1 - 2 * (z % 2)
    partner = {
        0: {"fsdp": (3 - x) * 2 + h},
        1: {"fsdp": x_flip * 2 + h},
        2: {"fsdp": x * 2 + 1 - h, "dp": 1 - lo},
        3: {"dp": 1 - lo},
        4: {"tile": (3 - z) * 2 + c},
        5: {"tile": z_flip * 2 + c},
    }
    other_core = {"tile": 2 * z + 1 - c}

    def remote(src, dst, send_sem, recv_sem, device):
        return pltpu.make_async_remote_copy(
            src_ref=src, dst_ref=dst, send_sem=send_sem, recv_sem=recv_sem,
            device_id=device, device_id_type=MESH,
        )

    barrier = pltpu.get_barrier_semaphore()
    for k in range(1, 8):
        pl.semaphore_signal(barrier, inc=1, device_id={"tile": (t + k) % 8}, device_id_type=MESH)
    frame = f * 2 + lo
    for k in range(1, 16):
        to = (frame + k) % 16
        pl.semaphore_signal(
            barrier, inc=1, device_id={"fsdp": to // 2, "dp": to % 2}, device_id_type=MESH
        )

    own_x = pltpu.make_async_copy(feat, xs.at[1, pl.ds(1 + 2 * c, 2)], loc_sem.at[0])
    own_x.start()
    own_w = []
    for part, full, order in GATHER:
        at = [slice(None) if d in full else mine[d] for d in (3, 4, 5)]
        own_w.append(
            pltpu.make_async_copy(
                weight.at[at[0], at[1], at[2], :, pl.ds(PCOLS * part, PCOLS)],
                wall.at[part, keep, h, at[0], at[1], at[2]],
                loc_sem.at[1 + part],
            )
        )

    @pl.when(active)
    def _():
        for copy in own_w:
            copy.start()

    own_ct = []
    for k in range(2):
        own_ct.append(
            pltpu.make_async_copy(cot.at[2 * k + c], ctv.at[2 * c + k], loc_sem.at[7 + k])
        )
        own_ct[-1].start()

    pl.semaphore_wait(barrier, 22)

    copies = {}
    base = 0
    for part, full, order in GATHER:
        done = set(full)
        for k, dim in enumerate(order):
            at = (part,) + tuple(slice(None) if d in done else mine[d] for d in range(1, 6))
            copies[part, k] = remote(
                wall.at[at], wall.at[at], g_send.at[base + k], g_recv.at[base + k], partner[dim]
            )
            done.add(dim)
        base += len(order)

    def when(condition, body):
        if condition is None:
            body()
        else:
            pl.when(condition)(body)

    def g_sends(order, k):
        return None if 0 in order[:k] else active

    def g_recvs(order, k):
        if order[k] == 0:
            return c != xa
        return None if 0 in order[:k] else active

    def gather_step(k):
        for part, _, order in GATHER:
            if k > 0 and k - 1 < len(order):
                when(g_recvs(order, k - 1), copies[part, k - 1].wait_recv)
            if k < len(order):
                if k == 0:
                    def first(part=part):
                        own_w[part].wait()
                        copies[part, 0].start()
                    when(active, first)
                else:
                    when(g_sends(order, k), copies[part, k].start)

    gather_step(0)

    own_x.wait()
    x_pair = remote(
        xs.at[1, pl.ds(1 + 2 * c, 2)], xs.at[1, pl.ds(1 + 2 * c, 2)], x_send.at[0], x_recv.at[0], other_core
    )
    x_pair.start()
    x_pair_in = remote(
        xs.at[1, pl.ds(3 - 2 * c, 2)], xs.at[1, pl.ds(3 - 2 * c, 2)], x_send.at[0], x_recv.at[0], other_core
    )
    sends_rim = jnp.where(c == 0, z > 0, z < 3)
    z_rim = jnp.where(c == 0, jnp.maximum(z - 1, 0), jnp.minimum(z + 1, 3))
    rim_out = [
        remote(xs.at[1, 1 + 3 * c], xs.at[1, 5 - 5 * c], x_send.at[1 + k], x_recv.at[1 + c], {"tile": 2 * z_rim + k})
        for k in range(2)
    ]

    @pl.when(sends_rim)
    def _():
        for copy in rim_out:
            copy.start()

    top_in = remote(xs.at[1, 0], xs.at[1, 0], x_send.at[1], x_recv.at[2], other_core)
    bottom_in = remote(xs.at[1, 5], xs.at[1, 5], x_send.at[1], x_recv.at[1], other_core)

    ct_pair = []
    for k in range(2):
        ct_pair.append(
            remote(cot.at[2 * k + 1 - c], ctv.at[2 * c + k], x_send.at[3 + k], x_recv.at[3 + k], other_core)
        )
        ct_pair[-1].start()

    gather_step(1)

    @pl.when(z == 0)
    def _():
        xs[1, 0] = jnp.zeros((WIDTH, CIN), jnp.bfloat16)
        ss[1, 0] = jnp.zeros((WIDTH, HALF), jnp.bfloat16)

    @pl.when(z == 3)
    def _():
        xs[1, 5] = jnp.zeros((WIDTH, CIN), jnp.bfloat16)
        ss[1, 5] = jnp.zeros((WIDTH, HALF), jnp.bfloat16)

    column = lax.broadcasted_iota(jnp.int32, (WIDTH, 128), 0)

    def shift_row(ref, row):
        for lane in range(4):
            at = pl.ds(128 * lane, 128)
            values = ref[1, row, :, at].astype(jnp.float32)
            right = jnp.where(column == 0, 0.0, pltpu.roll(values, 1, 0))
            left = jnp.where(column == WIDTH - 1, 0.0, pltpu.roll(values, WIDTH - 1, 0))
            ref[0, row, :, at] = right.astype(jnp.bfloat16)
            ref[2, row, :, at] = left.astype(jnp.bfloat16)

    def shift_rows(ref, first, count):
        @pl.loop(0, count)
        def _(k):
            shift_row(ref, first + k)

    shift_rows(xs, 1 + 2 * c, 2)
    gather_step(2)
    x_pair_in.wait_recv()
    shift_rows(xs, 3 - 2 * c, 2)
    gather_step(3)
    pl.when(z > 0)(top_in.wait_recv)
    pl.when(z < 3)(bottom_in.wait_recv)
    shift_rows(xs, 0, 1)
    shift_rows(xs, 5, 1)
    gather_step(4)
    for copy in own_ct:
        copy.wait()
    for copy in ct_pair:
        copy.wait_recv()
    gather_step(5)
    gather_step(6)

    def weight_rows(v):
        return jnp.concatenate(
            [
                wall[kk // 3, v, :, :, :, :, :, 256 * (kk % 3) : 256 * (kk % 3) + 256].reshape(256, 256)
                for kk in range(CHUNKS)
            ],
            axis=1,
        )

    def forward_row(r):
        lhs = jnp.concatenate(
            [
                xs[(kk // 2) % 3, r + kk // 6, :, 256 * (kk % 2) : 256 * (kk % 2) + 256]
                for kk in range(CHUNKS)
            ],
            axis=1,
        )
        for v in range(2):
            acc[:, 256 * v : 256 * v + 256] = lax.dot_general(
                lhs, weight_rows(v), (((1,), (1,)), ((), ())), preferred_element_type=jnp.float32
            )
        for lane in range(2):
            wide_a[lane] = ctv[r, :, 128 * lane : 128 * lane + 128].astype(jnp.float32)

        @pl.loop(0, WIDTH // 32)
        def _(j):
            j = pl.multiple_of(j * 32, 32)
            for v in range(2):
                for lane in range(2):
                    at = pl.ds(256 * v + 128 * lane, 128)
                    value = acc[pl.ds(j, 32), at]
                    grown = 0.5 * (1.0 + lax.erf(value * inv_root_two))
                    slope = grown + value * jnp.exp(-0.5 * value * value) * inv_root_tau
                    spots = pl.ds(2 * j + v, 32, 2)
                    wide_b[lane, spots, :] = value * grown
                    ss[1, r + 1, pl.ds(j, 32), at] = (wide_a[lane, spots, :] * slope).astype(jnp.bfloat16)

        for lane in range(2):
            upb[r, :, 128 * lane : 128 * lane + 128] = wide_b[lane].astype(jnp.bfloat16)

    @pl.loop(0, 2)
    def _(k):
        forward_row(3 * k)

    slope_up = remote(ss.at[1, 1], ss.at[1, 5], s_send.at[0], s_recv.at[0], {"tile": 2 * jnp.maximum(z - 1, 0) + c})
    slope_down = remote(ss.at[1, 4], ss.at[1, 0], s_send.at[1], s_recv.at[1], {"tile": 2 * jnp.minimum(z + 1, 3) + c})
    pl.when(z > 0)(slope_up.start)
    pl.when(z < 3)(slope_down.start)

    @pl.loop(0, 2)
    def _(k):
        forward_row(2 - k)

    up_own, up_pair = [], []
    for k in range(2):
        up_own.append(pltpu.make_async_copy(upb.at[2 * c + k], up_out.at[2 * k + c], loc_sem.at[9 + k]))
        up_pair.append(
            remote(upb.at[2 * (1 - c) + k], up_out.at[2 * k + c], u_send.at[k], u_recv.at[k], other_core)
        )
        up_own[-1].start()
        up_pair[-1].start()

    for r in range(4):
        st[:, WIDTH * r : WIDTH * r + WIDTH] = ss[1, r + 1].T

    sums = {}
    for part, order in enumerate(REDUCE):
        earlier = []
        for k, dim in enumerate(order):
            src = [part]
            dst = [part, 1 if 0 in earlier else 0]
            here = [part]
            got = [part, 1 if 0 in earlier else 0]
            for d in range(1, 6):
                if d in earlier:
                    src.append(mine[d])
                    here.append(mine[d])
                    dst.append(1 - mine[d])
                    got.append(1 - mine[d])
                elif d == dim:
                    src.append(1 - mine[d])
                    here.append(mine[d])
                    dst.append(1 - mine[d])
                    got.append(mine[d])
                else:
                    for at in (src, dst, here, got):
                        at.append(slice(None))
            copy = remote(
                gwb.at[tuple(src)], rcv.at[tuple(dst)], r_send.at[part, k], r_recv.at[part, k], partner[dim]
            )
            sums[part, k] = (copy, tuple(here), tuple(got))
            earlier.append(dim)

    def r_sends(order, k):
        if order[k] == 0:
            return c != xa
        return active if 0 in order[:k] else None

    def r_recvs(order, k):
        return active if 0 in order[: k + 1] else None

    def reduce_step(part, k):
        order = REDUCE[part]
        if k > 0:
            copy, here, got = sums[part, k - 1]

            def add():
                copy.wait_recv()
                total = gwb[here].astype(jnp.float32) + rcv[got].astype(jnp.float32)
                total = total.astype(jnp.bfloat16)
                if k < DIMS:
                    gwb[here] = total
                else:
                    fin[part, ye, za, ze] = total

            when(r_recvs(order, k - 1), add)
        if k < DIMS:
            when(r_sends(order, k), sums[part, k][0].start)

    for part in range(PARTS):
        for j in range(3):
            kk = 3 * part + j
            window = xs[(kk // 2) % 3, kk // 6 : kk // 6 + 4, :, 256 * (kk % 2) : 256 * (kk % 2) + 256]
            term = jnp.dot(
                st[...], window.reshape(4 * WIDTH, 256), preferred_element_type=jnp.float32
            )
            gwb[part, :, :, :, :, :, :, 256 * j : 256 * j + 256] = term.astype(jnp.bfloat16).reshape(
                2, 2, 2, 2, 2, 16, 256
            )
        reduce_step(part, 0)

    pl.when(z > 0)(lambda: remote(ss.at[1, 0], ss.at[1, 0], s_send.at[1], s_recv.at[1], other_core).wait_recv())
    pl.when(z < 3)(lambda: remote(ss.at[1, 5], ss.at[1, 5], s_send.at[0], s_recv.at[0], other_core).wait_recv())
    shift_rows(ss, 0, 6)

    def input_row(r, out):
        lhs = jnp.concatenate([ss[2 - tap % 3, r + 2 - tap // 3] for tap in range(9)], axis=1)
        for e in range(2):
            chunks = []
            for tap in range(9):
                kk = 2 * tap + e
                chunks.append(
                    wall[kk // 3, :, :, :, :, :, :, 256 * (kk % 3) : 256 * (kk % 3) + 256].reshape(512, 256)
                )
            out[:, 256 * e : 256 * e + 256] = jnp.dot(
                lhs, jnp.concatenate(chunks, axis=0), preferred_element_type=jnp.float32
            )

    @pl.loop(0, 2)
    def _(k):
        input_row(2 * (1 - c) + k, igp.at[k])

    ig_pair = remote(igp, igr, i_send.at[0], i_recv.at[0], other_core)
    ig_pair.start()
    for part in range(PARTS):
        reduce_step(part, 1)

    trow[4:8, :] = id_row[4:8, :]
    trow[0:4, :] = jnp.zeros((4, 128), jnp.float32)

    @pl.loop(0, 2)
    def _(k):
        input_row(2 * c + k, acc)

        @pl.when(k == 0)
        def _():
            ig_pair.wait_recv()

        total = acc[...] + igr[k]
        gfb[k] = total.astype(jnp.bfloat16)
        column_sum = jnp.sum(total, axis=0, keepdims=True)
        for lane in range(4):
            trow[lane : lane + 1, :] += column_sum[:, 128 * lane : 128 * lane + 128]

    gf_copy = pltpu.make_async_copy(gfb, gf_out, loc_sem.at[11])
    gf_copy.start()

    t_copies = []
    for k in range(1, 8):
        copy = remote(trow, tpeer.at[k - 1], t_send.at[k - 1], t_recv.at[k - 1], {"tile": (t + k) % 8})
        copy.start()
        t_copies.append(copy)

    for part in range(PARTS):
        reduce_step(part, 2)

    for copy in t_copies:
        copy.wait_recv()
    for copy in t_copies:
        copy.wait_send()
    total = trow[0:4, :]
    for k in range(7):
        total = total + tpeer[k, 0:4, :]
    tall[0, 0:4, :] = total
    tall[0, 4:8, :] = trow[4:8, :]
    v_copies = []
    for k in range(1, 16):
        to = (frame + k) % 16
        copy = remote(
            tall.at[0], tall.at[k], v_send.at[k - 1], v_recv.at[k - 1], {"fsdp": to // 2, "dp": to % 2}
        )
        copy.start()
        v_copies.append(copy)

    for k in range(3, 7):
        for part in range(PARTS):
            reduce_step(part, k)

    spreads = {}
    for g, order in enumerate(SPREAD):
        done = set()
        for k, dim in enumerate(order):
            at = (pl.ds(2 * g, 2),) + tuple(slice(None) if d in done else mine[d] for d in (3, 4, 5))
            spreads[g, k] = remote(fin.at[at], fin.at[at], f_send.at[g, k], f_recv.at[g, k], partner[dim])
            done.add(dim)

    to_pair = [
        remote(fin.at[pl.ds(2 * g, 2)], gw_out.at[pl.ds(2 * g, 2)], i_send.at[1 + g], i_recv.at[1 + g], other_core)
        for g in range(3)
    ]
    to_self = [
        pltpu.make_async_copy(fin.at[pl.ds(2 * g, 2)], gw_out.at[pl.ds(2 * g, 2)], loc_sem.at[12 + g])
        for g in range(3)
    ]

    @pl.when(active)
    def _():
        for k in range(4):
            for g in range(3):
                if k > 0:
                    spreads[g, k - 1].wait_recv()
                if k < 3:
                    spreads[g, k].start()
                else:
                    to_pair[g].start()
                    to_self[g].start()
        for g in range(3):
            to_self[g].wait()
            to_pair[g].wait_send()
            for k in range(3):
                spreads[g, k].wait_send()

    @pl.when(c != xa)
    def _():
        for g in range(3):
            to_pair[g].wait_recv()

    for copy in v_copies:
        copy.wait()
    tab_copy = pltpu.make_async_copy(tall, tab_out, loc_sem.at[15])
    tab_copy.start()

    for part, _, order in GATHER:
        for k in range(len(order)):
            when(g_sends(order, k), copies[part, k].wait_send)
    for part, order in enumerate(REDUCE):
        for k in range(DIMS):
            when(r_sends(order, k), sums[part, k][0].wait_send)
    x_pair.wait_send()

    @pl.when(sends_rim)
    def _():
        for copy in rim_out:
            copy.wait_send()

    for copy in ct_pair:
        copy.wait_send()
    pl.when(z > 0)(slope_up.wait_send)
    pl.when(z < 3)(slope_down.wait_send)
    for k in range(2):
        up_own[k].wait()
        up_pair[k].wait()
    ig_pair.wait_send()
    gf_copy.wait()
    tab_copy.wait()


def fused(inputs, weight, cot, id_row):
    any_space = pl.BlockSpec(memory_space=pl.ANY)
    vmem = pl.BlockSpec(memory_space=pltpu.VMEM)
    bf16, f32 = jnp.bfloat16, jnp.float32
    dma = pltpu.SemaphoreType.DMA
    return pl.pallas_call(
        kernel,
        out_shape=(
            jax.ShapeDtypeStruct((4, 2 * WIDTH, 256), bf16),
            jax.ShapeDtypeStruct((PARTS, 2, 2, 2, 16, PCOLS), bf16),
            jax.ShapeDtypeStruct((2, WIDTH, CIN), bf16),
            jax.ShapeDtypeStruct((16, 8, 128), f32),
        ),
        in_specs=[any_space, any_space, any_space, vmem],
        out_specs=[any_space] * 4,
        scratch_shapes=[
            pltpu.VMEM((3, 6, WIDTH, CIN), bf16),
            pltpu.VMEM((3, 6, WIDTH, HALF), bf16),
            pltpu.VMEM((HALF, 4 * WIDTH), bf16),
            pltpu.VMEM((PARTS, 2, 2, 2, 2, 2, 16, PCOLS), bf16),
            pltpu.VMEM((PARTS, 2, 2, 2, 2, 2, 16, PCOLS), bf16),
            pltpu.VMEM((PARTS, 2, 2, 2, 2, 2, 2, 16, PCOLS), bf16),
            pltpu.VMEM((PARTS, 2, 2, 2, 16, PCOLS), bf16),
            pltpu.VMEM((4, 2 * WIDTH, 256), bf16),
            pltpu.VMEM((4, 2 * WIDTH, 256), bf16),
            pltpu.VMEM((2, 2 * WIDTH, 128), f32),
            pltpu.VMEM((2, 2 * WIDTH, 128), f32),
            pltpu.VMEM((WIDTH, 512), f32),
            pltpu.VMEM((2, WIDTH, CIN), f32),
            pltpu.VMEM((2, WIDTH, CIN), f32),
            pltpu.VMEM((2, WIDTH, CIN), bf16),
            pltpu.VMEM((8, 128), f32),
            pltpu.VMEM((7, 8, 128), f32),
            pltpu.VMEM((16, 8, 128), f32),
            dma((16,)),
            dma((5,)),
            dma((5,)),
            dma((G_STEPS,)),
            dma((G_STEPS,)),
            dma((2,)),
            dma((2,)),
            dma((PARTS, DIMS)),
            dma((PARTS, DIMS)),
            dma((3, 3)),
            dma((3, 3)),
            dma((2,)),
            dma((2,)),
            dma((4,)),
            dma((4,)),
            dma((7,)),
            dma((7,)),
            dma((15,)),
            dma((15,)),
        ],
        compiler_params=pltpu.CompilerParams(
            collective_id=0, has_side_effects=True, vmem_limit_bytes=60 * 2**20
        ),
        cost_estimate=pl.CostEstimate(
            flops=6 * 768 * 4608 * 1024, bytes_accessed=2 * 10**7, transcendentals=3 * 768 * 1024
        ),
        name="conv_block",
    )(inputs, weight, cot, id_row)


def shards(features, frame_table, frame_ids, conv_weight, cotangent):
    video_len = frame_table.shape[0]
    shift = lax.dynamic_slice_in_dim(frame_table, frame_ids[0], 1, axis=0).astype(jnp.float32)
    inputs = (features[0].astype(jnp.float32) + shift[None]).astype(jnp.bfloat16)
    id_row = jnp.broadcast_to(frame_ids.astype(jnp.float32)[:, None], (8, 128))
    up, gw, gf, tab = fused(
        inputs, conv_weight.reshape(2, 2, 2, 16, 9 * CIN), cotangent[0], id_row
    )
    sums = tab[:, :4].reshape(16, CIN)
    frames = tab[:, 4, 0]
    picker = (frames[:, None] == jnp.arange(video_len, dtype=jnp.float32)[None, :]).astype(jnp.float32)
    grad_table = lax.dot_general(
        picker, sums, (((0,), (0,)), ((), ())),
        precision=lax.Precision.HIGHEST, preferred_element_type=jnp.float32,
    )
    grad_weight = gw.reshape(PARTS, 128, PCOLS).transpose(1, 0, 2).reshape(128, 9 * CIN).astype(jnp.float32)
    return (up[None], grad_weight, gf[None], grad_table)


def solution(mesh):
    return jax.shard_map(
        shards,
        mesh=mesh,
        in_specs=(
            P(("fsdp", "dp"), "tile", None, None),
            P(),
            P(("fsdp", "dp")),
            P("fsdp", None),
            P(("fsdp", "dp"), "tile", None, None),
        ),
        out_specs=(
            P(("fsdp", "dp"), "tile", None, None),
            P("fsdp", None),
            P(("fsdp", "dp"), "tile", None, None),
            P(),
        ),
        check_vma=False,
    )
```

time: 694 us -> 143 us (0.21)
  waiting for transfers between devices: 555 us -> 0 us
  Pallas kernels: 0 us -> 127 us
  matrix products: 76.6 us -> 1.8 us
  local copies, waits for them, and re-layouts: 29.5 us -> 8.51 us
  starting transfers between devices: 13.3 us -> 0 us
  between operations: 14.6 us -> 1.31 us
    psum x2 -> x0, waiting for transfers between devices: 271 us -> none  [the longest x1 152 us: shards(): grad_table = lax.psum(table_term, ('fsdp', 'tile', 'dp'))]
    reduce_scatter x1 -> x0, waiting for transfers between devices: 179 us -> none  [shards(): lax.psum_scatter(weight_term(padded, slopes), 'fsdp', scatter_dimension=0...]
    pallas_call x0 -> x1, Pallas kernels: none -> 127 us  [fused(): pl.pallas_call(kernel, out_shape=(jax.ShapeDtypeStruct((4, 2 * WIDTH, 256...]
    all_gather x1 -> x0, waiting for transfers between devices: 100 us -> none  [shards(): lax.all_gather(conv_weight, 'fsdp', axis=0, tiled=True)]
    dot_general x28 -> x1, matrix products: 76.6 us -> 1.8 us  [shards(): lax.dot_general(picker, sums, (((0,), (0,)), ((), ())), precision=lax.Pre...]
    ppermute x4 -> x0, starting transfers between devices: 12.9 us -> none  [the longest x2 9.08 us: extended(): lax.ppermute(tail, axis, [(i, (i + 1) % count) for i in range(ends)])]
    convert_element_type x3 -> x1, local copies, waits for them, and re-layouts: 13.3 us -> 1.98 us  [shards(): gw.reshape(PARTS, 128, PCOLS).transpose(1, 0, 2).reshape(128, 9 * CIN)]
  transfers between devices with their start and end apart: 8 -> 0, of which waited for: 6 -> 0; matrix products, arithmetic and copies ran while one was open for 8% -> 0% of each run, Pallas kernels for 0% -> 0%
where the time goes in v1:
time: 143 us
  Pallas kernels  127 us (89%)
  local copies, waits for them, and re-layouts  8.51 us (6%)
  other arithmetic  4.33 us (3%)
  matrix products  1.8 us (1%)
    pallas_call x1, Pallas kernels, fused(): pl.pallas_call(kernel, out_shape=(jax.ShapeDtypeStruct((4, 2 * WIDTH, 256...  127 us
    unnamed x9, local copies, waits for them, and re-layouts  5.73 us

profile of v1, /device:TPU:1, one launch (start us, length us, event | category | flops | bytes accessed | tf_op | source)
XLA Modules:
  0.0 142.9 jit_solution(15438885089528743298)
XLA Ops:
  1.3 0.7 dynamic-slice_convert_fusion
  2.0 2.2 %fusion.feat = bf16[2,384,512]{2,1,0:T(8,128)(2,1)} fusion(bf16[1,2,384,512]{3,2,1,0:T(8,128)(2,1)} %param.5, f32[512]{0:T(512)S(1)} %bitcast.27), kind=kLoop, calls=%fused_computation.1 | loop fusion | flops 1179648 | bytes 1574912 | tf_op jit(solution)/shard_map/convert_element_type | solution.py:571
  4.1 0.6 broadcast_in_dim.17.id_row
  4.7 127.0 %conv_block.1 = (bf16[4,768,256]{2,1,0:T(8,128)(2,1)}, bf16[6,2,2,2,16,768]{5,4,3,2,1,0:T(8,128)(2,1)}, bf16[2,384,512]{2,1,0:T(8,128)(2,1)}, f32[16,8,128]{2,1,0:T(8,128)}) custom-call(bf16[2,384,512]{2,1,0:T(8,128)(2,1)} %fusion.feat, bf16[2,2,2,16,4608]{4,3,2,1,0:T(8,128)(2,1)} %bitcast.29, bf16[4,768,256]{2,1,0:T(8,128)(2,1)} %bitcast.28, ...), custom_call_target="tpu_custom_call" | custom-call | flops 21743271936 | bytes 20000000 | tf_op jit(solution)/shard_map/conv_block/pallas_call | solution.py:509
  131.7 1.5 %bitcast_convert_fusion = f32[6,128,768]{2,1,0:T(8,128)S(1)} fusion(bf16[6,2,2,2,16,768]{5,4,3,2,1,0:T(8,128)(2,1)} %get-tuple-element.9), kind=kLoop, calls=%fused_computation.2 | loop fusion | flops 589824 | bytes 3538944 | tf_op jit(solution)/shard_map/convert_element_type | solution.py:583
  133.2 2.0 %copy.10 = f32[6,128,768]{1,2,0:T(8,128)} copy(f32[6,128,768]{2,1,0:T(8,128)S(1)} %bitcast_convert_fusion) | data formatting | bytes 4718592 | tf_op jit(solution)/shard_map/convert_element_type | solution.py:583
  135.2 0.0 copy-start.2
  135.2 0.0 copy-start
  135.2 3.2 %copy.11 = f32[128,4608]{1,0:T(8,128)} copy(f32[128,4608]{0,1:T(8,128)} %bitcast.23) | data formatting | bytes 4718592
  138.4 0.0 copy-done.2
  138.4 0.2 slice_reduce_fusion
  138.6 1.8 %fusion.1 = f32[600,512]{1,0:T(8,128)} fusion(f32[2,8,4,128]{3,2,1,0:T(4,128)S(1)} %bitcast.26, f32[16]{0:T(128)S(1)} %slice_reduce_fusion), kind=kOutput, calls=%fused_computation.4 | convolution fusion | flops 58992000 | bytes 1261632 | tf_op jit(solution)/shard_map/dot_general | solution.py:579
  140.4 0.0 copy-done
  140.4 0.0 copy-start.1
  140.4 1.1 copy.20
  141.5 0.5 copy-done.1
  142.1 0.9 copy.21
  (1 shorter events, 0.0 us)
Async XLA Ops:
  135.2 3.2 %copy-start.2 = (f32[16,8,128]{2,1,0:T(8,128)S(1)}, f32[16,8,128]{2,1,0:T(8,128)}, u32[]{:S(2)}) copy-start(f32[16,8,128]{2,1,0:T(8,128)} %get-tuple-element.11) | copy-start | bytes 196612
  135.2 5.2 %copy-start = (bf16[4,768,256]{2,1,0:T(8,128)(2,1)S(1)}, bf16[4,768,256]{2,1,0:T(8,128)(2,1)}, u32[]{:S(2)}) copy-start(bf16[4,768,256]{2,1,0:T(8,128)(2,1)} %get-tuple-element.8) | copy-start | bytes 4718596
  140.4 1.7 %copy-start.1 = (bf16[2,384,512]{2,1,0:T(8,128)(2,1)S(1)}, bf16[2,384,512]{2,1,0:T(8,128)(2,1)}, u32[]{:S(2)}) copy-start(bf16[2,384,512]{2,1,0:T(8,128)(2,1)} %get-tuple-element.10) | copy-start | bytes 2359300

commit v2 on v1

--- a/solution.py
+++ b/solution.py
@@ -17,28 +17,17 @@
 
 DIMS = 6
 
-GATHER = [
-    (0, (3, 4, 5), (2, 1, 0)),
-    (1, (3, 4, 5), (0, 2, 1)),
-    (2, (3, 4, 5), (1, 0, 2)),
-    (3, (), (2, 1, 0, 5, 4, 3)),
-    (4, (3,), (2, 1, 0, 5, 4)),
-    (5, (4, 3), (2, 1, 0, 5)),
-]
 REDUCE = [tuple((i + k) % DIMS for k in range(DIMS)) for i in range(PARTS)]
-SPREAD = [((3, 4, 5)[g:] + (3, 4, 5)[:g]) for g in range(3)]
-
-G_STEPS = sum(len(order) for _, _, order in GATHER)
 MESH = pl.DeviceIdType.MESH
 
 
 def kernel(
-    feat, weight, cot, id_row,
+    feat, weight, cot, shift_row, id_row,
     up_out, gw_out, gf_out, tab_out,
-    xs, ss, st, wall, gwb, rcv, fin, ctv, upb, wide_a, wide_b, acc, igp, igr, gfb,
+    xs, ss, st, wall, gwb, rcv, fin, ctv, cts, actv, upb, wide, acc, igp, igr, gfb,
     trow, tpeer, tall,
-    loc_sem, x_send, x_recv, g_send, g_recv, s_send, s_recv, r_send, r_recv,
-    f_send, f_recv, u_send, u_recv, i_send, i_recv, t_send, t_recv, v_send, v_recv,
+    loc_sem, x_send, x_recv, o_send, o_recv, n_send, n_recv, q_send, q_recv, s_send, s_recv,
+    r_send, r_recv, f_send, f_recv, u_send, u_recv, i_send, i_recv, t_send, t_recv, v_send, v_recv,
 ):
     f = lax.axis_index("fsdp")
     t = lax.axis_index("tile")
@@ -64,6 +53,11 @@
         5: {"tile": z_flip * 2 + c},
     }
     other_core = {"tile": 2 * z + 1 - c}
+    two_away = {"fsdp": (x + 2) % 4 * 2 + h}
+    quarter = (z + 2 * ye) % 4
+    holders = [
+        {"tile": (z + k // 2) % 4 * 2 + c, "dp": (lo + k % 2) % 2} for k in range(1, 8)
+    ]
 
     def remote(src, dst, send_sem, recv_sem, device):
         return pltpu.make_async_remote_copy(
@@ -81,18 +75,18 @@
             barrier, inc=1, device_id={"fsdp": to // 2, "dp": to % 2}, device_id_type=MESH
         )
 
+    for k in (3, 5, 7):
+        pl.semaphore_signal(barrier, inc=1, device_id=holders[k - 1], device_id_type=MESH)
+
+    near, far = keep, 1 - keep
     own_x = pltpu.make_async_copy(feat, xs.at[1, pl.ds(1 + 2 * c, 2)], loc_sem.at[0])
     own_x.start()
-    own_w = []
-    for part, full, order in GATHER:
-        at = [slice(None) if d in full else mine[d] for d in (3, 4, 5)]
-        own_w.append(
-            pltpu.make_async_copy(
-                weight.at[at[0], at[1], at[2], :, pl.ds(PCOLS * part, PCOLS)],
-                wall.at[part, keep, h, at[0], at[1], at[2]],
-                loc_sem.at[1 + part],
-            )
-        )
+    own_w = [
+        pltpu.make_async_copy(
+            weight.at[:, :, :, :, pl.ds(PCOLS * part, PCOLS)], wall.at[part, near, h], loc_sem.at[1 + part]
+        )
+        for part in range(PARTS)
+    ]
 
     @pl.when(active)
     def _():
@@ -106,71 +100,91 @@
         )
         own_ct[-1].start()
 
-    pl.semaphore_wait(barrier, 22)
-
-    copies = {}
-    base = 0
-    for part, full, order in GATHER:
-        done = set(full)
-        for k, dim in enumerate(order):
-            at = (part,) + tuple(slice(None) if d in done else mine[d] for d in range(1, 6))
-            copies[part, k] = remote(
-                wall.at[at], wall.at[at], g_send.at[base + k], g_recv.at[base + k], partner[dim]
+    own_x.wait()
+    for k in range(2):
+        for lane in range(4):
+            at = pl.ds(128 * lane, 128)
+            row = xs[1, 1 + 2 * c + k, :, at].astype(jnp.float32) + shift_row[:, at]
+            xs[1, 1 + 2 * c + k, :, at] = row.astype(jnp.bfloat16)
+
+    pl.semaphore_wait(barrier, 25)
+
+    def piece(pair, half, number):
+        return wall.at[:, pair, half, number // 2, number % 2]
+
+    def same(pair, half, number, send_sem, recv_sem, device):
+        return remote(piece(pair, half, number), piece(pair, half, number), send_sem, recv_sem, device)
+
+    turn = [(quarter + k) % 4 for k in range(4)]
+    to_flip = [same(near, h, turn[k], o_send.at[k], o_recv.at[k], partner[1]) for k in range(4)]
+    to_turn = [same(near, h, turn[k], o_send.at[4 + k], o_recv.at[4 + k], partner[0]) for k in range(4)]
+    to_far = same(near, h, quarter, o_send.at[8], o_recv.at[8], two_away)
+    from_flip = [same(far, h, turn[k], o_send.at[k], o_recv.at[k], partner[1]) for k in range(4)]
+    from_turn = to_turn
+    from_far = same(far, h, quarter, o_send.at[8], o_recv.at[8], two_away)
+    across = [same(pair, h, quarter, n_send.at[k], n_recv.at[k], partner[2]) for k, pair in enumerate((near, far))]
+    crossed = [same(pair, 1 - h, quarter, n_send.at[k], n_recv.at[k], partner[2]) for k, pair in enumerate((near, far))]
+    passed = {}
+    theirs = {3: (quarter + 2) % 4, 4: (3 - z + 2 * ye) % 4, 5: (z_flip + 2 * ye) % 4}
+    for k, (pair, half) in enumerate(((near, 1 - h), (far, 1 - h), (far, h))):
+        for j, dim in enumerate((3, 4, 5)):
+            passed[k, j] = (
+                same(pair, half, quarter, q_send.at[k, j], q_recv.at[k, j], partner[dim]),
+                same(pair, half, theirs[dim], q_send.at[k, j], q_recv.at[k, j], partner[dim]),
             )
-            done.add(dim)
-        base += len(order)
-
-    def when(condition, body):
-        if condition is None:
-            body()
-        else:
-            pl.when(condition)(body)
-
-    def g_sends(order, k):
-        return None if 0 in order[:k] else active
-
-    def g_recvs(order, k):
-        if order[k] == 0:
-            return c != xa
-        return None if 0 in order[:k] else active
-
-    def gather_step(k):
-        for part, _, order in GATHER:
-            if k > 0 and k - 1 < len(order):
-                when(g_recvs(order, k - 1), copies[part, k - 1].wait_recv)
-            if k < len(order):
-                if k == 0:
-                    def first(part=part):
-                        own_w[part].wait()
-                        copies[part, 0].start()
-                    when(active, first)
-                else:
-                    when(g_sends(order, k), copies[part, k].start)
-
-    gather_step(0)
-
-    own_x.wait()
+
+    def pass_on(k):
+        for j in range(3):
+            passed[k, j][0].start()
+
+    def passed_in(k):
+        for j in range(3):
+            passed[k, j][1].wait_recv()
+
+    @pl.when(active)
+    def _():
+        for copy in own_w:
+            copy.wait()
+        to_turn[0].start()
+        to_flip[0].start()
+        across[0].start()
+        to_far.start()
+        for k in range(1, 4):
+            to_turn[k].start()
+            to_flip[k].start()
+
     x_pair = remote(
         xs.at[1, pl.ds(1 + 2 * c, 2)], xs.at[1, pl.ds(1 + 2 * c, 2)], x_send.at[0], x_recv.at[0], other_core
     )
-    x_pair.start()
     x_pair_in = remote(
         xs.at[1, pl.ds(3 - 2 * c, 2)], xs.at[1, pl.ds(3 - 2 * c, 2)], x_send.at[0], x_recv.at[0], other_core
     )
+    rim_cols = WIDTH // 2
     sends_rim = jnp.where(c == 0, z > 0, z < 3)
     z_rim = jnp.where(c == 0, jnp.maximum(z - 1, 0), jnp.minimum(z + 1, 3))
     rim_out = [
-        remote(xs.at[1, 1 + 3 * c], xs.at[1, 5 - 5 * c], x_send.at[1 + k], x_recv.at[1 + c], {"tile": 2 * z_rim + k})
+        remote(
+            xs.at[1, 1 + 3 * c, pl.ds(rim_cols * k, rim_cols)],
+            xs.at[1, 5 - 5 * c, pl.ds(rim_cols * k, rim_cols)],
+            x_send.at[1 + k], x_recv.at[1 + c], {"tile": 2 * z_rim + k},
+        )
         for k in range(2)
     ]
 
+    def rim_part(row, core, sem):
+        at = xs.at[1, row, pl.ds(pl.multiple_of(rim_cols * core, rim_cols), rim_cols)]
+        return remote(at, at, x_send.at[sem], x_recv.at[sem], other_core)
+
+    top_in, bottom_in = rim_part(0, c, 2), rim_part(5, c, 1)
+    top_swap, bottom_swap = rim_part(0, c, 5), rim_part(5, c, 6)
+    top_swapped, bottom_swapped = rim_part(0, 1 - c, 5), rim_part(5, 1 - c, 6)
+
     @pl.when(sends_rim)
     def _():
         for copy in rim_out:
             copy.start()
 
-    top_in = remote(xs.at[1, 0], xs.at[1, 0], x_send.at[1], x_recv.at[2], other_core)
-    bottom_in = remote(xs.at[1, 5], xs.at[1, 5], x_send.at[1], x_recv.at[1], other_core)
+    x_pair.start()
 
     ct_pair = []
     for k in range(2):
@@ -178,8 +192,6 @@
             remote(cot.at[2 * k + 1 - c], ctv.at[2 * c + k], x_send.at[3 + k], x_recv.at[3 + k], other_core)
         )
         ct_pair[-1].start()
-
-    gather_step(1)
 
     @pl.when(z == 0)
     def _():
@@ -208,32 +220,64 @@
             shift_row(ref, first + k)
 
     shift_rows(xs, 1 + 2 * c, 2)
-    gather_step(2)
+
+    @pl.when(active)
+    def _():
+        from_flip[0].wait_recv()
+
+    @pl.when(c != xa)
+    def _():
+        from_turn[0].wait_recv()
+        across[0].start()
+        from_far.wait_recv()
+
+    across[1].start()
+    pl.when(c != xa)(lambda: pass_on(2))
+
     x_pair_in.wait_recv()
     shift_rows(xs, 3 - 2 * c, 2)
-    gather_step(3)
-    pl.when(z > 0)(top_in.wait_recv)
-    pl.when(z < 3)(bottom_in.wait_recv)
-    shift_rows(xs, 0, 1)
-    shift_rows(xs, 5, 1)
-    gather_step(4)
+
+    @pl.when(z > 0)
+    def _():
+        top_in.wait_recv()
+        top_swap.start()
+
+    @pl.when(z < 3)
+    def _():
+        bottom_in.wait_recv()
+        bottom_swap.start()
+
+    crossed[0].wait_recv()
+    pass_on(0)
+
     for copy in own_ct:
         copy.wait()
     for copy in ct_pair:
         copy.wait_recv()
-    gather_step(5)
-    gather_step(6)
-
-    def weight_rows(v):
-        return jnp.concatenate(
-            [
-                wall[kk // 3, v, :, :, :, :, :, 256 * (kk % 3) : 256 * (kk % 3) + 256].reshape(256, 256)
-                for kk in range(CHUNKS)
-            ],
-            axis=1,
-        )
-
-    def forward_row(r):
+
+    @pl.loop(0, 4)
+    def _(r):
+        for lane in range(2):
+            wide[lane] = ctv[r, :, 128 * lane : 128 * lane + 128].astype(jnp.float32)
+        for v in range(2):
+            for lane in range(2):
+                cts[v, r, :, 128 * lane : 128 * lane + 128] = wide[lane, pl.ds(v, WIDTH, 2), :].astype(jnp.bfloat16)
+
+    crossed[1].wait_recv()
+    pass_on(1)
+
+    @pl.when(z > 0)
+    def _():
+        top_swapped.wait_recv()
+
+    @pl.when(z < 3)
+    def _():
+        bottom_swapped.wait_recv()
+
+    shift_rows(xs, 0, 1)
+    shift_rows(xs, 5, 1)
+
+    def forward_row(v, r):
         lhs = jnp.concatenate(
             [
                 xs[(kk // 2) % 3, r + kk // 6, :, 256 * (kk % 2) : 256 * (kk % 2) + 256]
@@ -241,32 +285,52 @@
             ],
             axis=1,
         )
-        for v in range(2):
-            acc[:, 256 * v : 256 * v + 256] = lax.dot_general(
-                lhs, weight_rows(v), (((1,), (1,)), ((), ())), preferred_element_type=jnp.float32
-            )
-        for lane in range(2):
-            wide_a[lane] = ctv[r, :, 128 * lane : 128 * lane + 128].astype(jnp.float32)
+        rhs = jnp.concatenate(
+            [
+                wall[kk // 3, v, :, :, :, :, :, 256 * (kk % 3) : 256 * (kk % 3) + 256].reshape(256, 256)
+                for kk in range(CHUNKS)
+            ],
+            axis=1,
+        )
+        acc[:, :256] = lax.dot_general(
+            lhs, rhs, (((1,), (1,)), ((), ())), preferred_element_type=jnp.float32
+        )
 
         @pl.loop(0, WIDTH // 32)
         def _(j):
-            j = pl.multiple_of(j * 32, 32)
-            for v in range(2):
-                for lane in range(2):
-                    at = pl.ds(256 * v + 128 * lane, 128)
-                    value = acc[pl.ds(j, 32), at]
-                    grown = 0.5 * (1.0 + lax.erf(value * inv_root_two))
-                    slope = grown + value * jnp.exp(-0.5 * value * value) * inv_root_tau
-                    spots = pl.ds(2 * j + v, 32, 2)
-                    wide_b[lane, spots, :] = value * grown
-                    ss[1, r + 1, pl.ds(j, 32), at] = (wide_a[lane, spots, :] * slope).astype(jnp.bfloat16)
-
-        for lane in range(2):
-            upb[r, :, 128 * lane : 128 * lane + 128] = wide_b[lane].astype(jnp.bfloat16)
+            rows = pl.ds(pl.multiple_of(j * 32, 32), 32)
+            value = acc[rows, :256]
+            grown = 0.5 * (1.0 + lax.erf(value * inv_root_two))
+            slope = grown + value * jnp.exp(-0.5 * value * value) * inv_root_tau
+            actv[v, r, rows] = (value * grown).astype(jnp.bfloat16)
+            out = pl.ds(pl.multiple_of(256 * v, 256), 256)
+            ss[1, r + 1, rows, out] = (cts[v, r, rows].astype(jnp.float32) * slope).astype(jnp.bfloat16)
+
+    passed_in(0)
+
+    @pl.when(c != xa)
+    def _():
+        for k in range(1, 4):
+            from_turn[k].wait_recv()
+
+    @pl.loop(0, 4)
+    def _(r):
+        forward_row(near, r)
+
+    passed_in(1)
+
+    @pl.when(c != xa)
+    def _():
+        passed_in(2)
+
+    @pl.when(active)
+    def _():
+        for k in range(1, 4):
+            from_flip[k].wait_recv()
 
     @pl.loop(0, 2)
     def _(k):
-        forward_row(3 * k)
+        forward_row(far, 3 * k)
 
     slope_up = remote(ss.at[1, 1], ss.at[1, 5], s_send.at[0], s_recv.at[0], {"tile": 2 * jnp.maximum(z - 1, 0) + c})
     slope_down = remote(ss.at[1, 4], ss.at[1, 0], s_send.at[1], s_recv.at[1], {"tile": 2 * jnp.minimum(z + 1, 3) + c})
@@ -275,16 +339,7 @@
 
     @pl.loop(0, 2)
     def _(k):
-        forward_row(2 - k)
-
-    up_own, up_pair = [], []
-    for k in range(2):
-        up_own.append(pltpu.make_async_copy(upb.at[2 * c + k], up_out.at[2 * k + c], loc_sem.at[9 + k]))
-        up_pair.append(
-            remote(upb.at[2 * (1 - c) + k], up_out.at[2 * k + c], u_send.at[k], u_recv.at[k], other_core)
-        )
-        up_own[-1].start()
-        up_pair[-1].start()
+        forward_row(far, 2 - k)
 
     for r in range(4):
         st[:, WIDTH * r : WIDTH * r + WIDTH] = ss[1, r + 1].T
@@ -317,6 +372,12 @@
             sums[part, k] = (copy, tuple(here), tuple(got))
             earlier.append(dim)
 
+    def when(condition, body):
+        if condition is None:
+            body()
+        else:
+            pl.when(condition)(body)
+
     def r_sends(order, k):
         if order[k] == 0:
             return c != xa
@@ -428,47 +489,62 @@
         copy.start()
         v_copies.append(copy)
 
-    for k in range(3, 7):
+    @pl.loop(0, 4)
+    def _(r):
+        for lane in range(2):
+            lanes = pl.ds(128 * lane, 128)
+            for v in range(2):
+                wide[lane, pl.ds(v, WIDTH, 2), :] = actv[v, r, :, lanes].astype(jnp.float32)
+            upb[r, :, lanes] = wide[lane].astype(jnp.bfloat16)
+
+    up_own, up_pair = [], []
+    for k in range(2):
+        up_own.append(pltpu.make_async_copy(upb.at[2 * c + k], up_out.at[2 * k + c], loc_sem.at[9 + k]))
+        up_pair.append(
+            remote(upb.at[2 * (1 - c) + k], up_out.at[2 * k + c], u_send.at[k], u_recv.at[k], other_core)
+        )
+        up_own[-1].start()
+        up_pair[-1].start()
+
+    for k in range(3, 6):
         for part in range(PARTS):
             reduce_step(part, k)
 
-    spreads = {}
-    for g, order in enumerate(SPREAD):
-        done = set()
-        for k, dim in enumerate(order):
-            at = (pl.ds(2 * g, 2),) + tuple(slice(None) if d in done else mine[d] for d in (3, 4, 5))
-            spreads[g, k] = remote(fin.at[at], fin.at[at], f_send.at[g, k], f_recv.at[g, k], partner[dim])
-            done.add(dim)
-
-    to_pair = [
-        remote(fin.at[pl.ds(2 * g, 2)], gw_out.at[pl.ds(2 * g, 2)], i_send.at[1 + g], i_recv.at[1 + g], other_core)
-        for g in range(3)
-    ]
-    to_self = [
-        pltpu.make_async_copy(fin.at[pl.ds(2 * g, 2)], gw_out.at[pl.ds(2 * g, 2)], loc_sem.at[12 + g])
-        for g in range(3)
-    ]
+    spreads, to_pair, to_self = [], [], []
+    for g in range(2):
+        parts = pl.ds(3 * g, 3)
+        at = fin.at[parts, ye, za, ze]
+        spreads.append(
+            [remote(at, at, f_send.at[g, k], f_recv.at[g, k], holders[k]) for k in range(7)]
+        )
+        to_pair.append(remote(fin.at[parts], gw_out.at[parts], i_send.at[1 + g], i_recv.at[1 + g], other_core))
+        to_self.append(pltpu.make_async_copy(fin.at[parts], gw_out.at[parts], loc_sem.at[12 + g]))
+
+    for g in range(2):
+        for part in range(3 * g, 3 * g + 3):
+            reduce_step(part, 6)
+
+        @pl.when(active)
+        def _(g=g):
+            for copy in spreads[g]:
+                copy.start()
 
     @pl.when(active)
     def _():
-        for k in range(4):
-            for g in range(3):
-                if k > 0:
-                    spreads[g, k - 1].wait_recv()
-                if k < 3:
-                    spreads[g, k].start()
-                else:
-                    to_pair[g].start()
-                    to_self[g].start()
-        for g in range(3):
+        for g in range(2):
+            for copy in spreads[g]:
+                copy.wait_recv()
+            to_pair[g].start()
+            to_self[g].start()
+        for g in range(2):
+            for copy in spreads[g]:
+                copy.wait_send()
             to_self[g].wait()
             to_pair[g].wait_send()
-            for k in range(3):
-                spreads[g, k].wait_send()
 
     @pl.when(c != xa)
     def _():
-        for g in range(3):
+        for g in range(2):
             to_pair[g].wait_recv()
 
     for copy in v_copies:
@@ -476,9 +552,29 @@
     tab_copy = pltpu.make_async_copy(tall, tab_out, loc_sem.at[15])
     tab_copy.start()
 
-    for part, _, order in GATHER:
-        for k in range(len(order)):
-            when(g_sends(order, k), copies[part, k].wait_send)
+    @pl.when(active)
+    def _():
+        for copy in to_turn + to_flip + [to_far]:
+            copy.wait_send()
+
+    @pl.when(c != xa)
+    def _():
+        for j in range(3):
+            passed[2, j][0].wait_send()
+
+    for k in range(2):
+        across[k].wait_send()
+        for j in range(3):
+            passed[k, j][0].wait_send()
+
+    @pl.when(z > 0)
+    def _():
+        top_swap.wait_send()
+
+    @pl.when(z < 3)
+    def _():
+        bottom_swap.wait_send()
+
     for part, order in enumerate(REDUCE):
         for k in range(DIMS):
             when(r_sends(order, k), sums[part, k][0].wait_send)
@@ -501,7 +597,7 @@
     tab_copy.wait()
 
 
-def fused(inputs, weight, cot, id_row):
+def fused(features, weight, cot, shift_row, id_row):
     any_space = pl.BlockSpec(memory_space=pl.ANY)
     vmem = pl.BlockSpec(memory_space=pltpu.VMEM)
     bf16, f32 = jnp.bfloat16, jnp.float32
@@ -514,7 +610,7 @@
             jax.ShapeDtypeStruct((2, WIDTH, CIN), bf16),
             jax.ShapeDtypeStruct((16, 8, 128), f32),
         ),
-        in_specs=[any_space, any_space, any_space, vmem],
+        in_specs=[any_space, any_space, any_space, vmem, vmem],
         out_specs=[any_space] * 4,
         scratch_shapes=[
             pltpu.VMEM((3, 6, WIDTH, CIN), bf16),
@@ -525,8 +621,9 @@
             pltpu.VMEM((PARTS, 2, 2, 2, 2, 2, 2, 16, PCOLS), bf16),
             pltpu.VMEM((PARTS, 2, 2, 2, 16, PCOLS), bf16),
             pltpu.VMEM((4, 2 * WIDTH, 256), bf16),
+            pltpu.VMEM((2, 4, WIDTH, 256), bf16),
+            pltpu.VMEM((2, 4, WIDTH, 256), bf16),
             pltpu.VMEM((4, 2 * WIDTH, 256), bf16),
-            pltpu.VMEM((2, 2 * WIDTH, 128), f32),
             pltpu.VMEM((2, 2 * WIDTH, 128), f32),
             pltpu.VMEM((WIDTH, 512), f32),
             pltpu.VMEM((2, WIDTH, CIN), f32),
@@ -536,20 +633,24 @@
             pltpu.VMEM((7, 8, 128), f32),
             pltpu.VMEM((16, 8, 128), f32),
             dma((16,)),
-            dma((5,)),
-            dma((5,)),
-            dma((G_STEPS,)),
-            dma((G_STEPS,)),
+            dma((7,)),
+            dma((7,)),
+            dma((9,)),
+            dma((9,)),
+            dma((2,)),
+            dma((2,)),
+            dma((3, 3)),
+            dma((3, 3)),
             dma((2,)),
             dma((2,)),
             dma((PARTS, DIMS)),
             dma((PARTS, DIMS)),
-            dma((3, 3)),
-            dma((3, 3)),
+            dma((2, 7)),
+            dma((2, 7)),
             dma((2,)),
             dma((2,)),
-            dma((4,)),
-            dma((4,)),
+            dma((3,)),
+            dma((3,)),
             dma((7,)),
             dma((7,)),
             dma((15,)),
@@ -562,16 +663,15 @@
             flops=6 * 768 * 4608 * 1024, bytes_accessed=2 * 10**7, transcendentals=3 * 768 * 1024
         ),
         name="conv_block",
-    )(inputs, weight, cot, id_row)
+    )(features, weight, cot, shift_row, id_row)
 
 
 def shards(features, frame_table, frame_ids, conv_weight, cotangent):
     video_len = frame_table.shape[0]
     shift = lax.dynamic_slice_in_dim(frame_table, frame_ids[0], 1, axis=0).astype(jnp.float32)
-    inputs = (features[0].astype(jnp.float32) + shift[None]).astype(jnp.bfloat16)
     id_row = jnp.broadcast_to(frame_ids.astype(jnp.float32)[:, None], (8, 128))
     up, gw, gf, tab = fused(
-        inputs, conv_weight.reshape(2, 2, 2, 16, 9 * CIN), cotangent[0], id_row
+        features[0], conv_weight.reshape(2, 2, 2, 16, 9 * CIN), cotangent[0], shift, id_row
     )
     sums = tab[:, :4].reshape(16, CIN)
     frames = tab[:, 4, 0]

time: 143 us -> 111 us (0.78)
  Pallas kernels: 127 us -> 95.6 us
  other arithmetic: 4.33 us -> 2.76 us
    pallas_call x1, Pallas kernels: 127 us -> 95.6 us  [fused(): pl.pallas_call(kernel, out_shape=(jax.ShapeDtypeStruct((4, 2 * WIDTH, 256...]
where the time goes in v2:
time: 111 us; the launch traced here: 110 us
  Pallas kernels  95.6 us (86%)
  local copies, waits for them, and re-layouts  8.51 us (8%)
  other arithmetic  2.76 us (2%)
  matrix products  1.8 us (2%)
  between operations  1.31 us (1%)
    pallas_call x1, Pallas kernels, fused(): pl.pallas_call(kernel, out_shape=(jax.ShapeDtypeStruct((4, 2 * WIDTH, 256...  95.6 us
    unnamed x9, local copies, waits for them, and re-layouts  5.73 us

profile of v2, /device:TPU:1, one launch (start us, length us, event | category | flops | bytes accessed | tf_op | source)
XLA Modules:
  0.0 109.9 jit_solution(17389970305049412021)
XLA Ops:
  1.3 1.3 %dynamic-slice_convert_fusion.shift_row = f32[1,512]{1,0:T(1,128)} fusion(bf16[600,512]{1,0:T(8,128)(2,1)} %param.6, s32[]{:T(128)S(6)} %select_n.3), kind=kLoop, calls=%fused_computation.7 | loop fusion | flops 512 | bytes 3076 | tf_op jit(solution)/shard_map/convert_element_type | solution.py:671
  2.6 0.6 broadcast_in_dim.16.id_row
  3.2 95.6 %conv_block.1 = (bf16[4,768,256]{2,1,0:T(8,128)(2,1)}, bf16[6,2,2,2,16,768]{5,4,3,2,1,0:T(8,128)(2,1)}, bf16[2,384,512]{2,1,0:T(8,128)(2,1)}, f32[16,8,128]{2,1,0:T(8,128)}) custom-call(bf16[2,384,512]{2,1,0:T(8,128)(2,1)} %bitcast.26, bf16[2,2,2,16,4608]{4,3,2,1,0:T(8,128)(2,1)} %bitcast.25, bf16[4,768,256]{2,1,0:T(8,128)(2,1)} %bitcast.24, ...), custom_call_target="tpu_custom_call" | custom-call | flops 21743271936 | bytes 20000000 | tf_op jit(solution)/shard_map/conv_block/pallas_call | solution.py:605
  98.7 1.5 %bitcast_convert_fusion = f32[6,128,768]{2,1,0:T(8,128)S(1)} fusion(bf16[6,2,2,2,16,768]{5,4,3,2,1,0:T(8,128)(2,1)} %get-tuple-element.9), kind=kLoop, calls=%fused_computation | loop fusion | flops 589824 | bytes 3538944 | tf_op jit(solution)/shard_map/convert_element_type | solution.py:683
  100.2 2.0 %copy.10 = f32[6,128,768]{1,2,0:T(8,128)} copy(f32[6,128,768]{2,1,0:T(8,128)S(1)} %bitcast_convert_fusion) | data formatting | bytes 4718592 | tf_op jit(solution)/shard_map/convert_element_type | solution.py:683
  102.2 0.0 copy-start.2
  102.2 0.0 copy-start
  102.2 3.2 %copy.11 = f32[128,4608]{1,0:T(8,128)} copy(f32[128,4608]{0,1:T(8,128)} %bitcast.20) | data formatting | bytes 4718592
  105.4 0.0 copy-done.2
  105.4 0.2 slice_reduce_fusion
  105.6 1.8 %fusion = f32[600,512]{1,0:T(8,128)} fusion(f32[2,8,4,128]{3,2,1,0:T(4,128)S(1)} %bitcast.23, f32[16]{0:T(128)S(1)} %slice_reduce_fusion), kind=kOutput, calls=%fused_computation.2 | convolution fusion | flops 58992000 | bytes 1261632 | tf_op jit(solution)/shard_map/dot_general | solution.py:679
  107.4 0.0 copy-done
  107.4 0.0 copy-start.1
  107.4 1.1 %copy.20 = bf16[1,4,768,256]{3,2,1,0:T(8,128)(2,1)} copy(bf16[1,4,768,256]{3,2,1,0:T(8,128)(2,1)S(1)} %bitcast.21) | data formatting | bytes 3145728
  108.5 0.5 copy-done.1
  109.1 0.9 copy.21
  (1 shorter events, 0.0 us)
Async XLA Ops:
  102.2 3.2 %copy-start.2 = (f32[16,8,128]{2,1,0:T(8,128)S(1)}, f32[16,8,128]{2,1,0:T(8,128)}, u32[]{:S(2)}) copy-start(f32[16,8,128]{2,1,0:T(8,128)} %get-tuple-element.11) | copy-start | bytes 196612
  102.2 5.2 %copy-start = (bf16[4,768,256]{2,1,0:T(8,128)(2,1)S(1)}, bf16[4,768,256]{2,1,0:T(8,128)(2,1)}, u32[]{:S(2)}) copy-start(bf16[4,768,256]{2,1,0:T(8,128)(2,1)} %get-tuple-element.8) | copy-start | bytes 4718596
  107.4 1.7 %copy-start.1 = (bf16[2,384,512]{2,1,0:T(8,128)(2,1)S(1)}, bf16[2,384,512]{2,1,0:T(8,128)(2,1)}, u32[]{:S(2)}) copy-start(bf16[2,384,512]{2,1,0:T(8,128)(2,1)} %get-tuple-element.10) | copy-start | bytes 2359300

commit v3 on v2

--- a/solution.py
+++ b/solution.py
@@ -17,14 +17,17 @@
 
 DIMS = 6
 
-REDUCE = [tuple((i + k) % DIMS for k in range(DIMS)) for i in range(PARTS)]
+FIRST = [(0, 1), (1, 0), (2, 3), (3, 2), (4, 5), (5, 4)]
+NEAR_ORDER = (0, 2, 3, 4, 5, 1)
+FAR_ORDER = (1, 0, 2, 3, 4, 5)
+
 MESH = pl.DeviceIdType.MESH
 
 
 def kernel(
     feat, weight, cot, shift_row, id_row,
     up_out, gw_out, gf_out, tab_out,
-    xs, ss, st, wall, gwb, rcv, fin, ctv, cts, actv, upb, wide, acc, igp, igr, gfb,
+    xs, ss, st, wall, gwb, got0, got1, got2, got3, fin, ctv, cts, actv, upb, wide, acc, igp, igr, gfb,
     trow, tpeer, tall,
     loc_sem, x_send, x_recv, o_send, o_recv, n_send, n_recv, q_send, q_recv, s_send, s_recv,
     r_send, r_recv, f_send, f_recv, u_send, u_recv, i_send, i_recv, t_send, t_recv, v_send, v_recv,
@@ -149,9 +152,6 @@
         to_flip[0].start()
         across[0].start()
         to_far.start()
-        for k in range(1, 4):
-            to_turn[k].start()
-            to_flip[k].start()
 
     x_pair = remote(
         xs.at[1, pl.ds(1 + 2 * c, 2)], xs.at[1, pl.ds(1 + 2 * c, 2)], x_send.at[0], x_recv.at[0], other_core
@@ -219,20 +219,30 @@
         def _(k):
             shift_row(ref, first + k)
 
+    @pl.when(active)
+    def _():
+        to_turn[0].wait_send()
+        to_flip[0].wait_send()
+        to_turn[1].start()
+        to_flip[1].start()
+
     shift_rows(xs, 1 + 2 * c, 2)
 
     @pl.when(active)
     def _():
         from_flip[0].wait_recv()
+        across[1].start()
+        for k in range(2, 4):
+            to_turn[k].start()
+            to_flip[k].start()
 
     @pl.when(c != xa)
     def _():
         from_turn[0].wait_recv()
         across[0].start()
         from_far.wait_recv()
-
-    across[1].start()
-    pl.when(c != xa)(lambda: pass_on(2))
+        across[1].start()
+        pass_on(2)
 
     x_pair_in.wait_recv()
     shift_rows(xs, 3 - 2 * c, 2)
@@ -306,71 +316,8 @@
             out = pl.ds(pl.multiple_of(256 * v, 256), 256)
             ss[1, r + 1, rows, out] = (cts[v, r, rows].astype(jnp.float32) * slope).astype(jnp.bfloat16)
 
-    passed_in(0)
-
-    @pl.when(c != xa)
-    def _():
-        for k in range(1, 4):
-            from_turn[k].wait_recv()
-
-    @pl.loop(0, 4)
-    def _(r):
-        forward_row(near, r)
-
-    passed_in(1)
-
-    @pl.when(c != xa)
-    def _():
-        passed_in(2)
-
-    @pl.when(active)
-    def _():
-        for k in range(1, 4):
-            from_flip[k].wait_recv()
-
-    @pl.loop(0, 2)
-    def _(k):
-        forward_row(far, 3 * k)
-
-    slope_up = remote(ss.at[1, 1], ss.at[1, 5], s_send.at[0], s_recv.at[0], {"tile": 2 * jnp.maximum(z - 1, 0) + c})
-    slope_down = remote(ss.at[1, 4], ss.at[1, 0], s_send.at[1], s_recv.at[1], {"tile": 2 * jnp.minimum(z + 1, 3) + c})
-    pl.when(z > 0)(slope_up.start)
-    pl.when(z < 3)(slope_down.start)
-
-    @pl.loop(0, 2)
-    def _(k):
-        forward_row(far, 2 - k)
-
-    for r in range(4):
-        st[:, WIDTH * r : WIDTH * r + WIDTH] = ss[1, r + 1].T
-
-    sums = {}
-    for part, order in enumerate(REDUCE):
-        earlier = []
-        for k, dim in enumerate(order):
-            src = [part]
-            dst = [part, 1 if 0 in earlier else 0]
-            here = [part]
-            got = [part, 1 if 0 in earlier else 0]
-            for d in range(1, 6):
-                if d in earlier:
-                    src.append(mine[d])
-                    here.append(mine[d])
-                    dst.append(1 - mine[d])
-                    got.append(1 - mine[d])
-                elif d == dim:
-                    src.append(1 - mine[d])
-                    here.append(mine[d])
-                    dst.append(1 - mine[d])
-                    got.append(mine[d])
-                else:
-                    for at in (src, dst, here, got):
-                        at.append(slice(None))
-            copy = remote(
-                gwb.at[tuple(src)], rcv.at[tuple(dst)], r_send.at[part, k], r_recv.at[part, k], partner[dim]
-            )
-            sums[part, k] = (copy, tuple(here), tuple(got))
-            earlier.append(dim)
+    def at(part, fixed):
+        return (part,) + tuple(fixed.get(d, slice(None)) for d in range(1, 6))
 
     def when(condition, body):
         if condition is None:
@@ -378,43 +325,192 @@
         else:
             pl.when(condition)(body)
 
-    def r_sends(order, k):
-        if order[k] == 0:
-            return c != xa
-        return active if 0 in order[:k] else None
-
-    def r_recvs(order, k):
-        return active if 0 in order[: k + 1] else None
-
-    def reduce_step(part, k):
-        order = REDUCE[part]
-        if k > 0:
-            copy, here, got = sums[part, k - 1]
-
-            def add():
+    passive = c != xa
+    two_y = {"fsdp": x * 2 + 1 - h}
+    two_z = {"tile": (z + 2) % 4 * 2 + c}
+
+    halves, seconds, thirds, fourths = {}, {}, {}, {}
+    for part, (one, two) in enumerate(FIRST):
+        kept = {} if one == 0 else {one: mine[one]}
+        sends = passive if one == 0 else None
+        for n, pair in enumerate((near, far)):
+            if one == 1 and n == 0:
+                continue
+            there = {1: pair} if one < 2 else {1: pair, one: 1 - mine[one]}
+            here = {1: near} if one == 1 else ({1: pair} if one == 0 else {1: pair, one: mine[one]})
+            halves[part, n] = (
+                sends,
+                remote(
+                    gwb.at[at(part, there)], got0.at[at(part, there)],
+                    r_send.at[part, n], r_recv.at[part, n], partner[one],
+                ),
+                active if one == 0 else None,
+                at(part, here),
+            )
+        there = dict(kept) if two == 0 else {**kept, two: 1 - mine[two]}
+        kept = dict(kept) if two == 0 else {**kept, two: mine[two]}
+        seconds[part] = (
+            passive if two == 0 else (active if one == 0 else None),
+            remote(
+                gwb.at[at(part, there)], got1.at[at(part, there)],
+                r_send.at[part, 2], r_recv.at[part, 2], partner[two],
+            ),
+            active if 0 in (one, two) else None,
+            at(part, kept),
+        )
+        done_x = 0 in (one, two)
+        for step, table in ((1, thirds), (2, fourths)):
+            axis = (part // 2 + step) % 3
+            slots = got2 if step == 1 else got3
+            sem = 3 * step
+            copies = []
+            if axis == 0:
+                for j, (cond, pair, device) in enumerate(
+                    ((active, far, partner[1]), (passive, near, partner[0]), (passive, far, two_away))
+                ):
+                    copies.append((cond, {**kept, 1: pair}, device))
+                kept = {**kept, 1: near}
+                done_x = True
+                receives = active
+            else:
+                da, db = 2 * axis, 2 * axis + 1
+                cond = active if done_x else None
+                for flip_a, flip_b, device in (
+                    (1, 0, partner[da]), (0, 1, partner[db]), (1, 1, two_y if axis == 1 else two_z)
+                ):
+                    there = {
+                        **kept,
+                        da: 1 - mine[da] if flip_a else mine[da],
+                        db: 1 - mine[db] if flip_b else mine[db],
+                    }
+                    copies.append((cond, there, device))
+                kept = {**kept, da: mine[da], db: mine[db]}
+                receives = cond
+            rest = 5 - len(kept)
+            entry = []
+            for j, (cond, there, device) in enumerate(copies):
+                slot = (part, j) if step == 2 or rest == 2 else (part, j, 0)
+                entry.append(
+                    (
+                        cond,
+                        remote(
+                            gwb.at[at(part, there)], slots.at[slot],
+                            r_send.at[part, sem + j], r_recv.at[part, sem + j], device,
+                        ),
+                        slot,
+                    )
+                )
+            table[part] = (entry, receives, at(part, kept))
+
+    def add_half(part):
+        for n in range(2):
+            if (part, n) in halves:
+                _, copy, receives, here = halves[part, n]
+
+                def add(copy=copy, here=here):
+                    copy.wait_recv()
+                    total = gwb[here].astype(jnp.float32) + got0[here].astype(jnp.float32)
+                    gwb[here] = total.astype(jnp.bfloat16)
+
+                when(receives, add)
+        when(seconds[part][0], seconds[part][1].start)
+
+    def start_all(entry):
+        for cond, copy, _ in entry:
+            when(cond, copy.start)
+
+    def add_second(part):
+        _, copy, receives, here = seconds[part]
+
+        def add():
+            copy.wait_recv()
+            total = gwb[here].astype(jnp.float32) + got1[here].astype(jnp.float32)
+            gwb[here] = total.astype(jnp.bfloat16)
+
+        when(receives, add)
+        start_all(thirds[part][0])
+
+    def add_third(part):
+        entry, receives, here = thirds[part]
+
+        def add():
+            total = gwb[here].astype(jnp.float32)
+            for _, copy, slot in entry:
                 copy.wait_recv()
-                total = gwb[here].astype(jnp.float32) + rcv[got].astype(jnp.float32)
-                total = total.astype(jnp.bfloat16)
-                if k < DIMS:
-                    gwb[here] = total
-                else:
-                    fin[part, ye, za, ze] = total
-
-            when(r_recvs(order, k - 1), add)
-        if k < DIMS:
-            when(r_sends(order, k), sums[part, k][0].start)
-
-    for part in range(PARTS):
-        for j in range(3):
-            kk = 3 * part + j
-            window = xs[(kk // 2) % 3, kk // 6 : kk // 6 + 4, :, 256 * (kk % 2) : 256 * (kk % 2) + 256]
-            term = jnp.dot(
-                st[...], window.reshape(4 * WIDTH, 256), preferred_element_type=jnp.float32
-            )
-            gwb[part, :, :, :, :, :, :, 256 * j : 256 * j + 256] = term.astype(jnp.bfloat16).reshape(
-                2, 2, 2, 2, 2, 16, 256
-            )
-        reduce_step(part, 0)
+                total = total + got2[slot].astype(jnp.float32)
+            gwb[here] = total.astype(jnp.bfloat16)
+
+        when(receives, add)
+        start_all(fourths[part][0])
+
+    def add_fourth(part):
+        entry, _, here = fourths[part]
+
+        def add():
+            total = gwb[here].astype(jnp.float32)
+            for _, copy, slot in entry:
+                copy.wait_recv()
+                total = total + got3[slot].astype(jnp.float32)
+            fin[ye, za, ze, :, PCOLS * part : PCOLS * part + PCOLS] = total.astype(jnp.bfloat16)
+
+        pl.when(active)(add)
+
+    def weight_gradient(pair, order):
+        lanes = pl.ds(pl.multiple_of(256 * pair, 256), 256)
+        for r in range(4):
+            st[:, WIDTH * r : WIDTH * r + WIDTH] = ss[1, r + 1, :, lanes].T
+        for part in order:
+            for j in range(3):
+                kk = 3 * part + j
+                window = xs[(kk // 2) % 3, kk // 6 : kk // 6 + 4, :, 256 * (kk % 2) : 256 * (kk % 2) + 256]
+                term = jnp.dot(
+                    st[...], window.reshape(4 * WIDTH, 256), preferred_element_type=jnp.float32
+                )
+                gwb[part, pair, :, :, :, :, :, 256 * j : 256 * j + 256] = term.astype(jnp.bfloat16).reshape(
+                    2, 2, 2, 2, 16, 256
+                )
+            n = 0 if pair is near else 1
+            if (part, n) in halves:
+                when(halves[part, n][0], halves[part, n][1].start)
+
+    passed_in(0)
+
+    @pl.when(c != xa)
+    def _():
+        for k in range(1, 4):
+            from_turn[k].wait_recv()
+
+    @pl.loop(0, 4)
+    def _(r):
+        forward_row(near, r)
+
+    weight_gradient(near, NEAR_ORDER)
+
+    passed_in(1)
+
+    @pl.when(c != xa)
+    def _():
+        passed_in(2)
+
+    @pl.when(active)
+    def _():
+        for k in range(1, 4):
+            from_flip[k].wait_recv()
+
+    @pl.loop(0, 2)
+    def _(k):
+        forward_row(far, 3 * k)
+
+    slope_up = remote(ss.at[1, 1], ss.at[1, 5], s_send.at[0], s_recv.at[0], {"tile": 2 * jnp.maximum(z - 1, 0) + c})
+    slope_down = remote(ss.at[1, 4], ss.at[1, 0], s_send.at[1], s_recv.at[1], {"tile": 2 * jnp.minimum(z + 1, 3) + c})
+    pl.when(z > 0)(slope_up.start)
+    pl.when(z < 3)(slope_down.start)
+
+    @pl.loop(0, 2)
+    def _(k):
+        forward_row(far, 2 - k)
+
+    weight_gradient(far, FAR_ORDER)
 
     pl.when(z > 0)(lambda: remote(ss.at[1, 0], ss.at[1, 0], s_send.at[1], s_recv.at[1], other_core).wait_recv())
     pl.when(z < 3)(lambda: remote(ss.at[1, 5], ss.at[1, 5], s_send.at[0], s_recv.at[0], other_core).wait_recv())
@@ -439,8 +535,8 @@
 
     ig_pair = remote(igp, igr, i_send.at[0], i_recv.at[0], other_core)
     ig_pair.start()
-    for part in range(PARTS):
-        reduce_step(part, 1)
+    for part in FAR_ORDER:
+        add_half(part)
 
     trow[4:8, :] = id_row[4:8, :]
     trow[0:4, :] = jnp.zeros((4, 128), jnp.float32)
@@ -468,8 +564,8 @@
         copy.start()
         t_copies.append(copy)
 
-    for part in range(PARTS):
-        reduce_step(part, 2)
+    for part in FAR_ORDER:
+        add_second(part)
 
     for copy in t_copies:
         copy.wait_recv()
@@ -506,23 +602,23 @@
         up_own[-1].start()
         up_pair[-1].start()
 
-    for k in range(3, 6):
-        for part in range(PARTS):
-            reduce_step(part, k)
+    for part in FAR_ORDER:
+        add_third(part)
 
     spreads, to_pair, to_self = [], [], []
     for g in range(2):
-        parts = pl.ds(3 * g, 3)
-        at = fin.at[parts, ye, za, ze]
+        cols = pl.ds(3 * PCOLS * g, 3 * PCOLS)
+        piece_at = fin.at[ye, za, ze, :, cols]
         spreads.append(
-            [remote(at, at, f_send.at[g, k], f_recv.at[g, k], holders[k]) for k in range(7)]
-        )
-        to_pair.append(remote(fin.at[parts], gw_out.at[parts], i_send.at[1 + g], i_recv.at[1 + g], other_core))
-        to_self.append(pltpu.make_async_copy(fin.at[parts], gw_out.at[parts], loc_sem.at[12 + g]))
+            [remote(piece_at, piece_at, f_send.at[g, k], f_recv.at[g, k], holders[k]) for k in range(7)]
+        )
+        half_at, half_out = fin.at[:, :, :, :, cols], gw_out.at[:, :, :, :, cols]
+        to_pair.append(remote(half_at, half_out, i_send.at[1 + g], i_recv.at[1 + g], other_core))
+        to_self.append(pltpu.make_async_copy(half_at, half_out, loc_sem.at[12 + g]))
 
     for g in range(2):
         for part in range(3 * g, 3 * g + 3):
-            reduce_step(part, 6)
+            add_fourth(part)
 
         @pl.when(active)
         def _(g=g):
@@ -554,7 +650,7 @@
 
     @pl.when(active)
     def _():
-        for copy in to_turn + to_flip + [to_far]:
+        for copy in to_turn[1:] + to_flip[1:] + [to_far]:
             copy.wait_send()
 
     @pl.when(c != xa)
@@ -575,9 +671,11 @@
     def _():
         bottom_swap.wait_send()
 
-    for part, order in enumerate(REDUCE):
-        for k in range(DIMS):
-            when(r_sends(order, k), sums[part, k][0].wait_send)
+    for sends, copy, _, _ in list(halves.values()) + list(seconds.values()):
+        when(sends, copy.wait_send)
+    for entry, _, _ in list(thirds.values()) + list(fourths.values()):
+        for sends, copy, _ in entry:
+            when(sends, copy.wait_send)
     x_pair.wait_send()
 
     @pl.when(sends_rim)
@@ -606,7 +704,7 @@
         kernel,
         out_shape=(
             jax.ShapeDtypeStruct((4, 2 * WIDTH, 256), bf16),
-            jax.ShapeDtypeStruct((PARTS, 2, 2, 2, 16, PCOLS), bf16),
+            jax.ShapeDtypeStruct((2, 2, 2, 16, 9 * CIN), bf16),
             jax.ShapeDtypeStruct((2, WIDTH, CIN), bf16),
             jax.ShapeDtypeStruct((16, 8, 128), f32),
         ),
@@ -615,11 +713,14 @@
         scratch_shapes=[
             pltpu.VMEM((3, 6, WIDTH, CIN), bf16),
             pltpu.VMEM((3, 6, WIDTH, HALF), bf16),
-            pltpu.VMEM((HALF, 4 * WIDTH), bf16),
+            pltpu.VMEM((256, 4 * WIDTH), bf16),
             pltpu.VMEM((PARTS, 2, 2, 2, 2, 2, 16, PCOLS), bf16),
             pltpu.VMEM((PARTS, 2, 2, 2, 2, 2, 16, PCOLS), bf16),
-            pltpu.VMEM((PARTS, 2, 2, 2, 2, 2, 2, 16, PCOLS), bf16),
-            pltpu.VMEM((PARTS, 2, 2, 2, 16, PCOLS), bf16),
+            pltpu.VMEM((PARTS, 2, 2, 2, 2, 2, 16, PCOLS), bf16),
+            pltpu.VMEM((PARTS, 2, 2, 2, 2, 2, 16, PCOLS), bf16),
+            pltpu.VMEM((PARTS, 3, 2, 2, 16, PCOLS), bf16),
+            pltpu.VMEM((PARTS, 3, 16, PCOLS), bf16),
+            pltpu.VMEM((2, 2, 2, 16, 9 * CIN), bf16),
             pltpu.VMEM((4, 2 * WIDTH, 256), bf16),
             pltpu.VMEM((2, 4, WIDTH, 256), bf16),
             pltpu.VMEM((2, 4, WIDTH, 256), bf16),
@@ -643,8 +744,8 @@
             dma((3, 3)),
             dma((2,)),
             dma((2,)),
-            dma((PARTS, DIMS)),
-            dma((PARTS, DIMS)),
+            dma((PARTS, 9)),
+            dma((PARTS, 9)),
             dma((2, 7)),
             dma((2, 7)),
             dma((2,)),
@@ -680,7 +781,7 @@
         picker, sums, (((0,), (0,)), ((), ())),
         precision=lax.Precision.HIGHEST, preferred_element_type=jnp.float32,
     )
-    grad_weight = gw.reshape(PARTS, 128, PCOLS).transpose(1, 0, 2).reshape(128, 9 * CIN).astype(jnp.float32)
+    grad_weight = gw.reshape(128, 9 * CIN).astype(jnp.float32)
     return (up[None], grad_weight, gf[None], grad_table)
 
 

time: 111 us -> 105 us (0.946)
  local copies, waits for them, and re-layouts: 8.51 us -> 3.37 us
  Pallas kernels: 95.6 us -> 94 us
  other arithmetic: 2.76 us -> 4.32 us
    unnamed x9 -> x8, local copies, waits for them, and re-layouts: 5.73 us -> 2.56 us
    convert_element_type x1 -> x0, local copies, waits for them, and re-layouts: 1.98 us -> none  [shards(): gw.reshape(PARTS, 128, PCOLS).transpose(1, 0, 2).reshape(128, 9 * CIN)]
    pallas_call x1, Pallas kernels: 95.6 us -> 94 us  [fused(): pl.pallas_call(kernel, out_shape=(jax.ShapeDtypeStruct((4, 2 * WIDTH, 256...]
    convert_element_type x1, other arithmetic: 1.47 us -> 3.03 us  [shards(): grad_weight = gw.reshape(128, 9 * CIN).astype(jnp.float32)]
where the time goes in v3:
time: 105 us
  Pallas kernels  94 us (90%)
  other arithmetic  4.32 us (4%)
  local copies, waits for them, and re-layouts  3.37 us (3%)
  matrix products  1.8 us (2%)
  between operations  1.32 us (1%)
    pallas_call x1, Pallas kernels, fused(): pl.pallas_call(kernel, out_shape=(jax.ShapeDtypeStruct((4, 2 * WIDTH, 256...  94 us
    convert_element_type x1, other arithmetic, shards(): grad_weight = gw.reshape(128, 9 * CIN).astype(jnp.float32)  3.03 us
    unnamed x8, local copies, waits for them, and re-layouts  2.56 us

profile of v3, /device:TPU:1, one launch (start us, length us, event | category | flops | bytes accessed | tf_op | source)
XLA Modules:
  0.0 104.8 jit_solution(11746722924949931647)
XLA Ops:
  1.3 1.3 %dynamic-slice_convert_fusion.shift_row = f32[1,512]{1,0:T(1,128)} fusion(bf16[600,512]{1,0:T(8,128)(2,1)} %param.6, s32[]{:T(128)S(6)} %select_n.3), kind=kLoop, calls=%fused_computation.7 | loop fusion | flops 512 | bytes 3076 | tf_op jit(solution)/shard_map/convert_element_type | solution.py:772
  2.6 0.6 broadcast_in_dim.16.id_row
  3.2 94.0 %conv_block.1 = (bf16[4,768,256]{2,1,0:T(8,128)(2,1)}, bf16[2,2,2,16,4608]{4,3,2,1,0:T(8,128)(2,1)}, bf16[2,384,512]{2,1,0:T(8,128)(2,1)}, f32[16,8,128]{2,1,0:T(8,128)}) custom-call(bf16[2,384,512]{2,1,0:T(8,128)(2,1)} %bitcast.22, bf16[2,2,2,16,4608]{4,3,2,1,0:T(8,128)(2,1)} %bitcast.21, bf16[4,768,256]{2,1,0:T(8,128)(2,1)} %bitcast.20, ...), custom_call_target="tpu_custom_call" | custom-call | flops 21743271936 | bytes 20000000 | tf_op jit(solution)/shard_map/conv_block/pallas_call | solution.py:703
  97.2 0.0 copy-start.2
  97.2 0.0 copy-start
  97.2 3.0 %bitcast_convert_fusion = f32[128,4608]{1,0:T(8,128)} fusion(bf16[2,2,2,16,4608]{4,3,2,1,0:T(8,128)(2,1)} %get-tuple-element.9), kind=kLoop, calls=%fused_computation | loop fusion | flops 589824 | bytes 3538944 | tf_op jit(solution)/shard_map/convert_element_type | solution.py:784
  100.2 0.0 copy-done.2
  100.2 0.2 slice_reduce_fusion
  100.4 1.8 %fusion = f32[600,512]{1,0:T(8,128)} fusion(f32[2,8,4,128]{3,2,1,0:T(4,128)S(1)} %bitcast.19, f32[16]{0:T(128)S(1)} %slice_reduce_fusion), kind=kOutput, calls=%fused_computation.2 | convolution fusion | flops 58992000 | bytes 1261632 | tf_op jit(solution)/shard_map/dot_general | solution.py:780
  102.2 0.0 copy-done
  102.2 0.0 copy-start.1
  102.2 1.1 %copy.17 = bf16[1,4,768,256]{3,2,1,0:T(8,128)(2,1)} copy(bf16[1,4,768,256]{3,2,1,0:T(8,128)(2,1)S(1)} %bitcast.17) | data formatting | bytes 3145728
  103.4 0.5 copy-done.1
  103.9 0.9 copy.18
  (1 shorter events, 0.0 us)
Async XLA Ops:
  97.2 3.1 %copy-start.2 = (f32[16,8,128]{2,1,0:T(8,128)S(1)}, f32[16,8,128]{2,1,0:T(8,128)}, u32[]{:S(2)}) copy-start(f32[16,8,128]{2,1,0:T(8,128)} %get-tuple-element.11) | copy-start | bytes 196612
  97.2 5.1 %copy-start = (bf16[4,768,256]{2,1,0:T(8,128)(2,1)S(1)}, bf16[4,768,256]{2,1,0:T(8,128)(2,1)}, u32[]{:S(2)}) copy-start(bf16[4,768,256]{2,1,0:T(8,128)(2,1)} %get-tuple-element.8) | copy-start | bytes 4718596
  102.2 1.7 %copy-start.1 = (bf16[2,384,512]{2,1,0:T(8,128)(2,1)S(1)}, bf16[2,384,512]{2,1,0:T(8,128)(2,1)}, u32[]{:S(2)}) copy-start(bf16[2,384,512]{2,1,0:T(8,128)(2,1)} %get-tuple-element.10) | copy-start | bytes 2359300

commit v4 on v3

--- a/solution.py
+++ b/solution.py
@@ -43,7 +43,7 @@
     za = z // 2
     ze = (za + z % 2) % 2
     keep = (c + xe) % 2
-    active = c == xa
+    active, passive = c == xa, c != xa
     mine = {1: keep, 2: h, 3: ye, 4: za, 5: ze}
     x_flip = x + 1 - 2 * xb
     z_flip = z + 1 - 2 * (z % 2)
@@ -112,28 +112,30 @@
 
     pl.semaphore_wait(barrier, 25)
 
-    def piece(pair, half, number):
-        return wall.at[:, pair, half, number // 2, number % 2]
-
-    def same(pair, half, number, send_sem, recv_sem, device):
-        return remote(piece(pair, half, number), piece(pair, half, number), send_sem, recv_sem, device)
+    def same(pair, half, number, send_sem, recv_sem, device, eighth=None):
+        place = wall.at[:, pair, half, number // 2, number % 2]
+        if eighth is not None:
+            place = wall.at[:, pair, half, number // 2, number % 2, eighth]
+        return remote(place, place, send_sem, recv_sem, device)
 
     turn = [(quarter + k) % 4 for k in range(4)]
     to_flip = [same(near, h, turn[k], o_send.at[k], o_recv.at[k], partner[1]) for k in range(4)]
-    to_turn = [same(near, h, turn[k], o_send.at[4 + k], o_recv.at[4 + k], partner[0]) for k in range(4)]
+    to_turn = [same(near, h, turn[k], o_send.at[4 + k], o_recv.at[4 + k], partner[0]) for k in range(1, 4)]
     to_far = same(near, h, quarter, o_send.at[8], o_recv.at[8], two_away)
+    first_turn = [same(near, h, quarter, o_send.at[9 + e], o_recv.at[9 + e], partner[0], e) for e in range(2)]
     from_flip = [same(far, h, turn[k], o_send.at[k], o_recv.at[k], partner[1]) for k in range(4)]
-    from_turn = to_turn
     from_far = same(far, h, quarter, o_send.at[8], o_recv.at[8], two_away)
-    across = [same(pair, h, quarter, n_send.at[k], n_recv.at[k], partner[2]) for k, pair in enumerate((near, far))]
-    crossed = [same(pair, 1 - h, quarter, n_send.at[k], n_recv.at[k], partner[2]) for k, pair in enumerate((near, far))]
+    across = [same(near, h, quarter, n_send.at[e], n_recv.at[e], partner[2], e) for e in range(2)]
+    crossed = [same(near, 1 - h, quarter, n_send.at[e], n_recv.at[e], partner[2], e) for e in range(2)]
+    across_far = same(far, h, quarter, n_send.at[2], n_recv.at[2], partner[2])
+    crossed_far = same(far, 1 - h, quarter, n_send.at[2], n_recv.at[2], partner[2])
     passed = {}
     theirs = {3: (quarter + 2) % 4, 4: (3 - z + 2 * ye) % 4, 5: (z_flip + 2 * ye) % 4}
-    for k, (pair, half) in enumerate(((near, 1 - h), (far, 1 - h), (far, h))):
+    for k, (pair, half, e) in enumerate(((near, 1 - h, 0), (near, 1 - h, 1), (far, 1 - h, None), (far, h, None))):
         for j, dim in enumerate((3, 4, 5)):
             passed[k, j] = (
-                same(pair, half, quarter, q_send.at[k, j], q_recv.at[k, j], partner[dim]),
-                same(pair, half, theirs[dim], q_send.at[k, j], q_recv.at[k, j], partner[dim]),
+                same(pair, half, quarter, q_send.at[k, j], q_recv.at[k, j], partner[dim], e),
+                same(pair, half, theirs[dim], q_send.at[k, j], q_recv.at[k, j], partner[dim], e),
             )
 
     def pass_on(k):
@@ -148,10 +150,10 @@
     def _():
         for copy in own_w:
             copy.wait()
-        to_turn[0].start()
+        for e in range(2):
+            first_turn[e].start()
+            across[e].start()
         to_flip[0].start()
-        across[0].start()
-        to_far.start()
 
     x_pair = remote(
         xs.at[1, pl.ds(1 + 2 * c, 2)], xs.at[1, pl.ds(1 + 2 * c, 2)], x_send.at[0], x_recv.at[0], other_core
@@ -221,28 +223,28 @@
 
     @pl.when(active)
     def _():
-        to_turn[0].wait_send()
-        to_flip[0].wait_send()
-        to_turn[1].start()
+        for e in range(2):
+            first_turn[e].wait_send()
+        to_turn[0].start()
         to_flip[1].start()
 
     shift_rows(xs, 1 + 2 * c, 2)
 
     @pl.when(active)
     def _():
-        from_flip[0].wait_recv()
-        across[1].start()
-        for k in range(2, 4):
+        for e in range(2):
+            crossed[e].wait_recv()
+            pass_on(e)
+        to_far.start()
+        for k in range(1, 3):
             to_turn[k].start()
-            to_flip[k].start()
-
-    @pl.when(c != xa)
-    def _():
-        from_turn[0].wait_recv()
-        across[0].start()
-        from_far.wait_recv()
-        across[1].start()
-        pass_on(2)
+            to_flip[k + 1].start()
+
+    @pl.when(passive)
+    def _():
+        for e in range(2):
+            first_turn[e].wait_recv()
+            across[e].start()
 
     x_pair_in.wait_recv()
     shift_rows(xs, 3 - 2 * c, 2)
@@ -257,8 +259,11 @@
         bottom_in.wait_recv()
         bottom_swap.start()
 
-    crossed[0].wait_recv()
-    pass_on(0)
+    @pl.when(passive)
+    def _():
+        for e in range(2):
+            crossed[e].wait_recv()
+            pass_on(e)
 
     for copy in own_ct:
         copy.wait()
@@ -273,9 +278,6 @@
             for lane in range(2):
                 cts[v, r, :, 128 * lane : 128 * lane + 128] = wide[lane, pl.ds(v, WIDTH, 2), :].astype(jnp.bfloat16)
 
-    crossed[1].wait_recv()
-    pass_on(1)
-
     @pl.when(z > 0)
     def _():
         top_swapped.wait_recv()
@@ -286,6 +288,17 @@
 
     shift_rows(xs, 0, 1)
     shift_rows(xs, 5, 1)
+
+    @pl.when(active)
+    def _():
+        from_flip[0].wait_recv()
+        across_far.start()
+
+    @pl.when(passive)
+    def _():
+        from_far.wait_recv()
+        across_far.start()
+        pass_on(3)
 
     def forward_row(v, r):
         lhs = jnp.concatenate(
@@ -325,102 +338,129 @@
         else:
             pl.when(condition)(body)
 
-    passive = c != xa
     two_y = {"fsdp": x * 2 + 1 - h}
     two_z = {"tile": (z + 2) % 4 * 2 + c}
 
     halves, seconds, thirds, fourths = {}, {}, {}, {}
-    for part, (one, two) in enumerate(FIRST):
-        kept = {} if one == 0 else {one: mine[one]}
-        sends = passive if one == 0 else None
-        for n, pair in enumerate((near, far)):
-            if one == 1 and n == 0:
-                continue
-            there = {1: pair} if one < 2 else {1: pair, one: 1 - mine[one]}
-            here = {1: near} if one == 1 else ({1: pair} if one == 0 else {1: pair, one: mine[one]})
-            halves[part, n] = (
+
+    def half_copies(part, n, dim, there, sends):
+        place = at(part, there)
+        return [
+            (
                 sends,
                 remote(
-                    gwb.at[at(part, there)], got0.at[at(part, there)],
-                    r_send.at[part, n], r_recv.at[part, n], partner[one],
+                    gwb.at[place + (slice(None), pl.ds(256 * j, 256))],
+                    got0.at[place + (slice(None), pl.ds(256 * j, 256))],
+                    r_send.at[part, 3 * n + j], r_recv.at[part, 3 * n + j], partner[dim],
                 ),
-                active if one == 0 else None,
-                at(part, here),
             )
-        there = dict(kept) if two == 0 else {**kept, two: 1 - mine[two]}
-        kept = dict(kept) if two == 0 else {**kept, two: mine[two]}
-        seconds[part] = (
-            passive if two == 0 else (active if one == 0 else None),
+            for j in range(3)
+        ]
+
+    def second_copy(part, n, dim, there, sends):
+        place = at(part, there)
+        return (
+            sends,
             remote(
-                gwb.at[at(part, there)], got1.at[at(part, there)],
-                r_send.at[part, 2], r_recv.at[part, 2], partner[two],
+                gwb.at[place], got1.at[place], r_send.at[part, 6 + n], r_recv.at[part, 6 + n], partner[dim]
             ),
-            active if 0 in (one, two) else None,
-            at(part, kept),
-        )
-        done_x = 0 in (one, two)
-        for step, table in ((1, thirds), (2, fourths)):
-            axis = (part // 2 + step) % 3
-            slots = got2 if step == 1 else got3
-            sem = 3 * step
-            copies = []
-            if axis == 0:
-                for j, (cond, pair, device) in enumerate(
-                    ((active, far, partner[1]), (passive, near, partner[0]), (passive, far, two_away))
-                ):
-                    copies.append((cond, {**kept, 1: pair}, device))
-                kept = {**kept, 1: near}
-                done_x = True
-                receives = active
-            else:
-                da, db = 2 * axis, 2 * axis + 1
-                cond = active if done_x else None
-                for flip_a, flip_b, device in (
-                    (1, 0, partner[da]), (0, 1, partner[db]), (1, 1, two_y if axis == 1 else two_z)
-                ):
-                    there = {
-                        **kept,
-                        da: 1 - mine[da] if flip_a else mine[da],
-                        db: 1 - mine[db] if flip_b else mine[db],
-                    }
-                    copies.append((cond, there, device))
-                kept = {**kept, da: mine[da], db: mine[db]}
-                receives = cond
-            rest = 5 - len(kept)
-            entry = []
-            for j, (cond, there, device) in enumerate(copies):
-                slot = (part, j) if step == 2 or rest == 2 else (part, j, 0)
-                entry.append(
-                    (
-                        cond,
-                        remote(
-                            gwb.at[at(part, there)], slots.at[slot],
-                            r_send.at[part, sem + j], r_recv.at[part, sem + j], device,
-                        ),
-                        slot,
-                    )
+        )
+
+    def slot_copy(part, there, slots, slot, sem, device, sends):
+        return (
+            sends,
+            remote(
+                gwb.at[at(part, there)], slots.at[slot], r_send.at[part, sem], r_recv.at[part, sem], device
+            ),
+            slot,
+        )
+
+    def flips(axis):
+        da, db = 2 * axis, 2 * axis + 1
+        there = {da: 1 - mine[da], db: 1 - mine[db]}
+        return (
+            ({da: there[da], db: mine[db]}, partner[da]),
+            ({da: mine[da], db: there[db]}, partner[db]),
+            (there, two_y if axis == 1 else two_z),
+        )
+
+    def along_x(part, kept, slots, sem):
+        return [
+            slot_copy(part, {**kept, 1: pair}, slots, (part, j), sem + j, device, sends)
+            for j, (sends, pair, device) in enumerate(
+                ((passive, near, partner[0]), (active, far, partner[1]), (passive, far, two_away))
+            )
+        ]
+
+    for n, pair in enumerate((near, far)):
+        halves[0, n] = (half_copies(0, n, 0, {1: pair}, passive), active, at(0, {1: pair}))
+    halves[1, 1] = (half_copies(1, 1, 1, {1: far}, None), None, at(1, {1: near}))
+    seconds[0, 1] = (second_copy(0, 1, 1, {1: far}, active), active, at(0, {1: near}))
+    seconds[1, 1] = (second_copy(1, 1, 0, {1: near}, passive), active, at(1, {1: near}))
+    for part in (0, 1):
+        thirds[part, 1] = (
+            [
+                slot_copy(part, {1: near, **there}, got2, (part, j), 11 + j, device, active)
+                for j, (there, device) in enumerate(flips(1))
+            ],
+            active, at(part, {1: near, 2: h, 3: ye}),
+        )
+        fourths[part] = [
+            slot_copy(part, {1: near, 2: h, 3: ye, **there}, got3, (part, j), 14 + j, device, active)
+            for j, (there, device) in enumerate(flips(2))
+        ]
+    for part in range(2, 6):
+        one, two = FIRST[part]
+        first = {one: mine[one]}
+        both = {**first, two: mine[two]}
+        for n, pair in enumerate((near, far)):
+            halves[part, n] = (
+                half_copies(part, n, one, {1: pair, one: 1 - mine[one]}, None),
+                None, at(part, {1: pair, **first}),
+            )
+            seconds[part, n] = (
+                second_copy(part, n, two, {1: pair, **first, two: 1 - mine[two]}, None),
+                None, at(part, {1: pair, **both}),
+            )
+            if part < 4:
+                thirds[part, n] = (
+                    [
+                        slot_copy(
+                            part, {1: pair, **both, **there}, got2, (part, j, 0, pair), 8 + 3 * n + j, device, None
+                        )
+                        for j, (there, device) in enumerate(flips(2))
+                    ],
+                    None, at(part, {1: pair, **both, 4: za, 5: ze}),
                 )
-            table[part] = (entry, receives, at(part, kept))
-
-    def add_half(part):
-        for n in range(2):
-            if (part, n) in halves:
-                _, copy, receives, here = halves[part, n]
-
-                def add(copy=copy, here=here):
+        if part < 4:
+            fourths[part] = along_x(part, {**both, 4: za, 5: ze}, got3, 14)
+        else:
+            copies = along_x(part, both, got2, 8)
+            thirds[part, 0] = ([copies[0]], None, None)
+            thirds[part, 1] = (copies, active, at(part, {**both, 1: near}))
+            fourths[part] = [
+                slot_copy(part, {1: near, **both, **there}, got3, (part, j), 14 + j, device, active)
+                for j, (there, device) in enumerate(flips(1))
+            ]
+
+    def add_half(part, n):
+        if (part, n) in halves:
+            copies, receives, here = halves[part, n]
+
+            def add():
+                for _, copy in copies:
                     copy.wait_recv()
-                    total = gwb[here].astype(jnp.float32) + got0[here].astype(jnp.float32)
-                    gwb[here] = total.astype(jnp.bfloat16)
-
-                when(receives, add)
-        when(seconds[part][0], seconds[part][1].start)
-
-    def start_all(entry):
-        for cond, copy, _ in entry:
-            when(cond, copy.start)
-
-    def add_second(part):
-        _, copy, receives, here = seconds[part]
+                total = gwb[here].astype(jnp.float32) + got0[here].astype(jnp.float32)
+                gwb[here] = total.astype(jnp.bfloat16)
+
+            when(receives, add)
+        if (part, n) in seconds:
+            when(seconds[part, n][0][0], seconds[part, n][0][1].start)
+
+    def add_second(part, n):
+        if (part, n) not in seconds:
+            return
+        (_, copy), receives, here = seconds[part, n]
 
         def add():
             copy.wait_recv()
@@ -428,40 +468,49 @@
             gwb[here] = total.astype(jnp.bfloat16)
 
         when(receives, add)
-        start_all(thirds[part][0])
+        entry = thirds[part, n][0]
+        for sends, copy, _ in entry[1:] if part >= 4 and n == 1 else entry:
+            when(sends, copy.start)
 
     def add_third(part):
-        entry, receives, here = thirds[part]
+        for n in range(2):
+            if (part, n) in thirds and thirds[part, n][2] is not None:
+                entry, receives, here = thirds[part, n]
+
+                def add(entry=entry, here=here):
+                    total = gwb[here].astype(jnp.float32)
+                    for _, copy, slot in entry:
+                        copy.wait_recv()
+                        total = total + got2[slot].astype(jnp.float32)
+                    gwb[here] = total.astype(jnp.bfloat16)
+
+                when(receives, add)
+        for sends, copy, _ in fourths[part]:
+            when(sends, copy.start)
+
+    def add_fourth(part):
+        here = at(part, {1: near, 2: h, 3: ye, 4: za, 5: ze})
 
         def add():
             total = gwb[here].astype(jnp.float32)
-            for _, copy, slot in entry:
-                copy.wait_recv()
-                total = total + got2[slot].astype(jnp.float32)
-            gwb[here] = total.astype(jnp.bfloat16)
-
-        when(receives, add)
-        start_all(fourths[part][0])
-
-    def add_fourth(part):
-        entry, _, here = fourths[part]
-
-        def add():
-            total = gwb[here].astype(jnp.float32)
-            for _, copy, slot in entry:
+            for _, copy, slot in fourths[part]:
                 copy.wait_recv()
                 total = total + got3[slot].astype(jnp.float32)
-            fin[ye, za, ze, :, PCOLS * part : PCOLS * part + PCOLS] = total.astype(jnp.bfloat16)
+            total = total.astype(jnp.bfloat16)
+            for j in range(3):
+                lane = 3 * PCOLS * (part // 3) + PCOLS * j + 256 * (part % 3)
+                fin[ye, za, ze, :, lane : lane + 256] = total[:, 256 * j : 256 * j + 256]
 
         pl.when(active)(add)
 
     def weight_gradient(pair, order):
+        n = 0 if pair is near else 1
         lanes = pl.ds(pl.multiple_of(256 * pair, 256), 256)
         for r in range(4):
             st[:, WIDTH * r : WIDTH * r + WIDTH] = ss[1, r + 1, :, lanes].T
-        for part in order:
-            for j in range(3):
-                kk = 3 * part + j
+        for j in range(3):
+            for part in order:
+                kk = part + PARTS * j
                 window = xs[(kk // 2) % 3, kk // 6 : kk // 6 + 4, :, 256 * (kk % 2) : 256 * (kk % 2) + 256]
                 term = jnp.dot(
                     st[...], window.reshape(4 * WIDTH, 256), preferred_element_type=jnp.float32
@@ -469,28 +518,32 @@
                 gwb[part, pair, :, :, :, :, :, 256 * j : 256 * j + 256] = term.astype(jnp.bfloat16).reshape(
                     2, 2, 2, 2, 16, 256
                 )
-            n = 0 if pair is near else 1
-            if (part, n) in halves:
-                when(halves[part, n][0], halves[part, n][1].start)
+                if (part, n) in halves:
+                    sends, copy = halves[part, n][0][j]
+                    when(sends, copy.start)
 
     passed_in(0)
-
-    @pl.when(c != xa)
-    def _():
-        for k in range(1, 4):
-            from_turn[k].wait_recv()
-
-    @pl.loop(0, 4)
+    passed_in(1)
+
+    @pl.when(passive)
+    def _():
+        for copy in to_turn:
+            copy.wait_recv()
+
+    @pl.loop(0, 3)
     def _(r):
         forward_row(near, r)
 
+    crossed_far.wait_recv()
+    pass_on(2)
+    forward_row(near, 3)
     weight_gradient(near, NEAR_ORDER)
 
-    passed_in(1)
-
-    @pl.when(c != xa)
-    def _():
-        passed_in(2)
+    passed_in(2)
+
+    @pl.when(passive)
+    def _():
+        passed_in(3)
 
     @pl.when(active)
     def _():
@@ -510,7 +563,11 @@
     def _(k):
         forward_row(far, 2 - k)
 
+    for part in (0, 2, 3, 4, 5):
+        add_half(part, 0)
     weight_gradient(far, FAR_ORDER)
+    for part in range(2, 6):
+        add_second(part, 0)
 
     pl.when(z > 0)(lambda: remote(ss.at[1, 0], ss.at[1, 0], s_send.at[1], s_recv.at[1], other_core).wait_recv())
     pl.when(z < 3)(lambda: remote(ss.at[1, 5], ss.at[1, 5], s_send.at[0], s_recv.at[0], other_core).wait_recv())
@@ -536,7 +593,7 @@
     ig_pair = remote(igp, igr, i_send.at[0], i_recv.at[0], other_core)
     ig_pair.start()
     for part in FAR_ORDER:
-        add_half(part)
+        add_half(part, 1)
 
     trow[4:8, :] = id_row[4:8, :]
     trow[0:4, :] = jnp.zeros((4, 128), jnp.float32)
@@ -565,7 +622,27 @@
         t_copies.append(copy)
 
     for part in FAR_ORDER:
-        add_second(part)
+        add_second(part, 1)
+
+    @pl.loop(0, 4)
+    def _(r):
+        for lane in range(2):
+            lanes = pl.ds(128 * lane, 128)
+            for v in range(2):
+                wide[lane, pl.ds(v, WIDTH, 2), :] = actv[v, r, :, lanes].astype(jnp.float32)
+            upb[r, :, lanes] = wide[lane].astype(jnp.bfloat16)
+
+    up_own, up_pair = [], []
+    for k in range(2):
+        up_own.append(pltpu.make_async_copy(upb.at[2 * c + k], up_out.at[2 * k + c], loc_sem.at[9 + k]))
+        up_pair.append(
+            remote(upb.at[2 * (1 - c) + k], up_out.at[2 * k + c], u_send.at[k], u_recv.at[k], other_core)
+        )
+        up_own[-1].start()
+        up_pair[-1].start()
+
+    for part in FAR_ORDER:
+        add_third(part)
 
     for copy in t_copies:
         copy.wait_recv()
@@ -585,26 +662,6 @@
         copy.start()
         v_copies.append(copy)
 
-    @pl.loop(0, 4)
-    def _(r):
-        for lane in range(2):
-            lanes = pl.ds(128 * lane, 128)
-            for v in range(2):
-                wide[lane, pl.ds(v, WIDTH, 2), :] = actv[v, r, :, lanes].astype(jnp.float32)
-            upb[r, :, lanes] = wide[lane].astype(jnp.bfloat16)
-
-    up_own, up_pair = [], []
-    for k in range(2):
-        up_own.append(pltpu.make_async_copy(upb.at[2 * c + k], up_out.at[2 * k + c], loc_sem.at[9 + k]))
-        up_pair.append(
-            remote(upb.at[2 * (1 - c) + k], up_out.at[2 * k + c], u_send.at[k], u_recv.at[k], other_core)
-        )
-        up_own[-1].start()
-        up_pair[-1].start()
-
-    for part in FAR_ORDER:
-        add_third(part)
-
     spreads, to_pair, to_self = [], [], []
     for g in range(2):
         cols = pl.ds(3 * PCOLS * g, 3 * PCOLS)
@@ -612,9 +669,12 @@
         spreads.append(
             [remote(piece_at, piece_at, f_send.at[g, k], f_recv.at[g, k], holders[k]) for k in range(7)]
         )
-        half_at, half_out = fin.at[:, :, :, :, cols], gw_out.at[:, :, :, :, cols]
-        to_pair.append(remote(half_at, half_out, i_send.at[1 + g], i_recv.at[1 + g], other_core))
-        to_self.append(pltpu.make_async_copy(half_at, half_out, loc_sem.at[12 + g]))
+        for j in range(3):
+            held = fin.at[:, :, :, :, pl.ds(3 * PCOLS * g + PCOLS * j, PCOLS)]
+            out = gw_out.at[:, :, :, :, pl.ds(2 * PCOLS * j + PCOLS * g, PCOLS)]
+            n = 3 * g + j
+            to_pair.append(remote(held, out, i_send.at[1 + n], i_recv.at[1 + n], other_core))
+            to_self.append(pltpu.make_async_copy(held, out, loc_sem.at[12 + n]))
 
     for g in range(2):
         for part in range(3 * g, 3 * g + 3):
@@ -630,36 +690,39 @@
         for g in range(2):
             for copy in spreads[g]:
                 copy.wait_recv()
-            to_pair[g].start()
-            to_self[g].start()
+            for j in range(3):
+                to_pair[3 * g + j].start()
+                to_self[3 * g + j].start()
         for g in range(2):
             for copy in spreads[g]:
                 copy.wait_send()
-            to_self[g].wait()
-            to_pair[g].wait_send()
+        for j in range(6):
+            to_self[j].wait()
+            to_pair[j].wait_send()
 
     @pl.when(c != xa)
     def _():
-        for g in range(2):
-            to_pair[g].wait_recv()
+        for j in range(6):
+            to_pair[j].wait_recv()
 
     for copy in v_copies:
         copy.wait()
-    tab_copy = pltpu.make_async_copy(tall, tab_out, loc_sem.at[15])
+    tab_copy = pltpu.make_async_copy(tall, tab_out, loc_sem.at[18])
     tab_copy.start()
 
     @pl.when(active)
     def _():
-        for copy in to_turn[1:] + to_flip[1:] + [to_far]:
+        for copy in to_turn + to_flip + [to_far]:
             copy.wait_send()
 
-    @pl.when(c != xa)
+    @pl.when(passive)
     def _():
         for j in range(3):
-            passed[2, j][0].wait_send()
-
-    for k in range(2):
-        across[k].wait_send()
+            passed[3, j][0].wait_send()
+
+    for copy in across + [across_far]:
+        copy.wait_send()
+    for k in range(3):
         for j in range(3):
             passed[k, j][0].wait_send()
 
@@ -671,9 +734,15 @@
     def _():
         bottom_swap.wait_send()
 
-    for sends, copy, _, _ in list(halves.values()) + list(seconds.values()):
+    for copies, _, _ in halves.values():
+        for sends, copy in copies:
+            when(sends, copy.wait_send)
+    for (sends, copy), _, _ in seconds.values():
         when(sends, copy.wait_send)
-    for entry, _, _ in list(thirds.values()) + list(fourths.values()):
+    for (part, n), (entry, _, _) in thirds.items():
+        for sends, copy, _ in entry[1:] if part >= 4 and n == 1 else entry:
+            when(sends, copy.wait_send)
+    for entry in fourths.values():
         for sends, copy, _ in entry:
             when(sends, copy.wait_send)
     x_pair.wait_send()
@@ -733,25 +802,25 @@
             pltpu.VMEM((8, 128), f32),
             pltpu.VMEM((7, 8, 128), f32),
             pltpu.VMEM((16, 8, 128), f32),
-            dma((16,)),
+            dma((19,)),
             dma((7,)),
             dma((7,)),
-            dma((9,)),
-            dma((9,)),
+            dma((11,)),
+            dma((11,)),
+            dma((3,)),
+            dma((3,)),
+            dma((4, 3)),
+            dma((4, 3)),
             dma((2,)),
             dma((2,)),
-            dma((3, 3)),
-            dma((3, 3)),
-            dma((2,)),
-            dma((2,)),
-            dma((PARTS, 9)),
-            dma((PARTS, 9)),
+            dma((PARTS, 17)),
+            dma((PARTS, 17)),
             dma((2, 7)),
             dma((2, 7)),
             dma((2,)),
             dma((2,)),
-            dma((3,)),
-            dma((3,)),
+            dma((7,)),
+            dma((7,)),
             dma((7,)),
             dma((7,)),
             dma((15,)),

time: 105 us -> 112 us (1.067)
  Pallas kernels: 94 us -> 101 us
    pallas_call x1, Pallas kernels: 94 us -> 101 us  [fused(): pl.pallas_call(kernel, out_shape=(jax.ShapeDtypeStruct((4, 2 * WIDTH, 256...]
where the time goes in v4:
time: 112 us
  Pallas kernels  101 us (90%)
  other arithmetic  4.32 us (4%)
  local copies, waits for them, and re-layouts  3.37 us (3%)
  matrix products  1.8 us (2%)
  between operations  1.32 us (1%)
    pallas_call x1, Pallas kernels, fused(): pl.pallas_call(kernel, out_shape=(jax.ShapeDtypeStruct((4, 2 * WIDTH, 256...  101 us
    convert_element_type x1, other arithmetic, shards(): grad_weight = gw.reshape(128, 9 * CIN).astype(jnp.float32)  3.03 us
    unnamed x8, local copies, waits for them, and re-layouts  2.56 us

profile of v4, /device:TPU:1, one launch (start us, length us, event | category | flops | bytes accessed | tf_op | source)
XLA Modules:
  0.0 111.9 jit_solution(5355930314190682726)
XLA Ops:
  1.3 1.3 %dynamic-slice_convert_fusion.shift_row = f32[1,512]{1,0:T(1,128)} fusion(bf16[600,512]{1,0:T(8,128)(2,1)} %param.6, s32[]{:T(128)S(6)} %select_n.3), kind=kLoop, calls=%fused_computation.7 | loop fusion | flops 512 | bytes 3076 | tf_op jit(solution)/shard_map/convert_element_type | solution.py:841
  2.6 0.6 broadcast_in_dim.16.id_row
  3.2 101.1 %conv_block.1 = (bf16[4,768,256]{2,1,0:T(8,128)(2,1)}, bf16[2,2,2,16,4608]{4,3,2,1,0:T(8,128)(2,1)}, bf16[2,384,512]{2,1,0:T(8,128)(2,1)}, f32[16,8,128]{2,1,0:T(8,128)}) custom-call(bf16[2,384,512]{2,1,0:T(8,128)(2,1)} %bitcast.22, bf16[2,2,2,16,4608]{4,3,2,1,0:T(8,128)(2,1)} %bitcast.21, bf16[4,768,256]{2,1,0:T(8,128)(2,1)} %bitcast.20, ...), custom_call_target="tpu_custom_call" | custom-call | flops 21743271936 | bytes 20000000 | tf_op jit(solution)/shard_map/conv_block/pallas_call | solution.py:772
  104.3 0.0 copy-start.2
  104.3 0.0 copy-start
  104.3 3.0 %bitcast_convert_fusion = f32[128,4608]{1,0:T(8,128)} fusion(bf16[2,2,2,16,4608]{4,3,2,1,0:T(8,128)(2,1)} %get-tuple-element.9), kind=kLoop, calls=%fused_computation | loop fusion | flops 589824 | bytes 3538944 | tf_op jit(solution)/shard_map/convert_element_type | solution.py:853
  107.4 0.0 copy-done.2
  107.4 0.2 slice_reduce_fusion
  107.6 1.8 %fusion = f32[600,512]{1,0:T(8,128)} fusion(f32[2,8,4,128]{3,2,1,0:T(4,128)S(1)} %bitcast.19, f32[16]{0:T(128)S(1)} %slice_reduce_fusion), kind=kOutput, calls=%fused_computation.2 | convolution fusion | flops 58992000 | bytes 1261632 | tf_op jit(solution)/shard_map/dot_general | solution.py:849
  109.4 0.0 copy-done
  109.4 0.0 copy-start.1
  109.4 1.1 %copy.17 = bf16[1,4,768,256]{3,2,1,0:T(8,128)(2,1)} copy(bf16[1,4,768,256]{3,2,1,0:T(8,128)(2,1)S(1)} %bitcast.17) | data formatting | bytes 3145728
  110.5 0.5 copy-done.1
  111.1 0.9 copy.18
  (1 shorter events, 0.0 us)
Async XLA Ops:
  104.3 3.1 %copy-start.2 = (f32[16,8,128]{2,1,0:T(8,128)S(1)}, f32[16,8,128]{2,1,0:T(8,128)}, u32[]{:S(2)}) copy-start(f32[16,8,128]{2,1,0:T(8,128)} %get-tuple-element.11) | copy-start | bytes 196612
  104.3 5.1 %copy-start = (bf16[4,768,256]{2,1,0:T(8,128)(2,1)S(1)}, bf16[4,768,256]{2,1,0:T(8,128)(2,1)}, u32[]{:S(2)}) copy-start(bf16[4,768,256]{2,1,0:T(8,128)(2,1)} %get-tuple-element.8) | copy-start | bytes 4718596
  109.4 1.7 %copy-start.1 = (bf16[2,384,512]{2,1,0:T(8,128)(2,1)S(1)}, bf16[2,384,512]{2,1,0:T(8,128)(2,1)}, u32[]{:S(2)}) copy-start(bf16[2,384,512]{2,1,0:T(8,128)(2,1)} %get-tuple-element.10) | copy-start | bytes 2359300

commit v5 on v4

--- a/solution.py
+++ b/solution.py
@@ -18,8 +18,9 @@
 DIMS = 6
 
 FIRST = [(0, 1), (1, 0), (2, 3), (3, 2), (4, 5), (5, 4)]
-NEAR_ORDER = (0, 2, 3, 4, 5, 1)
-FAR_ORDER = (1, 0, 2, 3, 4, 5)
+NEAR_RUNS = ((0, 1, 2, 3, 4, 5),)
+FAR_RUNS = ((1, 0), (2, 3), (4, 5))
+ORDER = (0, 2, 3, 4, 5, 1)
 
 MESH = pl.DeviceIdType.MESH
 
@@ -27,7 +28,7 @@
 def kernel(
     feat, weight, cot, shift_row, id_row,
     up_out, gw_out, gf_out, tab_out,
-    xs, ss, st, wall, gwb, got0, got1, got2, got3, fin, ctv, cts, actv, upb, wide, acc, igp, igr, gfb,
+    xs, ss, st, wall, gwb, got0, got1, got2, got3, fin, ctv, cts, actv, upb, wide, acc, igp, igo, igr, gfb,
     trow, tpeer, tall,
     loc_sem, x_send, x_recv, o_send, o_recv, n_send, n_recv, q_send, q_recv, s_send, s_recv,
     r_send, r_recv, f_send, f_recv, u_send, u_recv, i_send, i_recv, t_send, t_recv, v_send, v_recv,
@@ -120,11 +121,11 @@
 
     turn = [(quarter + k) % 4 for k in range(4)]
     to_flip = [same(near, h, turn[k], o_send.at[k], o_recv.at[k], partner[1]) for k in range(4)]
-    to_turn = [same(near, h, turn[k], o_send.at[4 + k], o_recv.at[4 + k], partner[0]) for k in range(1, 4)]
-    to_far = same(near, h, quarter, o_send.at[8], o_recv.at[8], two_away)
+    to_turn = [same(near, h, turn[k], o_send.at[3 + k], o_recv.at[3 + k], partner[0]) for k in range(1, 4)]
     first_turn = [same(near, h, quarter, o_send.at[9 + e], o_recv.at[9 + e], partner[0], e) for e in range(2)]
+    relay = [same(near, h, quarter, o_send.at[7 + e], o_recv.at[7 + e], partner[1], e) for e in range(2)]
     from_flip = [same(far, h, turn[k], o_send.at[k], o_recv.at[k], partner[1]) for k in range(4)]
-    from_far = same(far, h, quarter, o_send.at[8], o_recv.at[8], two_away)
+    from_far = [same(far, h, quarter, o_send.at[7 + e], o_recv.at[7 + e], partner[1], e) for e in range(2)]
     across = [same(near, h, quarter, n_send.at[e], n_recv.at[e], partner[2], e) for e in range(2)]
     crossed = [same(near, 1 - h, quarter, n_send.at[e], n_recv.at[e], partner[2], e) for e in range(2)]
     across_far = same(far, h, quarter, n_send.at[2], n_recv.at[2], partner[2])
@@ -226,7 +227,6 @@
         for e in range(2):
             first_turn[e].wait_send()
         to_turn[0].start()
-        to_flip[1].start()
 
     shift_rows(xs, 1 + 2 * c, 2)
 
@@ -235,16 +235,16 @@
         for e in range(2):
             crossed[e].wait_recv()
             pass_on(e)
-        to_far.start()
         for k in range(1, 3):
             to_turn[k].start()
-            to_flip[k + 1].start()
+        to_flip[1].start()
 
     @pl.when(passive)
     def _():
         for e in range(2):
             first_turn[e].wait_recv()
             across[e].start()
+            relay[e].start()
 
     x_pair_in.wait_recv()
     shift_rows(xs, 3 - 2 * c, 2)
@@ -293,10 +293,13 @@
     def _():
         from_flip[0].wait_recv()
         across_far.start()
+        for k in range(2, 4):
+            to_flip[k].start()
 
     @pl.when(passive)
     def _():
-        from_far.wait_recv()
+        for copy in from_far:
+            copy.wait_recv()
         across_far.start()
         pass_on(3)
 
@@ -315,14 +318,14 @@
             ],
             axis=1,
         )
-        acc[:, :256] = lax.dot_general(
+        acc[...] = lax.dot_general(
             lhs, rhs, (((1,), (1,)), ((), ())), preferred_element_type=jnp.float32
         )
 
         @pl.loop(0, WIDTH // 32)
         def _(j):
             rows = pl.ds(pl.multiple_of(j * 32, 32), 32)
-            value = acc[rows, :256]
+            value = acc[rows]
             grown = 0.5 * (1.0 + lax.erf(value * inv_root_two))
             slope = grown + value * jnp.exp(-0.5 * value * value) * inv_root_tau
             actv[v, r, rows] = (value * grown).astype(jnp.bfloat16)
@@ -343,26 +346,19 @@
 
     halves, seconds, thirds, fourths = {}, {}, {}, {}
 
-    def half_copies(part, n, dim, there, sends):
+    def half_copy(part, n, dim, there, sends):
         place = at(part, there)
-        return [
-            (
-                sends,
-                remote(
-                    gwb.at[place + (slice(None), pl.ds(256 * j, 256))],
-                    got0.at[place + (slice(None), pl.ds(256 * j, 256))],
-                    r_send.at[part, 3 * n + j], r_recv.at[part, 3 * n + j], partner[dim],
-                ),
-            )
-            for j in range(3)
-        ]
+        return (
+            sends,
+            remote(gwb.at[place], got0.at[place], r_send.at[part, n], r_recv.at[part, n], partner[dim]),
+        )
 
     def second_copy(part, n, dim, there, sends):
         place = at(part, there)
         return (
             sends,
             remote(
-                gwb.at[place], got1.at[place], r_send.at[part, 6 + n], r_recv.at[part, 6 + n], partner[dim]
+                gwb.at[place], got1.at[place], r_send.at[part, 2 + n], r_recv.at[part, 2 + n], partner[dim]
             ),
         )
 
@@ -393,20 +389,33 @@
         ]
 
     for n, pair in enumerate((near, far)):
-        halves[0, n] = (half_copies(0, n, 0, {1: pair}, passive), active, at(0, {1: pair}))
-    halves[1, 1] = (half_copies(1, 1, 1, {1: far}, None), None, at(1, {1: near}))
+        halves[0, n] = (half_copy(0, n, 0, {1: pair}, passive), active, at(0, {1: pair}))
     seconds[0, 1] = (second_copy(0, 1, 1, {1: far}, active), active, at(0, {1: near}))
-    seconds[1, 1] = (second_copy(1, 1, 0, {1: near}, passive), active, at(1, {1: near}))
+    across_x = [
+        (
+            sends,
+            remote(
+                gwb.at[at(1, {1: pair})], slots.at[at(1, {1: place})], r_send.at[1, j], r_recv.at[1, j], device
+            ),
+        )
+        for j, (sends, pair, device, slots, place) in enumerate(
+            (
+                (passive, near, partner[0], got0, near),
+                (active, far, partner[1], got1, far),
+                (passive, far, two_away, got0, near),
+            )
+        )
+    ]
     for part in (0, 1):
         thirds[part, 1] = (
             [
-                slot_copy(part, {1: near, **there}, got2, (part, j), 11 + j, device, active)
+                slot_copy(part, {1: near, **there}, got2, (part, j), 7 + j, device, active)
                 for j, (there, device) in enumerate(flips(1))
             ],
             active, at(part, {1: near, 2: h, 3: ye}),
         )
         fourths[part] = [
-            slot_copy(part, {1: near, 2: h, 3: ye, **there}, got3, (part, j), 14 + j, device, active)
+            slot_copy(part, {1: near, 2: h, 3: ye, **there}, got3, (part, j), 10 + j, device, active)
             for j, (there, device) in enumerate(flips(2))
         ]
     for part in range(2, 6):
@@ -415,7 +424,7 @@
         both = {**first, two: mine[two]}
         for n, pair in enumerate((near, far)):
             halves[part, n] = (
-                half_copies(part, n, one, {1: pair, one: 1 - mine[one]}, None),
+                half_copy(part, n, one, {1: pair, one: 1 - mine[one]}, None),
                 None, at(part, {1: pair, **first}),
             )
             seconds[part, n] = (
@@ -426,30 +435,42 @@
                 thirds[part, n] = (
                     [
                         slot_copy(
-                            part, {1: pair, **both, **there}, got2, (part, j, 0, pair), 8 + 3 * n + j, device, None
+                            part, {1: pair, **both, **there}, got2, (part, j, 0, pair), 4 + 3 * n + j, device, None
                         )
                         for j, (there, device) in enumerate(flips(2))
                     ],
                     None, at(part, {1: pair, **both, 4: za, 5: ze}),
                 )
         if part < 4:
-            fourths[part] = along_x(part, {**both, 4: za, 5: ze}, got3, 14)
+            fourths[part] = along_x(part, {**both, 4: za, 5: ze}, got3, 10)
         else:
-            copies = along_x(part, both, got2, 8)
+            copies = along_x(part, both, got2, 4)
             thirds[part, 0] = ([copies[0]], None, None)
             thirds[part, 1] = (copies, active, at(part, {**both, 1: near}))
             fourths[part] = [
-                slot_copy(part, {1: near, **both, **there}, got3, (part, j), 14 + j, device, active)
+                slot_copy(part, {1: near, **both, **there}, got3, (part, j), 10 + j, device, active)
                 for j, (there, device) in enumerate(flips(1))
             ]
 
+    def add_across():
+        def add():
+            for _, copy in across_x:
+                copy.wait_recv()
+            here, there = at(1, {1: near}), at(1, {1: far})
+            total = gwb[here].astype(jnp.float32) + got0[here].astype(jnp.float32)
+            total = total + got1[here].astype(jnp.float32) + got0[there].astype(jnp.float32)
+            gwb[here] = total.astype(jnp.bfloat16)
+
+        pl.when(active)(add)
+        for sends, copy, _ in thirds[1, 1][0]:
+            when(sends, copy.start)
+
     def add_half(part, n):
         if (part, n) in halves:
-            copies, receives, here = halves[part, n]
+            (_, copy), receives, here = halves[part, n]
 
             def add():
-                for _, copy in copies:
-                    copy.wait_recv()
+                copy.wait_recv()
                 total = gwb[here].astype(jnp.float32) + got0[here].astype(jnp.float32)
                 gwb[here] = total.astype(jnp.bfloat16)
 
@@ -497,9 +518,7 @@
                 copy.wait_recv()
                 total = total + got3[slot].astype(jnp.float32)
             total = total.astype(jnp.bfloat16)
-            for j in range(3):
-                lane = 3 * PCOLS * (part // 3) + PCOLS * j + 256 * (part % 3)
-                fin[ye, za, ze, :, lane : lane + 256] = total[:, 256 * j : 256 * j + 256]
+            fin[ye, za, ze, :, PCOLS * part : PCOLS * part + PCOLS] = total
 
         pl.when(active)(add)
 
@@ -508,19 +527,24 @@
         lanes = pl.ds(pl.multiple_of(256 * pair, 256), 256)
         for r in range(4):
             st[:, WIDTH * r : WIDTH * r + WIDTH] = ss[1, r + 1, :, lanes].T
-        for j in range(3):
-            for part in order:
-                kk = part + PARTS * j
-                window = xs[(kk // 2) % 3, kk // 6 : kk // 6 + 4, :, 256 * (kk % 2) : 256 * (kk % 2) + 256]
-                term = jnp.dot(
-                    st[...], window.reshape(4 * WIDTH, 256), preferred_element_type=jnp.float32
-                )
-                gwb[part, pair, :, :, :, :, :, 256 * j : 256 * j + 256] = term.astype(jnp.bfloat16).reshape(
-                    2, 2, 2, 2, 16, 256
-                )
+        for run in order:
+            for part in run:
+                for j in range(3):
+                    kk = 3 * part + j
+                    window = xs[(kk // 2) % 3, kk // 6 : kk // 6 + 4, :, 256 * (kk % 2) : 256 * (kk % 2) + 256]
+                    term = jnp.dot(
+                        st[...], window.reshape(4 * WIDTH, 256), preferred_element_type=jnp.float32
+                    )
+                    gwb[part, pair, :, :, :, :, :, 256 * j : 256 * j + 256] = term.astype(jnp.bfloat16).reshape(
+                        2, 2, 2, 2, 16, 256
+                    )
+            for part in run:
                 if (part, n) in halves:
-                    sends, copy = halves[part, n][0][j]
+                    sends, copy = halves[part, n][0]
                     when(sends, copy.start)
+                if part == 1:
+                    for sends, copy in across_x[1:] if n else across_x[:1]:
+                        when(sends, copy.start)
 
     passed_in(0)
     passed_in(1)
@@ -530,14 +554,16 @@
         for copy in to_turn:
             copy.wait_recv()
 
-    @pl.loop(0, 3)
+    @pl.loop(0, 4)
     def _(r):
+        @pl.when(r == jnp.where(active, 2, 1))
+        def _():
+            crossed_far.wait_recv()
+            pass_on(2)
+
         forward_row(near, r)
 
-    crossed_far.wait_recv()
-    pass_on(2)
-    forward_row(near, 3)
-    weight_gradient(near, NEAR_ORDER)
+    weight_gradient(near, NEAR_RUNS)
 
     passed_in(2)
 
@@ -565,9 +591,7 @@
 
     for part in (0, 2, 3, 4, 5):
         add_half(part, 0)
-    weight_gradient(far, FAR_ORDER)
-    for part in range(2, 6):
-        add_second(part, 0)
+    weight_gradient(far, FAR_RUNS)
 
     pl.when(z > 0)(lambda: remote(ss.at[1, 0], ss.at[1, 0], s_send.at[1], s_recv.at[1], other_core).wait_recv())
     pl.when(z < 3)(lambda: remote(ss.at[1, 5], ss.at[1, 5], s_send.at[0], s_recv.at[0], other_core).wait_recv())
@@ -592,21 +616,27 @@
 
     ig_pair = remote(igp, igr, i_send.at[0], i_recv.at[0], other_core)
     ig_pair.start()
-    for part in FAR_ORDER:
+    for part in range(2, 6):
+        add_second(part, 0)
+    for part in (0, 2, 3, 4, 5):
         add_half(part, 1)
+    add_across()
 
     trow[4:8, :] = id_row[4:8, :]
     trow[0:4, :] = jnp.zeros((4, 128), jnp.float32)
 
     @pl.loop(0, 2)
     def _(k):
-        input_row(2 * c + k, acc)
-
-        @pl.when(k == 0)
-        def _():
-            ig_pair.wait_recv()
-
-        total = acc[...] + igr[k]
+        input_row(2 * c + k, igo.at[k])
+
+    for part in ORDER:
+        add_second(part, 1)
+
+    ig_pair.wait_recv()
+
+    @pl.loop(0, 2)
+    def _(k):
+        total = igo[k] + igr[k]
         gfb[k] = total.astype(jnp.bfloat16)
         column_sum = jnp.sum(total, axis=0, keepdims=True)
         for lane in range(4):
@@ -620,9 +650,6 @@
         copy = remote(trow, tpeer.at[k - 1], t_send.at[k - 1], t_recv.at[k - 1], {"tile": (t + k) % 8})
         copy.start()
         t_copies.append(copy)
-
-    for part in FAR_ORDER:
-        add_second(part, 1)
 
     @pl.loop(0, 4)
     def _(r):
@@ -641,7 +668,7 @@
         up_own[-1].start()
         up_pair[-1].start()
 
-    for part in FAR_ORDER:
+    for part in ORDER:
         add_third(part)
 
     for copy in t_copies:
@@ -653,14 +680,22 @@
         total = total + tpeer[k, 0:4, :]
     tall[0, 0:4, :] = total
     tall[0, 4:8, :] = trow[4:8, :]
+    y = 2 * h + lo
     v_copies = []
-    for k in range(1, 16):
-        to = (frame + k) % 16
-        copy = remote(
-            tall.at[0], tall.at[k], v_send.at[k - 1], v_recv.at[k - 1], {"fsdp": to // 2, "dp": to % 2}
-        )
+    for k in range(1, 4):
+        to = (y + k) % 4
+        v_copies.append(
+            remote(tall.at[0], tall.at[k], v_send.at[k - 1], v_recv.at[k - 1], {"fsdp": 2 * x + to // 2, "dp": to % 2})
+        )
+    for k in range(1, 4):
+        to = (x + k) % 4
+        v_copies.append(
+            remote(
+                tall.at[pl.ds(0, 4)], tall.at[pl.ds(4 * k, 4)], v_send.at[2 + k], v_recv.at[2 + k], {"fsdp": 2 * to + h}
+            )
+        )
+    for copy in v_copies[:3]:
         copy.start()
-        v_copies.append(copy)
 
     spreads, to_pair, to_self = [], [], []
     for g in range(2):
@@ -669,12 +704,9 @@
         spreads.append(
             [remote(piece_at, piece_at, f_send.at[g, k], f_recv.at[g, k], holders[k]) for k in range(7)]
         )
-        for j in range(3):
-            held = fin.at[:, :, :, :, pl.ds(3 * PCOLS * g + PCOLS * j, PCOLS)]
-            out = gw_out.at[:, :, :, :, pl.ds(2 * PCOLS * j + PCOLS * g, PCOLS)]
-            n = 3 * g + j
-            to_pair.append(remote(held, out, i_send.at[1 + n], i_recv.at[1 + n], other_core))
-            to_self.append(pltpu.make_async_copy(held, out, loc_sem.at[12 + n]))
+        held, out = fin.at[:, :, :, :, cols], gw_out.at[:, :, :, :, cols]
+        to_pair.append(remote(held, out, i_send.at[1 + g], i_recv.at[1 + g], other_core))
+        to_self.append(pltpu.make_async_copy(held, out, loc_sem.at[12 + g]))
 
     for g in range(2):
         for part in range(3 * g, 3 * g + 3):
@@ -685,38 +717,45 @@
             for copy in spreads[g]:
                 copy.start()
 
+    for copy in v_copies[:3]:
+        copy.wait_recv()
+    for copy in v_copies[3:]:
+        copy.start()
+
     @pl.when(active)
     def _():
         for g in range(2):
             for copy in spreads[g]:
                 copy.wait_recv()
-            for j in range(3):
-                to_pair[3 * g + j].start()
-                to_self[3 * g + j].start()
+            to_pair[g].start()
+            to_self[g].start()
         for g in range(2):
             for copy in spreads[g]:
                 copy.wait_send()
-        for j in range(6):
-            to_self[j].wait()
-            to_pair[j].wait_send()
+            to_self[g].wait()
+            to_pair[g].wait_send()
 
     @pl.when(c != xa)
     def _():
-        for j in range(6):
-            to_pair[j].wait_recv()
-
+        for g in range(2):
+            to_pair[g].wait_recv()
+
+    for copy in v_copies[3:]:
+        copy.wait_recv()
     for copy in v_copies:
-        copy.wait()
-    tab_copy = pltpu.make_async_copy(tall, tab_out, loc_sem.at[18])
+        copy.wait_send()
+    tab_copy = pltpu.make_async_copy(tall, tab_out, loc_sem.at[14])
     tab_copy.start()
 
     @pl.when(active)
     def _():
-        for copy in to_turn + to_flip + [to_far]:
+        for copy in to_turn + to_flip:
             copy.wait_send()
 
     @pl.when(passive)
     def _():
+        for copy in relay:
+            copy.wait_send()
         for j in range(3):
             passed[3, j][0].wait_send()
 
@@ -734,10 +773,9 @@
     def _():
         bottom_swap.wait_send()
 
-    for copies, _, _ in halves.values():
-        for sends, copy in copies:
-            when(sends, copy.wait_send)
-    for (sends, copy), _, _ in seconds.values():
+    for (sends, copy), _, _ in list(halves.values()) + list(seconds.values()):
+        when(sends, copy.wait_send)
+    for sends, copy in across_x:
         when(sends, copy.wait_send)
     for (part, n), (entry, _, _) in thirds.items():
         for sends, copy, _ in entry[1:] if part >= 4 and n == 1 else entry:
@@ -795,14 +833,15 @@
             pltpu.VMEM((2, 4, WIDTH, 256), bf16),
             pltpu.VMEM((4, 2 * WIDTH, 256), bf16),
             pltpu.VMEM((2, 2 * WIDTH, 128), f32),
-            pltpu.VMEM((WIDTH, 512), f32),
+            pltpu.VMEM((WIDTH, 256), f32),
+            pltpu.VMEM((2, WIDTH, CIN), f32),
             pltpu.VMEM((2, WIDTH, CIN), f32),
             pltpu.VMEM((2, WIDTH, CIN), f32),
             pltpu.VMEM((2, WIDTH, CIN), bf16),
             pltpu.VMEM((8, 128), f32),
             pltpu.VMEM((7, 8, 128), f32),
             pltpu.VMEM((16, 8, 128), f32),
-            dma((19,)),
+            dma((15,)),
             dma((7,)),
             dma((7,)),
             dma((11,)),
@@ -813,18 +852,18 @@
             dma((4, 3)),
             dma((2,)),
             dma((2,)),
-            dma((PARTS, 17)),
-            dma((PARTS, 17)),
+            dma((PARTS, 13)),
+            dma((PARTS, 13)),
             dma((2, 7)),
             dma((2, 7)),
             dma((2,)),
             dma((2,)),
+            dma((3,)),
+            dma((3,)),
             dma((7,)),
             dma((7,)),
-            dma((7,)),
-            dma((7,)),
-            dma((15,)),
-            dma((15,)),
+            dma((6,)),
+            dma((6,)),
         ],
         compiler_params=pltpu.CompilerParams(
             collective_id=0, has_side_effects=True, vmem_limit_bytes=60 * 2**20

time: 112 us -> 102 us (0.911)
  Pallas kernels: 101 us -> 91 us
    pallas_call x1, Pallas kernels: 101 us -> 91 us  [fused(): pl.pallas_call(kernel, out_shape=(jax.ShapeDtypeStruct((4, 2 * WIDTH, 256...]
where the time goes in v5:
time: 102 us
  Pallas kernels  91 us (89%)
  other arithmetic  4.32 us (4%)
  local copies, waits for them, and re-layouts  3.37 us (3%)
  matrix products  1.8 us (2%)
  between operations  1.32 us (1%)
    pallas_call x1, Pallas kernels, fused(): pl.pallas_call(kernel, out_shape=(jax.ShapeDtypeStruct((4, 2 * WIDTH, 256...  91 us
    convert_element_type x1, other arithmetic, shards(): grad_weight = gw.reshape(128, 9 * CIN).astype(jnp.float32)  3.03 us
    unnamed x8, local copies, waits for them, and re-layouts  2.56 us

profile of v5, /device:TPU:1, one launch (start us, length us, event | category | flops | bytes accessed | tf_op | source)
XLA Modules:
  0.0 101.8 jit_solution(3077205594175747496)
XLA Ops:
  1.3 1.3 %dynamic-slice_convert_fusion.shift_row = f32[1,512]{1,0:T(1,128)} fusion(bf16[600,512]{1,0:T(8,128)(2,1)} %param.6, s32[]{:T(128)S(6)} %select_n.3), kind=kLoop, calls=%fused_computation.7 | loop fusion | flops 512 | bytes 3076 | tf_op jit(solution)/shard_map/convert_element_type | solution.py:880
  2.6 0.6 broadcast_in_dim.16.id_row
  3.2 91.0 %conv_block.1 = (bf16[4,768,256]{2,1,0:T(8,128)(2,1)}, bf16[2,2,2,16,4608]{4,3,2,1,0:T(8,128)(2,1)}, bf16[2,384,512]{2,1,0:T(8,128)(2,1)}, f32[16,8,128]{2,1,0:T(8,128)}) custom-call(bf16[2,384,512]{2,1,0:T(8,128)(2,1)} %bitcast.22, bf16[2,2,2,16,4608]{4,3,2,1,0:T(8,128)(2,1)} %bitcast.21, bf16[4,768,256]{2,1,0:T(8,128)(2,1)} %bitcast.20, ...), custom_call_target="tpu_custom_call" | custom-call | flops 21743271936 | bytes 20000000 | tf_op jit(solution)/shard_map/conv_block/pallas_call | solution.py:810
  94.2 0.0 copy-start.2
  94.2 0.0 copy-start
  94.2 3.0 %bitcast_convert_fusion = f32[128,4608]{1,0:T(8,128)} fusion(bf16[2,2,2,16,4608]{4,3,2,1,0:T(8,128)(2,1)} %get-tuple-element.9), kind=kLoop, calls=%fused_computation | loop fusion | flops 589824 | bytes 3538944 | tf_op jit(solution)/shard_map/convert_element_type | solution.py:892
  97.2 0.0 copy-done.2
  97.3 0.2 slice_reduce_fusion
  97.5 1.8 %fusion = f32[600,512]{1,0:T(8,128)} fusion(f32[2,8,4,128]{3,2,1,0:T(4,128)S(1)} %bitcast.19, f32[16]{0:T(128)S(1)} %slice_reduce_fusion), kind=kOutput, calls=%fused_computation.2 | convolution fusion | flops 58992000 | bytes 1261632 | tf_op jit(solution)/shard_map/dot_general | solution.py:888
  99.3 0.0 copy-done
  99.3 0.0 copy-start.1
  99.3 1.1 %copy.17 = bf16[1,4,768,256]{3,2,1,0:T(8,128)(2,1)} copy(bf16[1,4,768,256]{3,2,1,0:T(8,128)(2,1)S(1)} %bitcast.17) | data formatting | bytes 3145728
  100.4 0.5 copy-done.1
  100.9 0.9 copy.18
  (1 shorter events, 0.0 us)
Async XLA Ops:
  94.2 3.1 %copy-start.2 = (f32[16,8,128]{2,1,0:T(8,128)S(1)}, f32[16,8,128]{2,1,0:T(8,128)}, u32[]{:S(2)}) copy-start(f32[16,8,128]{2,1,0:T(8,128)} %get-tuple-element.11) | copy-start | bytes 196612
  94.2 5.1 %copy-start = (bf16[4,768,256]{2,1,0:T(8,128)(2,1)S(1)}, bf16[4,768,256]{2,1,0:T(8,128)(2,1)}, u32[]{:S(2)}) copy-start(bf16[4,768,256]{2,1,0:T(8,128)(2,1)} %get-tuple-element.8) | copy-start | bytes 4718596
  99.3 1.7 %copy-start.1 = (bf16[2,384,512]{2,1,0:T(8,128)(2,1)S(1)}, bf16[2,384,512]{2,1,0:T(8,128)(2,1)}, u32[]{:S(2)}) copy-start(bf16[2,384,512]{2,1,0:T(8,128)(2,1)} %get-tuple-element.10) | copy-start | bytes 2359300

commit v6 on v5

--- a/solution.py
+++ b/solution.py
@@ -19,14 +19,16 @@
 
 FIRST = [(0, 1), (1, 0), (2, 3), (3, 2), (4, 5), (5, 4)]
 NEAR_RUNS = ((0, 1, 2, 3, 4, 5),)
-FAR_RUNS = ((1, 0), (2, 3), (4, 5))
+FAR_RUNS = ((0, 1), (2, 3), (4, 5))
+SPANS = ((0, 3), (3, 2), (5, 4), (9, 4), (13, 3), (16, 2))
+GCOLS = 1024
 ORDER = (0, 2, 3, 4, 5, 1)
 
 MESH = pl.DeviceIdType.MESH
 
 
 def kernel(
-    feat, weight, cot, shift_row, id_row,
+    feat, weight, cot, shift_row_in, frame_id,
     up_out, gw_out, gf_out, tab_out,
     xs, ss, st, wall, gwb, got0, got1, got2, got3, fin, ctv, cts, actv, upb, wide, acc, igp, igo, igr, gfb,
     trow, tpeer, tall,
@@ -108,7 +110,7 @@
     for k in range(2):
         for lane in range(4):
             at = pl.ds(128 * lane, 128)
-            row = xs[1, 1 + 2 * c + k, :, at].astype(jnp.float32) + shift_row[:, at]
+            row = xs[1, 1 + 2 * c + k, :, at].astype(jnp.float32) + shift_row_in[:, at]
             xs[1, 1 + 2 * c + k, :, at] = row.astype(jnp.bfloat16)
 
     pl.semaphore_wait(barrier, 25)
@@ -333,7 +335,13 @@
             ss[1, r + 1, rows, out] = (cts[v, r, rows].astype(jnp.float32) * slope).astype(jnp.bfloat16)
 
     def at(part, fixed):
-        return (part,) + tuple(fixed.get(d, slice(None)) for d in range(1, 6))
+        return (part,) + tuple(fixed.get(d, slice(None)) for d in range(1, 6)) + (slice(None), lanes_of(part))
+
+    def lanes_of(part):
+        return pl.ds(0, 256 * SPANS[part][1])
+
+    def in_slot(slots, slot):
+        return slot + (slice(None),) * (len(slots.shape) - 1 - len(slot)) + (lanes_of(slot[0]),)
 
     def when(condition, body):
         if condition is None:
@@ -366,7 +374,7 @@
         return (
             sends,
             remote(
-                gwb.at[at(part, there)], slots.at[slot], r_send.at[part, sem], r_recv.at[part, sem], device
+                gwb.at[at(part, there)], slots.at[in_slot(slots, slot)], r_send.at[part, sem], r_recv.at[part, sem], device
             ),
             slot,
         )
@@ -502,7 +510,7 @@
                     total = gwb[here].astype(jnp.float32)
                     for _, copy, slot in entry:
                         copy.wait_recv()
-                        total = total + got2[slot].astype(jnp.float32)
+                        total = total + got2[in_slot(got2, slot)].astype(jnp.float32)
                     gwb[here] = total.astype(jnp.bfloat16)
 
                 when(receives, add)
@@ -516,9 +524,10 @@
             total = gwb[here].astype(jnp.float32)
             for _, copy, slot in fourths[part]:
                 copy.wait_recv()
-                total = total + got3[slot].astype(jnp.float32)
+                total = total + got3[in_slot(got3, slot)].astype(jnp.float32)
             total = total.astype(jnp.bfloat16)
-            fin[ye, za, ze, :, PCOLS * part : PCOLS * part + PCOLS] = total
+            first, count = SPANS[part]
+            fin[ye, za, ze, :, 256 * first : 256 * (first + count)] = total
 
         pl.when(active)(add)
 
@@ -529,8 +538,9 @@
             st[:, WIDTH * r : WIDTH * r + WIDTH] = ss[1, r + 1, :, lanes].T
         for run in order:
             for part in run:
-                for j in range(3):
-                    kk = 3 * part + j
+                first, count = SPANS[part]
+                for j in range(count):
+                    kk = first + j
                     window = xs[(kk // 2) % 3, kk // 6 : kk // 6 + 4, :, 256 * (kk % 2) : 256 * (kk % 2) + 256]
                     term = jnp.dot(
                         st[...], window.reshape(4 * WIDTH, 256), preferred_element_type=jnp.float32
@@ -556,7 +566,7 @@
 
     @pl.loop(0, 4)
     def _(r):
-        @pl.when(r == jnp.where(active, 2, 1))
+        @pl.when(r == jnp.where(active, 3, 2))
         def _():
             crossed_far.wait_recv()
             pass_on(2)
@@ -580,6 +590,8 @@
     def _(k):
         forward_row(far, 3 * k)
 
+    rim_above = remote(ss.at[1, 0], ss.at[1, 0], s_send.at[1], s_recv.at[1], other_core)
+    rim_below = remote(ss.at[1, 5], ss.at[1, 5], s_send.at[0], s_recv.at[0], other_core)
     slope_up = remote(ss.at[1, 1], ss.at[1, 5], s_send.at[0], s_recv.at[0], {"tile": 2 * jnp.maximum(z - 1, 0) + c})
     slope_down = remote(ss.at[1, 4], ss.at[1, 0], s_send.at[1], s_recv.at[1], {"tile": 2 * jnp.minimum(z + 1, 3) + c})
     pl.when(z > 0)(slope_up.start)
@@ -593,9 +605,7 @@
         add_half(part, 0)
     weight_gradient(far, FAR_RUNS)
 
-    pl.when(z > 0)(lambda: remote(ss.at[1, 0], ss.at[1, 0], s_send.at[1], s_recv.at[1], other_core).wait_recv())
-    pl.when(z < 3)(lambda: remote(ss.at[1, 5], ss.at[1, 5], s_send.at[0], s_recv.at[0], other_core).wait_recv())
-    shift_rows(ss, 0, 6)
+    shift_rows(ss, 1, 4)
 
     def input_row(r, out):
         lhs = jnp.concatenate([ss[2 - tap % 3, r + 2 - tap // 3] for tap in range(9)], axis=1)
@@ -612,7 +622,16 @@
 
     @pl.loop(0, 2)
     def _(k):
-        input_row(2 * (1 - c) + k, igp.at[k])
+        @pl.when(k == 1)
+        def _():
+            pl.when(z > 0)(rim_above.wait_recv)
+            pl.when(z < 3)(rim_below.wait_recv)
+            shift_row(ss, 0)
+            shift_row(ss, 5)
+
+        r = jnp.where(k == 0, 2 - c, 3 - 3 * c)
+        input_row(r, igp.at[r - 2 * (1 - c)])
+
 
     ig_pair = remote(igp, igr, i_send.at[0], i_recv.at[0], other_core)
     ig_pair.start()
@@ -622,7 +641,7 @@
         add_half(part, 1)
     add_across()
 
-    trow[4:8, :] = id_row[4:8, :]
+    trow[4:8, :] = jnp.full((4, 128), frame_id[0], jnp.int32).astype(jnp.float32)
     trow[0:4, :] = jnp.zeros((4, 128), jnp.float32)
 
     @pl.loop(0, 2)
@@ -699,7 +718,8 @@
 
     spreads, to_pair, to_self = [], [], []
     for g in range(2):
-        cols = pl.ds(3 * PCOLS * g, 3 * PCOLS)
+        first, last = SPANS[3 * g][0], SPANS[3 * g + 2][0] + SPANS[3 * g + 2][1]
+        cols = pl.ds(256 * first, 256 * (last - first))
         piece_at = fin.at[ye, za, ze, :, cols]
         spreads.append(
             [remote(piece_at, piece_at, f_send.at[g, k], f_recv.at[g, k], holders[k]) for k in range(7)]
@@ -802,7 +822,7 @@
     tab_copy.wait()
 
 
-def fused(features, weight, cot, shift_row, id_row):
+def fused(features, weight, cot, shift_row, frame_id):
     any_space = pl.BlockSpec(memory_space=pl.ANY)
     vmem = pl.BlockSpec(memory_space=pltpu.VMEM)
     bf16, f32 = jnp.bfloat16, jnp.float32
@@ -815,18 +835,18 @@
             jax.ShapeDtypeStruct((2, WIDTH, CIN), bf16),
             jax.ShapeDtypeStruct((16, 8, 128), f32),
         ),
-        in_specs=[any_space, any_space, any_space, vmem, vmem],
+        in_specs=[any_space, any_space, any_space, vmem, pl.BlockSpec(memory_space=pltpu.SMEM)],
         out_specs=[any_space] * 4,
         scratch_shapes=[
             pltpu.VMEM((3, 6, WIDTH, CIN), bf16),
             pltpu.VMEM((3, 6, WIDTH, HALF), bf16),
             pltpu.VMEM((256, 4 * WIDTH), bf16),
             pltpu.VMEM((PARTS, 2, 2, 2, 2, 2, 16, PCOLS), bf16),
-            pltpu.VMEM((PARTS, 2, 2, 2, 2, 2, 16, PCOLS), bf16),
-            pltpu.VMEM((PARTS, 2, 2, 2, 2, 2, 16, PCOLS), bf16),
-            pltpu.VMEM((PARTS, 2, 2, 2, 2, 2, 16, PCOLS), bf16),
-            pltpu.VMEM((PARTS, 3, 2, 2, 16, PCOLS), bf16),
-            pltpu.VMEM((PARTS, 3, 16, PCOLS), bf16),
+            pltpu.VMEM((PARTS, 2, 2, 2, 2, 2, 16, GCOLS), bf16),
+            pltpu.VMEM((PARTS, 2, 2, 2, 2, 2, 16, GCOLS), bf16),
+            pltpu.VMEM((PARTS, 2, 2, 2, 2, 2, 16, GCOLS), bf16),
+            pltpu.VMEM((PARTS, 3, 2, 2, 16, GCOLS), bf16),
+            pltpu.VMEM((PARTS, 3, 16, GCOLS), bf16),
             pltpu.VMEM((2, 2, 2, 16, 9 * CIN), bf16),
             pltpu.VMEM((4, 2 * WIDTH, 256), bf16),
             pltpu.VMEM((2, 4, WIDTH, 256), bf16),
@@ -872,22 +892,21 @@
             flops=6 * 768 * 4608 * 1024, bytes_accessed=2 * 10**7, transcendentals=3 * 768 * 1024
         ),
         name="conv_block",
-    )(features, weight, cot, shift_row, id_row)
+    )(features, weight, cot, shift_row, frame_id)
 
 
 def shards(features, frame_table, frame_ids, conv_weight, cotangent):
     video_len = frame_table.shape[0]
     shift = lax.dynamic_slice_in_dim(frame_table, frame_ids[0], 1, axis=0).astype(jnp.float32)
-    id_row = jnp.broadcast_to(frame_ids.astype(jnp.float32)[:, None], (8, 128))
     up, gw, gf, tab = fused(
-        features[0], conv_weight.reshape(2, 2, 2, 16, 9 * CIN), cotangent[0], shift, id_row
+        features[0], conv_weight.reshape(2, 2, 2, 16, 9 * CIN), cotangent[0], shift, frame_ids
     )
     sums = tab[:, :4].reshape(16, CIN)
     frames = tab[:, 4, 0]
     picker = (frames[:, None] == jnp.arange(video_len, dtype=jnp.float32)[None, :]).astype(jnp.float32)
     grad_table = lax.dot_general(
         picker, sums, (((0,), (0,)), ((), ())),
-        precision=lax.Precision.HIGHEST, preferred_element_type=jnp.float32,
+        precision=lax.Precision.HIGH, preferred_element_type=jnp.float32,
     )
     grad_weight = gw.reshape(128, 9 * CIN).astype(jnp.float32)
     return (up[None], grad_weight, gf[None], grad_table)

time: 102 us -> 98.3 us (0.964)
  Pallas kernels: 91 us -> 88 us
    pallas_call x1, Pallas kernels: 91 us -> 88 us  [fused(): pl.pallas_call(kernel, out_shape=(jax.ShapeDtypeStruct((4, 2 * WIDTH, 256...]
where the time goes in v6:
time: 98.3 us; the launch traced here: 98 us
  Pallas kernels  88 us (90%)
  other arithmetic  4.32 us (4%)
  local copies, waits for them, and re-layouts  2.77 us (3%)
  matrix products  1.64 us (2%)
  between operations  1.31 us (1%)
    pallas_call x1, Pallas kernels, fused(): pl.pallas_call(kernel, out_shape=(jax.ShapeDtypeStruct((4, 2 * WIDTH, 256...  88 us
    convert_element_type x1, other arithmetic, shards(): grad_weight = gw.reshape(128, 9 * CIN).astype(jnp.float32)  3.03 us
    unnamed x8, local copies, waits for them, and re-layouts  2.56 us

profile of v6, /device:TPU:1, one launch (start us, length us, event | category | flops | bytes accessed | tf_op | source)
XLA Modules:
  0.0 98.0 jit_solution(7983408797557863245)
XLA Ops:
  1.3 1.3 %dynamic-slice_convert_fusion.shift_row_in = f32[1,512]{1,0:T(1,128)} fusion(bf16[600,512]{1,0:T(8,128)(2,1)} %param.6, s32[]{:T(128)S(6)} %select_n.3), kind=kLoop, calls=%fused_computation.7 | loop fusion | flops 512 | bytes 3076 | tf_op jit(solution)/shard_map/convert_element_type | solution.py:900
  2.6 88.0 %conv_block.1 = (bf16[4,768,256]{2,1,0:T(8,128)(2,1)}, bf16[2,2,2,16,4608]{4,3,2,1,0:T(8,128)(2,1)}, bf16[2,384,512]{2,1,0:T(8,128)(2,1)}, f32[16,8,128]{2,1,0:T(8,128)}) custom-call(bf16[2,384,512]{2,1,0:T(8,128)(2,1)} %bitcast.21, bf16[2,2,2,16,4608]{4,3,2,1,0:T(8,128)(2,1)} %bitcast.20, bf16[4,768,256]{2,1,0:T(8,128)(2,1)} %bitcast.19, ...), custom_call_target="tpu_custom_call" | custom-call | flops 21743271936 | bytes 20000000 | tf_op jit(solution)/shard_map/conv_block/pallas_call | solution.py:830
  90.5 0.0 copy-start.2
  90.6 0.0 copy-start
  90.6 3.0 %bitcast_convert_fusion = f32[128,4608]{1,0:T(8,128)} fusion(bf16[2,2,2,16,4608]{4,3,2,1,0:T(8,128)(2,1)} %get-tuple-element.9), kind=kLoop, calls=%fused_computation | loop fusion | flops 589824 | bytes 3538944 | tf_op jit(solution)/shard_map/convert_element_type | solution.py:911
  93.6 0.0 copy-done.2
  93.6 0.2 slice_reduce_fusion
  93.8 1.6 %fusion = f32[600,512]{1,0:T(8,128)} fusion(f32[2,8,4,128]{3,2,1,0:T(4,128)S(1)} %bitcast.18, f32[16]{0:T(128)S(1)} %slice_reduce_fusion), kind=kOutput, calls=%fused_computation.2 | convolution fusion | flops 29500800 | bytes 1261632 | tf_op jit(solution)/shard_map/dot_general | solution.py:907
  95.4 0.0 copy-done
  95.5 0.0 copy-start.1
  95.5 1.1 %copy.17 = bf16[1,4,768,256]{3,2,1,0:T(8,128)(2,1)} copy(bf16[1,4,768,256]{3,2,1,0:T(8,128)(2,1)S(1)} %bitcast.16) | data formatting | bytes 3145728
  96.6 0.5 copy-done.1
  97.1 0.9 copy.18
  (1 shorter events, 0.0 us)
Async XLA Ops:
  90.5 3.1 %copy-start.2 = (f32[16,8,128]{2,1,0:T(8,128)S(1)}, f32[16,8,128]{2,1,0:T(8,128)}, u32[]{:S(2)}) copy-start(f32[16,8,128]{2,1,0:T(8,128)} %get-tuple-element.11) | copy-start | bytes 196612
  90.6 4.9 %copy-start = (bf16[4,768,256]{2,1,0:T(8,128)(2,1)S(1)}, bf16[4,768,256]{2,1,0:T(8,128)(2,1)}, u32[]{:S(2)}) copy-start(bf16[4,768,256]{2,1,0:T(8,128)(2,1)} %get-tuple-element.8) | copy-start | bytes 4718596
  95.5 1.7 %copy-start.1 = (bf16[2,384,512]{2,1,0:T(8,128)(2,1)S(1)}, bf16[2,384,512]{2,1,0:T(8,128)(2,1)}, u32[]{:S(2)}) copy-start(bf16[2,384,512]{2,1,0:T(8,128)(2,1)} %get-tuple-element.10) | copy-start | bytes 2359300

commit v7 on v6

--- a/solution.py
+++ b/solution.py
@@ -17,12 +17,11 @@
 
 DIMS = 6
 
-FIRST = [(0, 1), (1, 0), (2, 3), (3, 2), (4, 5), (5, 4)]
+FIRST = [None, None, (2, 3), (3, 2), (4, 5), (5, 4)]
 NEAR_RUNS = ((0, 1, 2, 3, 4, 5),)
 FAR_RUNS = ((0, 1), (2, 3), (4, 5))
-SPANS = ((0, 3), (3, 2), (5, 4), (9, 4), (13, 3), (16, 2))
+SPANS = ((0, 2), (2, 2), (4, 4), (8, 4), (12, 3), (15, 3))
 GCOLS = 1024
-ORDER = (0, 2, 3, 4, 5, 1)
 
 MESH = pl.DeviceIdType.MESH
 
@@ -396,24 +395,25 @@
             )
         ]
 
-    for n, pair in enumerate((near, far)):
-        halves[0, n] = (half_copy(0, n, 0, {1: pair}, passive), active, at(0, {1: pair}))
-    seconds[0, 1] = (second_copy(0, 1, 1, {1: far}, active), active, at(0, {1: near}))
-    across_x = [
-        (
-            sends,
-            remote(
-                gwb.at[at(1, {1: pair})], slots.at[at(1, {1: place})], r_send.at[1, j], r_recv.at[1, j], device
-            ),
-        )
-        for j, (sends, pair, device, slots, place) in enumerate(
+    across_x = {
+        part: [
             (
-                (passive, near, partner[0], got0, near),
-                (active, far, partner[1], got1, far),
-                (passive, far, two_away, got0, near),
+                sends,
+                remote(
+                    gwb.at[at(part, {1: pair})], slots.at[at(part, {1: place})],
+                    r_send.at[part, j], r_recv.at[part, j], device,
+                ),
             )
-        )
-    ]
+            for j, (sends, pair, device, slots, place) in enumerate(
+                (
+                    (passive, near, partner[0], got0, near),
+                    (active, far, partner[1], got1, far),
+                    (passive, far, two_away, got0, near),
+                )
+            )
+        ]
+        for part in (0, 1)
+    }
     for part in (0, 1):
         thirds[part, 1] = (
             [
@@ -460,17 +460,17 @@
                 for j, (there, device) in enumerate(flips(1))
             ]
 
-    def add_across():
+    def add_across(part):
         def add():
-            for _, copy in across_x:
+            for _, copy in across_x[part]:
                 copy.wait_recv()
-            here, there = at(1, {1: near}), at(1, {1: far})
+            here, there = at(part, {1: near}), at(part, {1: far})
             total = gwb[here].astype(jnp.float32) + got0[here].astype(jnp.float32)
             total = total + got1[here].astype(jnp.float32) + got0[there].astype(jnp.float32)
             gwb[here] = total.astype(jnp.bfloat16)
 
         pl.when(active)(add)
-        for sends, copy, _ in thirds[1, 1][0]:
+        for sends, copy, _ in thirds[part, 1][0]:
             when(sends, copy.start)
 
     def add_half(part, n):
@@ -552,8 +552,8 @@
                 if (part, n) in halves:
                     sends, copy = halves[part, n][0]
                     when(sends, copy.start)
-                if part == 1:
-                    for sends, copy in across_x[1:] if n else across_x[:1]:
+                if part in across_x:
+                    for sends, copy in across_x[part][1:] if n else across_x[part][:1]:
                         when(sends, copy.start)
 
     passed_in(0)
@@ -601,7 +601,7 @@
     def _(k):
         forward_row(far, 2 - k)
 
-    for part in (0, 2, 3, 4, 5):
+    for part in range(2, 6):
         add_half(part, 0)
     weight_gradient(far, FAR_RUNS)
 
@@ -637,9 +637,10 @@
     ig_pair.start()
     for part in range(2, 6):
         add_second(part, 0)
-    for part in (0, 2, 3, 4, 5):
+    for part in range(2, 6):
         add_half(part, 1)
-    add_across()
+    for part in range(2):
+        add_across(part)
 
     trow[4:8, :] = jnp.full((4, 128), frame_id[0], jnp.int32).astype(jnp.float32)
     trow[0:4, :] = jnp.zeros((4, 128), jnp.float32)
@@ -648,7 +649,7 @@
     def _(k):
         input_row(2 * c + k, igo.at[k])
 
-    for part in ORDER:
+    for part in range(2, 6):
         add_second(part, 1)
 
     ig_pair.wait_recv()
@@ -687,7 +688,7 @@
         up_own[-1].start()
         up_pair[-1].start()
 
-    for part in ORDER:
+    for part in range(PARTS):
         add_third(part)
 
     for copy in t_copies:
@@ -795,7 +796,7 @@
 
     for (sends, copy), _, _ in list(halves.values()) + list(seconds.values()):
         when(sends, copy.wait_send)
-    for sends, copy in across_x:
+    for sends, copy in across_x[0] + across_x[1]:
         when(sends, copy.wait_send)
     for (part, n), (entry, _, _) in thirds.items():
         for sends, copy, _ in entry[1:] if part >= 4 and n == 1 else entry:

time: 98.3 us -> 94.5 us (0.961)
  Pallas kernels: 88 us -> 84.2 us
    pallas_call x1, Pallas kernels: 88 us -> 84.2 us  [fused(): pl.pallas_call(kernel, out_shape=(jax.ShapeDtypeStruct((4, 2 * WIDTH, 256...]
where the time goes in v7:
time: 94.5 us; the launch traced here: 94.2 us
  Pallas kernels  84.2 us (89%)
  other arithmetic  4.32 us (5%)
  local copies, waits for them, and re-layouts  2.77 us (3%)
  matrix products  1.64 us (2%)
  between operations  1.31 us (1%)
    pallas_call x1, Pallas kernels, fused(): pl.pallas_call(kernel, out_shape=(jax.ShapeDtypeStruct((4, 2 * WIDTH, 256...  84.2 us
    convert_element_type x1, other arithmetic, shards(): grad_weight = gw.reshape(128, 9 * CIN).astype(jnp.float32)  3.03 us
    unnamed x8, local copies, waits for them, and re-layouts  2.56 us

profile of v7, /device:TPU:1, one launch (start us, length us, event | category | flops | bytes accessed | tf_op | source)
XLA Modules:
  0.0 94.2 jit_solution(12439285648288404441)
XLA Ops:
  1.3 1.3 %dynamic-slice_convert_fusion.shift_row_in = f32[1,512]{1,0:T(1,128)} fusion(bf16[600,512]{1,0:T(8,128)(2,1)} %param.6, s32[]{:T(128)S(6)} %select_n.3), kind=kLoop, calls=%fused_computation.7 | loop fusion | flops 512 | bytes 3076 | tf_op jit(solution)/shard_map/convert_element_type | solution.py:901
  2.6 84.2 %conv_block.1 = (bf16[4,768,256]{2,1,0:T(8,128)(2,1)}, bf16[2,2,2,16,4608]{4,3,2,1,0:T(8,128)(2,1)}, bf16[2,384,512]{2,1,0:T(8,128)(2,1)}, f32[16,8,128]{2,1,0:T(8,128)}) custom-call(bf16[2,384,512]{2,1,0:T(8,128)(2,1)} %bitcast.21, bf16[2,2,2,16,4608]{4,3,2,1,0:T(8,128)(2,1)} %bitcast.20, bf16[4,768,256]{2,1,0:T(8,128)(2,1)} %bitcast.19, ...), custom_call_target="tpu_custom_call" | custom-call | flops 21743271936 | bytes 20000000 | tf_op jit(solution)/shard_map/conv_block/pallas_call | solution.py:831
  86.8 0.0 copy-start.2
  86.8 0.0 copy-start
  86.8 3.0 %bitcast_convert_fusion = f32[128,4608]{1,0:T(8,128)} fusion(bf16[2,2,2,16,4608]{4,3,2,1,0:T(8,128)(2,1)} %get-tuple-element.9), kind=kLoop, calls=%fused_computation | loop fusion | flops 589824 | bytes 3538944 | tf_op jit(solution)/shard_map/convert_element_type | solution.py:912
  89.8 0.0 copy-done.2
  89.8 0.2 slice_reduce_fusion
  90.0 1.6 %fusion = f32[600,512]{1,0:T(8,128)} fusion(f32[2,8,4,128]{3,2,1,0:T(4,128)S(1)} %bitcast.18, f32[16]{0:T(128)S(1)} %slice_reduce_fusion), kind=kOutput, calls=%fused_computation.2 | convolution fusion | flops 29500800 | bytes 1261632 | tf_op jit(solution)/shard_map/dot_general | solution.py:908
  91.7 0.0 copy-done
  91.7 0.0 copy-start.1
  91.7 1.1 %copy.17 = bf16[1,4,768,256]{3,2,1,0:T(8,128)(2,1)} copy(bf16[1,4,768,256]{3,2,1,0:T(8,128)(2,1)S(1)} %bitcast.16) | data formatting | bytes 3145728
  92.8 0.5 copy-done.1
  93.3 0.9 copy.18
  (1 shorter events, 0.0 us)
Async XLA Ops:
  86.8 3.1 %copy-start.2 = (f32[16,8,128]{2,1,0:T(8,128)S(1)}, f32[16,8,128]{2,1,0:T(8,128)}, u32[]{:S(2)}) copy-start(f32[16,8,128]{2,1,0:T(8,128)} %get-tuple-element.11) | copy-start | bytes 196612
  86.8 4.9 %copy-start = (bf16[4,768,256]{2,1,0:T(8,128)(2,1)S(1)}, bf16[4,768,256]{2,1,0:T(8,128)(2,1)}, u32[]{:S(2)}) copy-start(bf16[4,768,256]{2,1,0:T(8,128)(2,1)} %get-tuple-element.8) | copy-start | bytes 4718596
  91.7 1.7 %copy-start.1 = (bf16[2,384,512]{2,1,0:T(8,128)(2,1)S(1)}, bf16[2,384,512]{2,1,0:T(8,128)(2,1)}, u32[]{:S(2)}) copy-start(bf16[2,384,512]{2,1,0:T(8,128)(2,1)} %get-tuple-element.10) | copy-start | bytes 2359300

commit v8 on v7

--- a/solution.py
+++ b/solution.py
@@ -718,19 +718,22 @@
         copy.start()
 
     spreads, to_pair, to_self = [], [], []
-    for g in range(2):
-        first, last = SPANS[3 * g][0], SPANS[3 * g + 2][0] + SPANS[3 * g + 2][1]
+    groups = ((0, 1, 2), (3, 4, 5))
+    for g, parts in enumerate(groups):
+        first, last = SPANS[parts[0]][0], SPANS[parts[-1]][0] + SPANS[parts[-1]][1]
         cols = pl.ds(256 * first, 256 * (last - first))
         piece_at = fin.at[ye, za, ze, :, cols]
         spreads.append(
             [remote(piece_at, piece_at, f_send.at[g, k], f_recv.at[g, k], holders[k]) for k in range(7)]
         )
-        held, out = fin.at[:, :, :, :, cols], gw_out.at[:, :, :, :, cols]
-        to_pair.append(remote(held, out, i_send.at[1 + g], i_recv.at[1 + g], other_core))
-        to_self.append(pltpu.make_async_copy(held, out, loc_sem.at[12 + g]))
-
-    for g in range(2):
-        for part in range(3 * g, 3 * g + 3):
+        for n, row in enumerate((ye, 1 - ye)):
+            held, out = fin.at[row, :, :, :, cols], gw_out.at[row, :, :, :, cols]
+            sem = 2 * g + n
+            to_pair.append(remote(held, out, i_send.at[1 + sem], i_recv.at[1 + sem], other_core))
+            to_self.append(pltpu.make_async_copy(held, out, loc_sem.at[12 + sem]))
+
+    for g, parts in enumerate(groups):
+        for part in parts:
             add_fourth(part)
 
         @pl.when(active)
@@ -746,26 +749,28 @@
     @pl.when(active)
     def _():
         for g in range(2):
-            for copy in spreads[g]:
-                copy.wait_recv()
-            to_pair[g].start()
-            to_self[g].start()
+            for n in range(2):
+                for k in range(1 - n, 7, 2):
+                    spreads[g][k].wait_recv()
+                to_pair[2 * g + n].start()
+                to_self[2 * g + n].start()
         for g in range(2):
             for copy in spreads[g]:
                 copy.wait_send()
-            to_self[g].wait()
-            to_pair[g].wait_send()
-
-    @pl.when(c != xa)
-    def _():
-        for g in range(2):
-            to_pair[g].wait_recv()
+        for n in range(4):
+            to_self[n].wait()
+            to_pair[n].wait_send()
+
+    @pl.when(passive)
+    def _():
+        for n in range(4):
+            to_pair[n].wait_recv()
 
     for copy in v_copies[3:]:
         copy.wait_recv()
     for copy in v_copies:
         copy.wait_send()
-    tab_copy = pltpu.make_async_copy(tall, tab_out, loc_sem.at[14])
+    tab_copy = pltpu.make_async_copy(tall, tab_out, loc_sem.at[16])
     tab_copy.start()
 
     @pl.when(active)
@@ -862,7 +867,7 @@
             pltpu.VMEM((8, 128), f32),
             pltpu.VMEM((7, 8, 128), f32),
             pltpu.VMEM((16, 8, 128), f32),
-            dma((15,)),
+            dma((17,)),
             dma((7,)),
             dma((7,)),
             dma((11,)),
@@ -879,8 +884,8 @@
             dma((2, 7)),
             dma((2,)),
             dma((2,)),
-            dma((3,)),
-            dma((3,)),
+            dma((5,)),
+            dma((5,)),
             dma((7,)),
             dma((7,)),
             dma((6,)),
@@ -896,20 +901,87 @@
     )(features, weight, cot, shift_row, frame_id)
 
 
+def finish(up, gw, gf, tab, up_out, gw_out, gf_out, table_out, gw_in, gw_wide, tab_in, table, up_in, gf_in, sems):
+    moves = [
+        (
+            pltpu.make_async_copy(source.at[k], held.at[k], sems.at[2 * (first + k)]),
+            pltpu.make_async_copy(held.at[k], out.at[k], sems.at[2 * (first + k) + 1]),
+        )
+        for source, held, out, first, count in ((up, up_in, up_out, 0, 4), (gf, gf_in, gf_out, 4, 2))
+        for k in range(count)
+    ]
+    loads = [
+        pltpu.make_async_copy(gw.at[k // 4, k // 2 % 2, k % 2], gw_in.at[k], sems.at[12 + k]) for k in range(8)
+    ]
+    stores = [
+        pltpu.make_async_copy(gw_wide.at[pl.ds(16 * k, 16)], gw_out.at[pl.ds(16 * k, 16)], sems.at[20 + k])
+        for k in range(8)
+    ]
+    tab_load = pltpu.make_async_copy(tab, tab_in, sems.at[28])
+    table_store = pltpu.make_async_copy(table, table_out, sems.at[29])
+    tab_load.start()
+    for copy in loads + [load for load, _ in moves]:
+        copy.start()
+
+    tab_load.wait()
+    sums = jnp.concatenate([tab_in[:, k, :] for k in range(4)], axis=1)
+    frames = tab_in[:, 4, 0:1]
+    rows = 128 * -(-table.shape[0] // 128)
+    video = lax.broadcasted_iota(jnp.int32, (16, rows), 1).astype(jnp.float32)
+    picker = jnp.where(frames == video, 1.0, 0.0)
+    total = lax.dot_general(
+        picker, sums, (((0,), (0,)), ((), ())),
+        precision=lax.Precision.HIGHEST, preferred_element_type=jnp.float32,
+    )
+    table[...] = total[: table.shape[0]]
+    table_store.start()
+
+    for k in range(8):
+        loads[k].wait()
+        gw_wide[16 * k : 16 * k + 16, :] = gw_in[k].astype(jnp.float32)
+        stores[k].start()
+    for load, store in moves:
+        load.wait()
+        store.start()
+    for copy in stores + [store for _, store in moves] + [table_store]:
+        copy.wait()
+
+
+def finished(up, gw, gf, tab, video_len):
+    hbm = pl.BlockSpec(memory_space=pltpu.HBM)
+    bf16, f32 = jnp.bfloat16, jnp.float32
+    return pl.pallas_call(
+        finish,
+        out_shape=(
+            jax.ShapeDtypeStruct((4, 2 * WIDTH, 256), bf16),
+            jax.ShapeDtypeStruct((128, 9 * CIN), f32),
+            jax.ShapeDtypeStruct((2, WIDTH, CIN), bf16),
+            jax.ShapeDtypeStruct((video_len, CIN), f32),
+        ),
+        in_specs=[hbm] * 4,
+        out_specs=[hbm] * 4,
+        scratch_shapes=[
+            pltpu.VMEM((8, 16, 9 * CIN), bf16),
+            pltpu.VMEM((128, 9 * CIN), f32),
+            pltpu.VMEM((16, 8, 128), f32),
+            pltpu.VMEM((video_len, CIN), f32),
+            pltpu.VMEM((4, 2 * WIDTH, 256), bf16),
+            pltpu.VMEM((2, WIDTH, CIN), bf16),
+            pltpu.SemaphoreType.DMA((30,)),
+        ],
+        compiler_params=pltpu.CompilerParams(vmem_limit_bytes=60 * 2**20),
+        cost_estimate=pl.CostEstimate(flops=10**8, bytes_accessed=10**7, transcendentals=0),
+        name="finish",
+    )(up, gw, gf, tab)
+
+
 def shards(features, frame_table, frame_ids, conv_weight, cotangent):
     video_len = frame_table.shape[0]
     shift = lax.dynamic_slice_in_dim(frame_table, frame_ids[0], 1, axis=0).astype(jnp.float32)
     up, gw, gf, tab = fused(
         features[0], conv_weight.reshape(2, 2, 2, 16, 9 * CIN), cotangent[0], shift, frame_ids
     )
-    sums = tab[:, :4].reshape(16, CIN)
-    frames = tab[:, 4, 0]
-    picker = (frames[:, None] == jnp.arange(video_len, dtype=jnp.float32)[None, :]).astype(jnp.float32)
-    grad_table = lax.dot_general(
-        picker, sums, (((0,), (0,)), ((), ())),
-        precision=lax.Precision.HIGH, preferred_element_type=jnp.float32,
-    )
-    grad_weight = gw.reshape(128, 9 * CIN).astype(jnp.float32)
+    up, grad_weight, gf, grad_table = finished(up, gw, gf, tab, video_len)
     return (up[None], grad_weight, gf[None], grad_table)
 
 

time: 94.5 us -> 92.1 us (0.975)
  Pallas kernels: 84.2 us -> 89.2 us
  other arithmetic: 4.32 us -> 1.28 us
  local copies, waits for them, and re-layouts: 2.77 us -> 0 us
  matrix products: 1.64 us -> 0 us
    pallas_call x0 -> x1, Pallas kernels: none -> 4.95 us  [finished(): pl.pallas_call(finish, out_shape=(jax.ShapeDtypeStruct((4, 2 * WIDTH, 256...]
    convert_element_type x1 -> x0, other arithmetic: 3.03 us -> none  [shards(): grad_weight = gw.reshape(128, 9 * CIN).astype(jnp.float32)]
    unnamed x8 -> x0, local copies, waits for them, and re-layouts: 2.56 us -> none
    dot_general x1 -> x0, matrix products: 1.64 us -> none  [shards(): lax.dot_general(picker, sums, (((0,), (0,)), ((), ())), precision=lax.Pre...]
where the time goes in v8:
time: 92.1 us; the launch traced here: 91.9 us
  Pallas kernels  89.2 us (97%)
  between operations  1.45 us (2%)
  other arithmetic  1.28 us (1%)
    pallas_call x1, Pallas kernels, fused(): pl.pallas_call(kernel, out_shape=(jax.ShapeDtypeStruct((4, 2 * WIDTH, 256...  84.2 us
    pallas_call x1, Pallas kernels, finished(): pl.pallas_call(finish, out_shape=(jax.ShapeDtypeStruct((4, 2 * WIDTH, 256...  4.95 us

profile of v8, /device:TPU:1, one launch (start us, length us, event | category | flops | bytes accessed | tf_op | source)
XLA Modules:
  0.0 91.9 jit_solution(10969249864012050700)
XLA Ops:
  1.3 1.3 %dynamic-slice_convert_fusion.shift_row_in = f32[1,512]{1,0:T(1,128)} fusion(bf16[600,512]{1,0:T(8,128)(2,1)} %param.6, s32[]{:T(128)S(6)} %select_n.3), kind=kLoop, calls=%fused_computation | loop fusion | flops 512 | bytes 3076 | tf_op jit(solution)/shard_map/convert_element_type | solution.py:980
  2.6 84.2 %conv_block.1 = (bf16[4,768,256]{2,1,0:T(8,128)(2,1)}, bf16[2,2,2,16,4608]{4,3,2,1,0:T(8,128)(2,1)}, bf16[2,384,512]{2,1,0:T(8,128)(2,1)}, f32[16,8,128]{2,1,0:T(8,128)}) custom-call(bf16[2,384,512]{2,1,0:T(8,128)(2,1)} %bitcast.12, bf16[2,2,2,16,4608]{4,3,2,1,0:T(8,128)(2,1)} %bitcast.11, bf16[4,768,256]{2,1,0:T(8,128)(2,1)} %bitcast.9, ...), custom_call_target="tpu_custom_call" | custom-call | flops 21743271936 | bytes 20000000 | tf_op jit(solution)/shard_map/conv_block/pallas_call | solution.py:836
  86.8 5.0 %finish.1 = (bf16[4,768,256]{2,1,0:T(8,128)(2,1)}, f32[128,4608]{1,0:T(8,128)}, bf16[2,384,512]{2,1,0:T(8,128)(2,1)}, f32[600,512]{1,0:T(8,128)}) custom-call(bf16[4,768,256]{2,1,0:T(8,128)(2,1)} %get-tuple-element.12.up, bf16[2,2,2,16,4608]{4,3,2,1,0:T(8,128)(2,1)} %get-tuple-element.13.gw, bf16[2,384,512]{2,1,0:T(8,128)(2,1)} %get-tuple-element.14.gf, ...), custom_call_target="tpu_custom_call" | custom-call | flops 100000000 | bytes 10000000 | tf_op jit(solution)/shard_map/finish/pallas_call | solution.py:953

commit v9 on v8

--- a/solution.py
+++ b/solution.py
@@ -129,11 +129,11 @@
     from_far = [same(far, h, quarter, o_send.at[7 + e], o_recv.at[7 + e], partner[1], e) for e in range(2)]
     across = [same(near, h, quarter, n_send.at[e], n_recv.at[e], partner[2], e) for e in range(2)]
     crossed = [same(near, 1 - h, quarter, n_send.at[e], n_recv.at[e], partner[2], e) for e in range(2)]
-    across_far = same(far, h, quarter, n_send.at[2], n_recv.at[2], partner[2])
-    crossed_far = same(far, 1 - h, quarter, n_send.at[2], n_recv.at[2], partner[2])
+    across_far = [same(far, h, quarter, n_send.at[2 + e], n_recv.at[2 + e], partner[2], e) for e in range(2)]
+    crossed_far = [same(far, 1 - h, quarter, n_send.at[2 + e], n_recv.at[2 + e], partner[2], e) for e in range(2)]
     passed = {}
     theirs = {3: (quarter + 2) % 4, 4: (3 - z + 2 * ye) % 4, 5: (z_flip + 2 * ye) % 4}
-    for k, (pair, half, e) in enumerate(((near, 1 - h, 0), (near, 1 - h, 1), (far, 1 - h, None), (far, h, None))):
+    for k, (pair, half, e) in enumerate(((near, 1 - h, 0), (near, 1 - h, 1), (far, 1 - h, 0), (far, 1 - h, 1), (far, h, None))):
         for j, dim in enumerate((3, 4, 5)):
             passed[k, j] = (
                 same(pair, half, quarter, q_send.at[k, j], q_recv.at[k, j], partner[dim], e),
@@ -293,16 +293,17 @@
     @pl.when(active)
     def _():
         from_flip[0].wait_recv()
-        across_far.start()
+        for copy in across_far:
+            copy.start()
         for k in range(2, 4):
             to_flip[k].start()
 
     @pl.when(passive)
     def _():
-        for copy in from_far:
-            copy.wait_recv()
-        across_far.start()
-        pass_on(3)
+        for e in range(2):
+            from_far[e].wait_recv()
+            across_far[e].start()
+        pass_on(4)
 
     def forward_row(v, r):
         lhs = jnp.concatenate(
@@ -566,20 +567,23 @@
 
     @pl.loop(0, 4)
     def _(r):
-        @pl.when(r == jnp.where(active, 3, 2))
-        def _():
-            crossed_far.wait_recv()
-            pass_on(2)
+        for e in range(2):
+
+            @pl.when(r == jnp.where(active, 2 + e, 1 + e))
+            def _(e=e):
+                crossed_far[e].wait_recv()
+                pass_on(2 + e)
 
         forward_row(near, r)
 
     weight_gradient(near, NEAR_RUNS)
 
     passed_in(2)
+    passed_in(3)
 
     @pl.when(passive)
     def _():
-        passed_in(3)
+        passed_in(4)
 
     @pl.when(active)
     def _():
@@ -783,11 +787,11 @@
         for copy in relay:
             copy.wait_send()
         for j in range(3):
-            passed[3, j][0].wait_send()
-
-    for copy in across + [across_far]:
+            passed[4, j][0].wait_send()
+
+    for copy in across + across_far:
         copy.wait_send()
-    for k in range(3):
+    for k in range(4):
         for j in range(3):
             passed[k, j][0].wait_send()
 
@@ -872,10 +876,10 @@
             dma((7,)),
             dma((11,)),
             dma((11,)),
-            dma((3,)),
-            dma((3,)),
-            dma((4, 3)),
-            dma((4, 3)),
+            dma((4,)),
+            dma((4,)),
+            dma((5, 3)),
+            dma((5, 3)),
             dma((2,)),
             dma((2,)),
             dma((PARTS, 13)),

time: 92.1 us -> 91.2 us (level)
  no operation moved by 1% of the time
where the time goes in v9:
time: 91.2 us; the launch traced here: 91 us
  Pallas kernels  88.3 us (97%)
  between operations  1.45 us (2%)
  other arithmetic  1.28 us (1%)
    pallas_call x1, Pallas kernels, fused(): pl.pallas_call(kernel, out_shape=(jax.ShapeDtypeStruct((4, 2 * WIDTH, 256...  83.3 us
    pallas_call x1, Pallas kernels, finished(): pl.pallas_call(finish, out_shape=(jax.ShapeDtypeStruct((4, 2 * WIDTH, 256...  4.95 us

profile of v9, /device:TPU:1, one launch (start us, length us, event | category | flops | bytes accessed | tf_op | source)
XLA Modules:
  0.0 91.0 jit_solution(12653280209108843476)
XLA Ops:
  1.3 1.3 %dynamic-slice_convert_fusion.shift_row_in = f32[1,512]{1,0:T(1,128)} fusion(bf16[600,512]{1,0:T(8,128)(2,1)} %param.6, s32[]{:T(128)S(6)} %select_n.3), kind=kLoop, calls=%fused_computation | loop fusion | flops 512 | bytes 3076 | tf_op jit(solution)/shard_map/convert_element_type | solution.py:984
  2.6 83.3 %conv_block.1 = (bf16[4,768,256]{2,1,0:T(8,128)(2,1)}, bf16[2,2,2,16,4608]{4,3,2,1,0:T(8,128)(2,1)}, bf16[2,384,512]{2,1,0:T(8,128)(2,1)}, f32[16,8,128]{2,1,0:T(8,128)}) custom-call(bf16[2,384,512]{2,1,0:T(8,128)(2,1)} %bitcast.12, bf16[2,2,2,16,4608]{4,3,2,1,0:T(8,128)(2,1)} %bitcast.11, bf16[4,768,256]{2,1,0:T(8,128)(2,1)} %bitcast.9, ...), custom_call_target="tpu_custom_call" | custom-call | flops 21743271936 | bytes 20000000 | tf_op jit(solution)/shard_map/conv_block/pallas_call | solution.py:840
  85.9 4.9 %finish.1 = (bf16[4,768,256]{2,1,0:T(8,128)(2,1)}, f32[128,4608]{1,0:T(8,128)}, bf16[2,384,512]{2,1,0:T(8,128)(2,1)}, f32[600,512]{1,0:T(8,128)}) custom-call(bf16[4,768,256]{2,1,0:T(8,128)(2,1)} %get-tuple-element.12.up, bf16[2,2,2,16,4608]{4,3,2,1,0:T(8,128)(2,1)} %get-tuple-element.13.gw, bf16[2,384,512]{2,1,0:T(8,128)(2,1)} %get-tuple-element.14.gf, ...), custom_call_target="tpu_custom_call" | custom-call | flops 100000000 | bytes 10000000 | tf_op jit(solution)/shard_map/finish/pallas_call | solution.py:957
